TPU v7x, 256 devices: a whole 4x4x8 slice. The times are simulated.
256 devices in a mesh: blk: 8 (over y, x_hi), view: 32 (over z, x_lo, core).
Axes of the slice: x: 4 (x_hi: 2, x_lo: 2; x = x_hi * 2 + x_lo), y: 4, z: 8, core: 2. Of those that a mesh axis runs over, the one named last changes fastest.
Arguments:
- anchors: float32 [262144, 256], P(('blk', 'view')), may hold values from -0.5 to 0.5
- keys: float32 [262144, 256], P(('blk', 'view')), may hold values from -0.5 to 0.5
- matches: int32 [256, 1024], P(('blk', 'view')), may hold values from 0 to 1023, each once within a row
Outputs:
- loss: float32 [262144], P(('blk', 'view'))
- anchor_grad: float32 [262144, 256], P(('blk', 'view'))
- key_grad: float32 [262144, 256], P(('blk', 'view'))
Inputs may be any that keep to these rules, and one draw needn't show every extreme that they name: Each row of matches is a permutation of 0 to 1023.
All inputs are finite; a program needn't handle non-finite values.
Results may differ from a plain program's by a relative error of at most 0.008.
Values may be sent and summed in bfloat16 or wider, within the bound.
No kernel may reach another device: no remote copies, remote signals or barrier semaphores. Data moves between devices by JAX's collectives and lax.ppermute only.
A program may use at most 64 MiB of HBM per device.

v0:
```python
import math

import jax
import jax.numpy as jnp
from jax import lax
from jax.sharding import PartitionSpec as P

TAU_INV = 40.0


def partner_2(block, axis, distance):
    count = lax.axis_size(axis)
    route = []
    for low in range(count):
        high = low | 1 << distance
        if high != low and high < count:
            route += [(low, high), (high, low)]
    return lax.ppermute(block, axis, route)


def unit_rows(x):
    scale = lax.rsqrt(jnp.sum(x * x, axis=1, keepdims=True) + 1e-06)
    return (x * scale, scale)


def pull_back(unit, scale, grad):
    return scale * (grad - unit * jnp.sum(unit * grad, axis=1, keepdims=True))


def dot_rows(left, right):
    return lax.dot_general(
        left, right, (((1,), (1,)), ((), ())), preferred_element_type=jnp.float32
    )


def dot_cols(left, right):
    return lax.dot_general(
        left, right, (((0,), (0,)), ((), ())), preferred_element_type=jnp.float32
    )


def split_rows(array, width):
    return array.reshape((array.shape[0] // width, width) + array.shape[1:])


def absorb(a_low, carry, piece):
    width = math.gcd(piece.shape[0], 512)

    def absorb_inner(state, block):
        total, weighted = state
        expo = jnp.exp(dot_rows(a_low, block) * TAU_INV)
        return (
            (
                total + jnp.sum(expo, axis=1),
                weighted
                + jnp.dot(expo.astype(jnp.bfloat16), block, preferred_element_type=jnp.float32),
            ),
            None,
        )

    carry, unused = lax.scan(absorb_inner, carry, split_rows(piece, width))
    return carry


def per_device(anchors, keys, matches):
    rows, width_e = anchors.shape
    bit = lax.axis_size("view").bit_length() - 2
    a_unit, a_scale = unit_rows(anchors)
    k_unit, k_scale = unit_rows(keys)
    a_low = a_unit.astype(jnp.bfloat16)
    k_low = k_unit.astype(jnp.bfloat16)
    partner = partner_2(k_low, "view", bit)
    onehot = (matches[0][:, None] == jnp.arange(rows, dtype=jnp.int32)[None, :]).astype(
        jnp.bfloat16
    )
    matched = jnp.dot(onehot, partner, preferred_element_type=jnp.float32)
    positive = jnp.sum(a_low.astype(jnp.float32) * matched, axis=1) * TAU_INV
    start_sums = (jnp.zeros((rows,), jnp.float32), jnp.zeros((rows, width_e), jnp.float32))
    pool = lax.all_gather(partner, "blk", axis=0, tiled=True)
    total, weighted = absorb(a_low, start_sums, pool)
    log_total = jnp.log(total)
    count = rows * lax.axis_size("blk")
    width = math.gcd(count, 512)

    def key_inner(unused, index):
        block = lax.dynamic_slice_in_dim(pool, index * width, width, 0)
        probs = jnp.exp(dot_rows(a_low, block) * TAU_INV - log_total[:, None]).astype(jnp.bfloat16)
        return (None, dot_cols(probs, a_low) * TAU_INV)

    unused, parts = lax.scan(key_inner, None, jnp.arange(count // width, dtype=jnp.int32))
    key_dir = lax.psum_scatter(
        parts.reshape(count, width_e).astype(jnp.bfloat16), "blk", scatter_dimension=0, tiled=True
    ).astype(jnp.float32)
    loss = log_total - positive
    anchor_dir = TAU_INV * (weighted / total[:, None] - matched)
    key_dir = key_dir - TAU_INV * dot_cols(onehot, a_low)
    returned = partner_2(key_dir.astype(jnp.bfloat16), "view", bit).astype(key_dir.dtype)
    return (loss, pull_back(a_unit, a_scale, anchor_dir), pull_back(k_unit, k_scale, returned))


def solution(mesh):
    placed = (P(("blk", "view"), None), P(("blk", "view"), None), P(("blk", "view"), None))
    return jax.shard_map(
        per_device,
        mesh=mesh,
        in_specs=placed,
        out_specs=(P(("blk", "view")), P(("blk", "view"), None), P(("blk", "view"), None)),
        check_vma=False,
    )
```

profile of v0, /device:TPU:32, one launch (start us, length us, event | category | flops | bytes accessed | tf_op | source)
XLA Modules:
  0.0 377.7 jit_solution(11638667630856399881)
XLA Ops:
  10.3 6.4 %collective-permute-start = (bf16[1024,256]{0,1:T(8,128)(2,1)S(1)}, bf16[1024,256]{0,1:T(8,128)(2,1)S(1)}, u32[]{:S(2)}, u32[]{:S(2)}) collective-permute-start(bf16[1024,256]{0,1:T(8,128)(2,1)S(1)} %multiply_convert_fusion.1), channel_id=1, source_target_pairs={{0,16},{16,0},{1,17},{17,1},{2,18},{18,2},{3,19},{19,3},{4,20},{20... | collective-permute-start | bytes 1572872 | tf_op jit(solution)/shard_map/ppermute | solution.py:18
  16.7 23.3 %collective-permute-done = bf16[1024,256]{0,1:T(8,128)(2,1)S(1)} collective-permute-done((bf16[1024,256]{0,1:T(8,128)(2,1)S(1)}, bf16[1024,256]{0,1:T(8,128)(2,1)S(1)}, u32[]{:S(2)}, u32[]{:S(2)}) %collective-permute-start) | collective-permute-done | bytes 524320 | tf_op jit(solution)/shard_map/ppermute | solution.py:18
  40.9 2.5 copy.7
  46.5 72.4 %all-gather.2.cloned.1.call-done = bf16[8192,256]{0,1:T(8,128)(2,1)} async-done(((bf16[1024,256]{0,1:T(8,128)(2,1)}), bf16[8192,256]{0,1:T(8,128)(2,1)}) %all-gather.2.cloned.1.call-update) | async-done | bytes 4194320 | tf_op jit(solution)/shard_map/all_gather | solution.py:79
  118.8 6.4 %copy.18 = bf16[8192,256]{1,0:T(8,128)(2,1)} copy(bf16[8192,256]{0,1:T(8,128)(2,1)} %all-gather.2.cloned.1.call-done) | data formatting | bytes 8388608
  125.2 52.2 %while.24 = (s32[]{:T(128)}, f32[1024]{0:T(1024)S(1)}, f32[1024,256]{1,0:T(8,128)S(1)}, bf16[16,512,256]{2,1,0:T(8,128)(2,1)}, bf16[1024,256]{1,0:T(8,128)(2,1)S(1)}, /*index=5*/s32[]{:T(128)}, s32[]{:T(128)}) while((s32[]{:T(128)}, f32[1024]{0:T(1024)S(1)}, f32[1024,256]{1,0:T(8,128)S(1)}, bf16[16,512,256]{2,1,0:T(8,128)(2,1)}, ...), condition=%wide.region_4.0_spmd.clone, body=%wide.region_2.4_spmd.clone.sunk | while | flops 539493376 | bytes 7356520 | solution.py:61
  178.8 4.0 %multiply_reduce_fusion = (f32[1024]{0:T(1024)S(1)}, f32[1024]{0:T(1024)S(1)}, f32[1024,256]{0,1:T(8,128)}) fusion(f32[1024,256]{0,1:T(8,128)} %copy.7, f32[1024]{0:T(1024)S(1)} %add_rsqrt_fusion, f32[1024,256]{0,1:T(8,128)} %copy.10, f32[1024]{0:T(1024)S(1)} %get-tuple-element.63, bf16[1024,256]{0,1:T(8,128)(2,1)S(1)} %multiply_convert_fusion, ...), kind=kOutput, calls=%fused_computation.37 | convolution fusion | flops 540276736 | bytes 4214784 | tf_op jit(solution)/shard_map/dot_general | solution.py:76
  183.4 60.6 %while.23 = (s32[]{:T(128)}, bf16[16,512,256]{2,1,0:T(8,128)(2,1)}, s32[16]{0:T(128)S(1)}, bf16[8192,256]{1,0:T(8,128)(2,1)}, bf16[1024,256]{1,0:T(8,128)(2,1)S(...) while((s32[]{:T(128)}, bf16[16,512,256]{2,1,0:T(8,128)(2,1)}, ...), condition=%wide.region_8.9_spmd, body=%wide.region_7.8_spmd.sunk | while | flops 538574848 | bytes 1839279 | solution.py:90
  192.2 2.5 fusion.49
  196.0 2.5 fusion.49
  199.8 2.5 fusion.49
  203.6 2.5 fusion.49
  207.4 2.5 fusion.49
  211.2 2.5 fusion.49
  222.6 2.5 fusion.49
  226.4 2.5 fusion.49
  241.5 2.5 fusion.49
  244.1 6.4 %copy.19 = bf16[8192,256]{0,1:T(8,128)(2,1)} copy(bf16[8192,256]{1,0:T(8,128)(2,1)} %bitcast.36) | data formatting | bytes 8388608 | tf_op jit(solution)/shard_map/convert_element_type | solution.py:92
  250.5 87.6 %reduce-scatter.2.cloned.1.call-done = bf16[1024,256]{0,1:T(8,128)(2,1)} async-done(((bf16[8192,256]{0,1:T(8,128)(2,1)}), bf16[1024,256]{0,1:T(8,128)(2,1)}) %reduce-scatter.2.cloned.1.call-update) | async-done | bytes 524304 | tf_op jit(solution)/shard_map/reduce_scatter | solution.py:91
  338.1 3.0 fusion.29
  341.1 4.9 %collective-permute-start.1 = (bf16[1024,256]{0,1:T(8,128)(2,1)}, bf16[1024,256]{0,1:T(8,128)(2,1)S(1)}, u32[]{:S(2)}, u32[]{:S(2)}) collective-permute-start(bf16[1024,256]{0,1:T(8,128)(2,1)} %fusion.29), channel_id=1, source_target_pairs={{0,16},{16,0},{1,17},{17,1},{2,18},{18,2},{3,19},{19,3},{4,20},{20... | collective-permute-start | bytes 1572872 | tf_op jit(solution)/shard_map/ppermute | solution.py:18
  345.9 2.5 subtract_multiply_fusion
  348.5 2.5 copy.15
  351.0 18.1 %collective-permute-done.1 = bf16[1024,256]{0,1:T(8,128)(2,1)S(1)} collective-permute-done((bf16[1024,256]{0,1:T(8,128)(2,1)}, bf16[1024,256]{0,1:T(8,128)(2,1)S(1)}, u32[]{:S(2)}, u32[]{:S(2)}) %collective-permute-start.1) | collective-permute-done | bytes 524320 | tf_op jit(solution)/shard_map/ppermute | solution.py:18
  (100 shorter events, 89.9 us)
Async XLA Ops:
  7.2 111.7 %all-gather.2.cloned.1.call-start = ((), (), s32[]{:S(2)}) async-start(), calls=%async_computation.1 | async-start | bytes 4718592 | tf_op jit(solution)/shard_map/all_gather | solution.py:79
  10.3 29.7 %collective-permute-start = (bf16[1024,256]{0,1:T(8,128)(2,1)S(1)}, bf16[1024,256]{0,1:T(8,128)(2,1)S(1)}, u32[]{:S(2)}, u32[]{:S(2)}) collective-permute-start(bf16[1024,256]{0,1:T(8,128)(2,1)S(1)} %multiply_convert_fusion.1), channel_id=1, source_target_pairs={{0,16},{16,0},{1,17},{17,1},{2,18},{18,2},{3,19},{19,3},{4,20},{20... | collective-permute-start | bytes 1572872 | tf_op jit(solution)/shard_map/ppermute | solution.py:18
  40.0 0.8 copy-start.2
  40.9 297.2 %reduce-scatter.2.cloned.1.call-start = ((), (), s32[]{:S(2)}) async-start(), calls=%async_computation.2 | async-start | bytes 4718592 | tf_op jit(solution)/shard_map/reduce_scatter | solution.py:91
  125.2 53.5 %copy-start.3 = (s32[1,1024]{1,0:T(1,128)S(1)}, s32[1,1024]{1,0:T(1,128)}, u32[]{:S(2)}) copy-start(s32[1,1024]{1,0:T(1,128)} %param.9) | copy-start | bytes 12292
  250.4 95.5 %copy-start = (f32[1024,256]{0,1:T(8,128)S(1)}, f32[1024,256]{0,1:T(8,128)}, u32[]{:S(2)}) copy-start(f32[1024,256]{0,1:T(8,128)} %copy.7) | copy-start | bytes 3145732
  338.1 7.8 %copy-start.1 = (f32[1024,256]{0,1:T(8,128)S(1)}, f32[1024,256]{0,1:T(8,128)}, u32[]{:S(2)}) copy-start(f32[1024,256]{0,1:T(8,128)} %get-tuple-element.126) | copy-start | bytes 3145732
  341.1 28.1 %collective-permute-start.1 = (bf16[1024,256]{0,1:T(8,128)(2,1)}, bf16[1024,256]{0,1:T(8,128)(2,1)S(1)}, u32[]{:S(2)}, u32[]{:S(2)}) collective-permute-start(bf16[1024,256]{0,1:T(8,128)(2,1)} %fusion.29), channel_id=1, source_target_pairs={{0,16},{16,0},{1,17},{17,1},{2,18},{18,2},{3,19},{19,3},{4,20},{20... | collective-permute-start | bytes 1572872 | tf_op jit(solution)/shard_map/ppermute | solution.py:18
Sparse Core Ops, SparseCore 0:
  41.0 77.8 all-gather.1
  250.6 87.4 reduce-scatter.1
where the time goes:
time: 380 us; the launch traced here: 378 us
  waiting for transfers between devices  202 us (53%)
  matrix products  98.8 us (26%)
  local copies, waits for them, and re-layouts  33.2 us (9%)
  between operations  14.1 us (4%)
  starting transfers between devices  11.3 us (3%)
  loops' own time  10.8 us (3%)
  other arithmetic  7.91 us (2%)
    reduce_scatter x1, waiting for transfers between devices, per_device(): lax.psum_scatter(parts.reshape(count, width_e).astype(jnp.bfloat16), 'blk...  87.6 us
    all_gather x1, waiting for transfers between devices, per_device(): pool = lax.all_gather(partner, 'blk', axis=0, tiled=True)  72.4 us
    dot_general x17, matrix products, dot_cols(): lax.dot_general(left, right, (((0,), (0,)), ((), ())), preferred_element_...  43.3 us
    ppermute x2, waiting for transfers between devices, partner_2(): return lax.ppermute(block, axis, route)  41.4 us
    dot_general x16, matrix products, absorb_inner(): jnp.dot(expo.astype(jnp.bfloat16), block, preferred_element_type=jnp.floa...  28.4 us
    dot_general x16, matrix products, dot_rows(): lax.dot_general(left, right, (((1,), (1,)), ((), ())), preferred_element_...  23.1 us
    unnamed x14, local copies, waits for them, and re-layouts  15.4 us
    ppermute x2, starting transfers between devices, partner_2(): return lax.ppermute(block, axis, route)  11.2 us
  transfers between devices with their start and end apart: 4, of which 4 were waited for; matrix products, arithmetic and copies ran while one was open for 3% of the time, Pallas kernels for 0%

commit v1 on v0

v1 whole, which is shorter than its diff:
```python
import math

import jax
import jax.numpy as jnp
from jax import lax
from jax.experimental import pallas as pl
from jax.experimental.pallas import tpu as pltpu
from jax.sharding import PartitionSpec as P

TAU_INV = 40.0
EXP2_SCALE = TAU_INV * math.log2(math.e)
TILE = 256


def view_half(block):
    count = lax.axis_size("view")
    route = [(i, (i + count // 2) % count) for i in range(count)]
    return lax.ppermute(block, "view", route)


def x_swap(block):
    return lax.ppermute(block, "blk", [(i, i ^ 1) for i in range(lax.axis_size("blk"))])


def y_shift(block, distance):
    count = lax.axis_size("blk")
    half = count // 2
    route = [(i, (i // 2 + distance) % half * 2 + i % 2) for i in range(count)]
    return lax.ppermute(block, "blk", route)


def unit_rows(x):
    scale = lax.rsqrt(jnp.sum(x * x, axis=1, keepdims=True) + 1e-06)
    return (x * scale, scale)


def pull_back(unit, scale, grad):
    return scale * (grad - unit * jnp.sum(unit * grad, axis=1, keepdims=True))


def dot_cols(left, right):
    return lax.dot_general(
        left, right, (((0,), (0,)), ((), ())), preferred_element_type=jnp.float32
    )


def expo_kernel(a_ref, *refs):
    n = (len(refs) - 2) // 2
    keys, expos, total_ref, weighted_ref = refs[:n], refs[n : 2 * n], refs[-2], refs[-1]
    a = a_ref[...]
    lanes = jnp.zeros((a.shape[0], 128), jnp.float32)
    weighted = jnp.zeros(weighted_ref.shape, jnp.float32)
    for k_ref, e_ref in zip(keys, expos):
        k = k_ref[...]
        scores = lax.dot_general(
            a, k, (((1,), (1,)), ((), ())), preferred_element_type=jnp.float32
        )
        expo = jnp.exp2(scores * EXP2_SCALE)
        for c in range(0, expo.shape[1], 128):
            lanes += expo[:, c : c + 128]
        low = expo.astype(jnp.bfloat16)
        e_ref[...] = low
        weighted += jnp.dot(low, k, preferred_element_type=jnp.float32)
    total_ref[...] = jnp.broadcast_to(jnp.sum(lanes.T, axis=0, keepdims=True), total_ref.shape)
    weighted_ref[...] = weighted


def expo_pass(a, keys):
    rows, width = a.shape
    n = len(keys)
    pool = rows * n
    whole = pl.BlockSpec((rows, width), lambda i: (0, 0))
    tile_e = pl.BlockSpec((TILE, rows), lambda i: (i, 0))
    out = pl.pallas_call(
        expo_kernel,
        grid=(rows // TILE,),
        in_specs=[pl.BlockSpec((TILE, width), lambda i: (i, 0))] + [whole] * n,
        out_specs=[tile_e] * n
        + [
            pl.BlockSpec((8, TILE), lambda i: (0, i)),
            pl.BlockSpec((TILE, width), lambda i: (i, 0)),
        ],
        out_shape=[jax.ShapeDtypeStruct((rows, rows), jnp.bfloat16)] * n
        + [
            jax.ShapeDtypeStruct((8, rows), jnp.float32),
            jax.ShapeDtypeStruct((rows, width), jnp.float32),
        ],
        compiler_params=pltpu.CompilerParams(vmem_limit_bytes=40 * 2**20),
        cost_estimate=pl.CostEstimate(
            flops=4 * rows * pool * width,
            bytes_accessed=2 * rows * pool + 2 * pool * width,
            transcendentals=rows * pool,
        ),
        name="expo_pass",
    )(a, *keys)
    return out[:n], out[n][0], out[n + 1]


def key_kernel(e0_ref, e1_ref, b0_ref, b1_ref, out_ref):
    grad = dot_cols(e0_ref[...], b0_ref[...]) + dot_cols(e1_ref[...], b1_ref[...])
    out_ref[...] = (TAU_INV * grad).astype(out_ref.dtype)


def key_pass(e0, e1, b0, b1, dtype):
    rows, width = b0.shape
    tile = pl.BlockSpec((rows, TILE), lambda i: (0, i))
    whole = pl.BlockSpec((rows, width), lambda i: (0, 0))
    return pl.pallas_call(
        key_kernel,
        grid=(rows // TILE,),
        in_specs=[tile, tile, whole, whole],
        out_specs=pl.BlockSpec((TILE, width), lambda i: (i, 0)),
        out_shape=jax.ShapeDtypeStruct((rows, width), dtype),
        compiler_params=pltpu.CompilerParams(vmem_limit_bytes=40 * 2**20),
        cost_estimate=pl.CostEstimate(
            flops=4 * rows * rows * width, bytes_accessed=4 * rows * rows, transcendentals=0
        ),
        name="key_pass",
    )(e0, e1, b0, b1)


def per_device(anchors, keys, matches):
    rows, width_e = anchors.shape
    half = lax.axis_size("blk") // 2
    a_unit, a_scale = unit_rows(anchors)
    a_low = a_unit.astype(jnp.bfloat16)
    mine = view_half(a_low)
    paired = view_half(matches)
    k_unit, k_scale = unit_rows(keys)
    k_low = k_unit.astype(jnp.bfloat16)
    pool = [k_low] + [y_shift(k_low, d) for d in range(1, half)]
    other = x_swap(mine)
    onehot = (paired[0][:, None] == jnp.arange(rows, dtype=jnp.int32)[None, :]).astype(
        jnp.bfloat16
    )
    matched = jnp.dot(onehot, k_low, preferred_element_type=jnp.float32)
    positive = jnp.sum(mine.astype(jnp.float32) * matched, axis=1) * TAU_INV
    key_own = -TAU_INV * dot_cols(onehot, mine)
    expo_m, total_m, weighted_m = expo_pass(mine, pool)
    expo_o, total_o, weighted_o = expo_pass(other, pool)
    received = x_swap(jnp.stack([total_o, total_m]))
    total_m = total_m + received[0]
    total_o = total_o + received[1]
    weighted_m = weighted_m + x_swap(weighted_o.astype(jnp.bfloat16)).astype(jnp.float32)
    b_m = (mine.astype(jnp.float32) / total_m[:, None]).astype(jnp.bfloat16)
    b_o = (other.astype(jnp.float32) / total_o[:, None]).astype(jnp.bfloat16)
    parts = []
    for d in (2, 1, 3):
        part = key_pass(expo_m[d], expo_o[d], b_m, b_o, jnp.bfloat16)
        parts.append(y_shift(part, half - d))
    key_dir = key_own + key_pass(expo_m[0], expo_o[0], b_m, b_o, jnp.float32)
    for part in parts:
        key_dir = key_dir + part.astype(jnp.float32)
    loss = view_half((jnp.log(total_m) - positive)[None, :])[0]
    anchor_dir = TAU_INV * (weighted_m / total_m[:, None] - matched)
    anchor_dir = view_half(anchor_dir.astype(jnp.bfloat16)).astype(jnp.float32)
    return (loss, pull_back(a_unit, a_scale, anchor_dir), pull_back(k_unit, k_scale, key_dir))


def solution(mesh):
    placed = (P(("blk", "view"), None), P(("blk", "view"), None), P(("blk", "view"), None))
    return jax.shard_map(
        per_device,
        mesh=mesh,
        in_specs=placed,
        out_specs=(P(("blk", "view")), P(("blk", "view"), None), P(("blk", "view"), None)),
        check_vma=False,
    )
```

time: 380 us -> 119 us (0.31)
  waiting for transfers between devices: 202 us -> 48.3 us
  matrix products: 98.8 us -> 2.39 us
  local copies, waits for them, and re-layouts: 33.2 us -> 0.62 us
  starting transfers between devices: 11.3 us -> 35.3 us
  Pallas kernels: 0 us -> 23.6 us
  between operations: 14.1 us -> 0.86 us
  loops' own time: 10.8 us -> 0 us
    reduce_scatter x1 -> x0, waiting for transfers between devices: 87.6 us -> none  [per_device(): lax.psum_scatter(parts.reshape(count, width_e).astype(jnp.bfloat16), 'blk...]
    all_gather x1 -> x0, waiting for transfers between devices: 72.4 us -> none  [per_device(): pool = lax.all_gather(partner, 'blk', axis=0, tiled=True)]
    dot_general x33 -> x1, matrix products: 55.5 us -> 0.97 us  [per_device(): matched = jnp.dot(onehot, k_low, preferred_element_type=jnp.float32)]
    dot_general x17 -> x1, matrix products: 43.3 us -> 1.42 us  [dot_cols(): lax.dot_general(left, right, (((0,), (0,)), ((), ())), preferred_element_...]
    ppermute x2 -> x13, starting transfers between devices: 11.2 us -> 35.3 us  [the longest x4 17.1 us: view_half(): return lax.ppermute(block, 'view', route)]
    pallas_call x0 -> x6, Pallas kernels: none -> 23.6 us  [the longest x2 13.4 us: expo_pass(): pl.pallas_call(expo_kernel, grid=(rows // TILE,), in_specs=[pl.BlockSpec(...]
    unnamed x14 -> x7, local copies, waits for them, and re-layouts: 15.4 us -> 0.61 us
    another operation x2 -> x0, loops' own time: 10.8 us -> none  [the longest x1 10.2 us: per_device(): lax.scan(key_inner, None, jnp.arange(count // width, dtype=jnp.int32))]
  transfers between devices with their start and end apart: 4 -> 13, of which waited for: 4 -> 7; matrix products, arithmetic and copies ran while one was open for 3% -> 4% of each run, Pallas kernels for 0% -> 12%
where the time goes in v1:
time: 119 us
  waiting for transfers between devices  48.3 us (41%)
  starting transfers between devices  35.3 us (30%)
  Pallas kernels  23.6 us (20%)
  other arithmetic  7.51 us (6%)
  matrix products  2.39 us (2%)
    ppermute x4, waiting for transfers between devices, view_half(): return lax.ppermute(block, 'view', route)  32.1 us
    ppermute x4, starting transfers between devices, view_half(): return lax.ppermute(block, 'view', route)  17.1 us
    ppermute x3, waiting for transfers between devices, x_swap(): lax.ppermute(block, 'blk', [(i, i ^ 1) for i in range(lax.axis_size('blk'...  15 us
    pallas_call x2, Pallas kernels, expo_pass(): pl.pallas_call(expo_kernel, grid=(rows // TILE,), in_specs=[pl.BlockSpec(...  13.4 us
    ppermute x6, starting transfers between devices, y_shift(): return lax.ppermute(block, 'blk', route)  11.5 us
    pallas_call x4, Pallas kernels, key_pass(): pl.pallas_call(key_kernel, grid=(rows // TILE,), in_specs=[tile, tile, wh...  10.2 us
    ppermute x3, starting transfers between devices, x_swap(): lax.ppermute(block, 'blk', [(i, i ^ 1) for i in range(lax.axis_size('blk'...  6.73 us
    mul x2, other arithmetic, pull_back(): return scale * (grad - unit * jnp.sum(unit * grad, axis=1, keepdims=True))  2.64 us
  transfers between devices with their start and end apart: 13, of which 7 were waited for; matrix products, arithmetic and copies ran while one was open for 4% of the time, Pallas kernels for 12%

profile of v1, /device:TPU:32, one launch (start us, length us, event | category | flops | bytes accessed | tf_op | source)
XLA Modules:
  0.0 118.6 jit_solution(15956555049660027279)
XLA Ops:
  0.6 1.5 %multiply_reduce_fusion.2 = f32[1024]{0:T(1024)S(1)} fusion(f32[1024,256]{1,0:T(8,128)} %param.3), kind=kLoop, calls=%fused_computation.20 | loop fusion | flops 523264 | bytes 1052672 | tf_op jit(solution)/shard_map/reduce_sum | solution.py:33
  2.2 1.4 %multiply_convert_fusion.2 = bf16[1024,256]{1,0:T(8,128)(2,1)S(1)} fusion(f32[1024,256]{1,0:T(8,128)} %param.3, f32[1024]{0:T(1024)S(1)} %add_rsqrt_fusion.1), kind=kLoop, calls=%fused_computation.22 | loop fusion | flops 524288 | bytes 1576960 | tf_op jit(solution)/shard_map/convert_element_type | solution.py:126
  3.6 6.4 %collective-permute-start = (bf16[1024,256]{1,0:T(8,128)(2,1)S(1)}, bf16[1024,256]{1,0:T(8,128)(2,1)S(1)}, u32[]{:S(2)}, u32[]{:S(2)}) collective-permute-start(bf16[1024,256]{1,0:T(8,128)(2,1)S(1)} %multiply_convert_fusion.2), channel_id=1, source_target_pairs={{0,16},{1,17},{2,18},{3,19},{4,20},{5,21},{6,22},{7,23},{8,24},{9,... | collective-permute-start | bytes 1572872 | tf_op jit(solution)/shard_map/ppermute | solution.py:18
  10.4 1.7 %collective-permute-start.1 = (bf16[1024,256]{1,0:T(8,128)(2,1)S(1)}, bf16[1024,256]{1,0:T(8,128)(2,1)S(1)}, u32[]{:S(2)}, u32[]{:S(2)}) collective-permute-start(bf16[1024,256]{1,0:T(8,128)(2,1)S(1)} %multiply_convert_fusion.1.refs_0_), channel_id=1, source_target_pairs={{0,64},{32,96},{64,128},{96,160},{128,192},{160,224},{192,0},{224,... | collective-permute-start | bytes 1572872 | tf_op jit(solution)/shard_map/ppermute | solution.py:29
  12.1 2.9 %collective-permute-start.2 = (bf16[1024,256]{1,0:T(8,128)(2,1)S(1)}, bf16[1024,256]{1,0:T(8,128)(2,1)S(1)}, u32[]{:S(2)}, u32[]{:S(2)}) collective-permute-start(bf16[1024,256]{1,0:T(8,128)(2,1)S(1)} %multiply_convert_fusion.1.refs_0_), channel_id=1, source_target_pairs={{0,128},{32,160},{64,192},{96,224},{128,0},{160,32},{192,64},{224,... | collective-permute-start | bytes 1572872 | tf_op jit(solution)/shard_map/ppermute | solution.py:29
  15.0 1.3 %collective-permute-start.3 = (bf16[1024,256]{1,0:T(8,128)(2,1)S(1)}, bf16[1024,256]{1,0:T(8,128)(2,1)S(1)}, u32[]{:S(2)}, u32[]{:S(2)}) collective-permute-start(bf16[1024,256]{1,0:T(8,128)(2,1)S(1)} %multiply_convert_fusion.1.refs_0_), channel_id=1, source_target_pairs={{0,192},{32,224},{64,0},{96,32},{128,64},{160,96},{192,128},{224,1... | collective-permute-start | bytes 1572872 | tf_op jit(solution)/shard_map/ppermute | solution.py:29
  16.4 17.1 %collective-permute-done.a_ref = bf16[1024,256]{1,0:T(8,128)(2,1)S(1)} collective-permute-done((bf16[1024,256]{1,0:T(8,128)(2,1)S(1)}, bf16[1024,256]{1,0:T(8,128)(2,1)S(1)}, u32[]{:S(2)}, u32[]{:S(2)}) %collective-permute-start) | collective-permute-done | bytes 524320 | tf_op jit(solution)/shard_map/ppermute | solution.py:18
  33.4 3.0 %collective-permute-start.4 = (bf16[1024,256]{1,0:T(8,128)(2,1)S(1)}, bf16[1024,256]{1,0:T(8,128)(2,1)S(1)}, u32[]{:S(2)}, u32[]{:S(2)}) collective-permute-start(bf16[1024,256]{1,0:T(8,128)(2,1)S(1)} %collective-permute-done.a_ref), channel_id=1, source_target_pairs={{0,32},{32,0},{64,96},{96,64},{128,160},{160,128},{192,224},{224,1... | collective-permute-start | bytes 1572872 | tf_op jit(solution)/shard_map/ppermute | solution.py:22
  37.6 6.7 %expo_pass.2 = (bf16[1024,1024]{1,0:T(8,128)(2,1)S(1)}, bf16[1024,1024]{1,0:T(8,128)(2,1)S(1)}, bf16[1024,1024]{1,0:T(8,128)(2,1)S(1)}, bf16[1024,1024]{1,0:T(8,...) custom-call(bf16[1024,256]{1,0:T(8,128)(2,1)S(1)} %collective-permute-done.a_ref, ...), custom_call_target="tpu_custom_call" | custom-call | flops 4294967296 | bytes 10485760 | tf_op jit(solution)/shard_map/expo_pass/pallas_call | solution.py:74
  45.3 2.6 %collective-permute-done.4.a_ref = bf16[1024,256]{1,0:T(8,128)(2,1)S(1)} collective-permute-done((bf16[1024,256]{1,0:T(8,128)(2,1)S(1)}, bf16[1024,256]{1,0:T(8,128)(2,1)S(1)}, u32[]{:S(2)}, u32[]{:S(2)}) %collective-permute-start.4) | collective-permute-done | bytes 524320 | tf_op jit(solution)/shard_map/ppermute | solution.py:22
  47.9 6.7 %expo_pass.3 = (bf16[1024,1024]{1,0:T(8,128)(2,1)S(1)}, bf16[1024,1024]{1,0:T(8,128)(2,1)S(1)}, bf16[1024,1024]{1,0:T(8,128)(2,1)S(1)}, bf16[1024,1024]{1,0:T(8,...) custom-call(bf16[1024,256]{1,0:T(8,128)(2,1)S(1)} %collective-permute-done.4.a_ref, ...), custom_call_target="tpu_custom_call" | custom-call | flops 4294967296 | bytes 10485760 | tf_op jit(solution)/shard_map/expo_pass/pallas_call | solution.py:74
  54.6 3.1 %collective-permute-start.5 = (f32[2,1024]{1,0:T(2,128)S(1)}, f32[2,1024]{1,0:T(2,128)S(1)}, u32[]{:S(2)}, u32[]{:S(2)}) collective-permute-start(f32[2,1024]{1,0:T(2,128)S(1)} %pad_maximum_fusion), channel_id=1, source_target_pairs={{0,32},{32,0},{64,96},{96,64},{128,160},{160,128},{192,224},{224,1... | collective-permute-start | bytes 24584 | tf_op jit(solution)/shard_map/ppermute | solution.py:22
  58.4 1.5 %collective-permute-done.5 = f32[2,1024]{1,0:T(2,128)S(1)} collective-permute-done((f32[2,1024]{1,0:T(2,128)S(1)}, f32[2,1024]{1,0:T(2,128)S(1)}, u32[]{:S(2)}, u32[]{:S(2)}) %collective-permute-start.5) | collective-permute-done | bytes 8224 | tf_op jit(solution)/shard_map/ppermute | solution.py:22
  60.1 11.0 %collective-permute-done.8 = bf16[1024,256]{1,0:T(8,128)(2,1)S(1)} collective-permute-done((bf16[1024,256]{1,0:T(8,128)(2,1)S(1)}, bf16[1024,256]{1,0:T(8,128)(2,1)S(1)}, u32[]{:S(2)}, u32[]{:S(2)}) %collective-permute-start.8) | collective-permute-done | bytes 524320 | tf_op jit(solution)/shard_map/ppermute | solution.py:22
  71.5 2.6 %key_pass.5 = bf16[1024,256]{1,0:T(8,128)(2,1)S(1)} custom-call(bf16[1024,1024]{1,0:T(8,128)(2,1)S(1)} %get-tuple-element.21.e0_ref, bf16[1024,1024]{1,0:T(8,128)(2,1)S(1)} %get-tuple-element.22.e1_ref, bf16[1024,256]{1,0:T(8,128)(2,1)S(1)} %get-tuple-element.32.b0_ref, bf16[1024,256]{1,0:T(8,128)(2,1)S(1)} %divide_convert_fusion.b1_ref), custom_call_target="tpu_custom_call" | custom-call | flops 1073741824 | bytes 4194304 | tf_op jit(solution)/shard_map/key_pass/pallas_call | solution.py:108
  74.0 3.3 %collective-permute-start.10 = (bf16[1024,256]{1,0:T(8,128)(2,1)S(1)}, bf16[1024,256]{1,0:T(8,128)(2,1)S(1)}, u32[]{:S(2)}, u32[]{:S(2)}) collective-permute-start(bf16[1024,256]{1,0:T(8,128)(2,1)S(1)} %key_pass.5), channel_id=1, source_target_pairs={{0,128},{32,160},{64,192},{96,224},{128,0},{160,32},{192,64},{224,... | collective-permute-start | bytes 1572872 | tf_op jit(solution)/shard_map/ppermute | solution.py:29
  77.3 2.6 %key_pass.6 = bf16[1024,256]{1,0:T(8,128)(2,1)S(1)} custom-call(bf16[1024,1024]{1,0:T(8,128)(2,1)S(1)} %get-tuple-element.23.e0_ref, bf16[1024,1024]{1,0:T(8,128)(2,1)S(1)} %get-tuple-element.24.e1_ref, bf16[1024,256]{1,0:T(8,128)(2,1)S(1)} %get-tuple-element.32.b0_ref, bf16[1024,256]{1,0:T(8,128)(2,1)S(1)} %divide_convert_fusion.b1_ref), custom_call_target="tpu_custom_call" | custom-call | flops 1073741824 | bytes 4194304 | tf_op jit(solution)/shard_map/key_pass/pallas_call | solution.py:108
  81.2 2.6 %key_pass.7 = bf16[1024,256]{1,0:T(8,128)(2,1)S(1)} custom-call(bf16[1024,1024]{1,0:T(8,128)(2,1)S(1)} %get-tuple-element.25.e0_ref, bf16[1024,1024]{1,0:T(8,128)(2,1)S(1)} %get-tuple-element.26.e1_ref, bf16[1024,256]{1,0:T(8,128)(2,1)S(1)} %get-tuple-element.32.b0_ref, bf16[1024,256]{1,0:T(8,128)(2,1)S(1)} %divide_convert_fusion.b1_ref), custom_call_target="tpu_custom_call" | custom-call | flops 1073741824 | bytes 4194304 | tf_op jit(solution)/shard_map/key_pass/pallas_call | solution.py:108
  84.8 5.3 %collective-permute-start.7 = (f32[1,1024]{1,0:T(1,128)S(1)}, f32[1,1024]{1,0:T(1,128)S(1)}, u32[]{:S(2)}, u32[]{:S(2)}) collective-permute-start(f32[1,1024]{1,0:T(1,128)S(1)} %get-tuple-element.29), channel_id=1, source_target_pairs={{0,16},{1,17},{2,18},{3,19},{4,20},{5,21},{6,22},{7,23},{8,24},{9,... | collective-permute-start | bytes 12296 | tf_op jit(solution)/shard_map/ppermute | solution.py:18
  90.1 1.4 %fusion.4 = f32[1024,256]{1,0:T(8,128)S(1)} fusion(bf16[1024,256]{1,0:T(8,128)(2,1)S(1)} %collective-permute-done.a_ref, s32[1024]{0:T(1024)S(1)} %bitcast.12), kind=kOutput, calls=%fused_computation.5 | convolution fusion | flops 538181632 | bytes 1576960 | tf_op jit(solution)/shard_map/dot_general | solution.py:42
  92.3 5.4 %collective-permute-start.9 = (bf16[1024,256]{1,0:T(8,128)(2,1)S(1)}, bf16[1024,256]{1,0:T(8,128)(2,1)S(1)}, u32[]{:S(2)}, u32[]{:S(2)}) collective-permute-start(bf16[1024,256]{1,0:T(8,128)(2,1)S(1)} %get-tuple-element.33), channel_id=1, source_target_pairs={{0,16},{1,17},{2,18},{3,19},{4,20},{5,21},{6,22},{7,23},{8,24},{9,... | collective-permute-start | bytes 1572872 | tf_op jit(solution)/shard_map/ppermute | solution.py:18
  97.7 2.6 %key_pass.4 = f32[1024,256]{1,0:T(8,128)S(1)} custom-call(bf16[1024,1024]{1,0:T(8,128)(2,1)S(1)} %get-tuple-element.19.e0_ref, bf16[1024,1024]{1,0:T(8,128)(2,1)S(1)} %get-tuple-element.20.e1_ref, bf16[1024,256]{1,0:T(8,128)(2,1)S(1)} %get-tuple-element.32.b0_ref, bf16[1024,256]{1,0:T(8,128)(2,1)S(1)} %divide_convert_fusion.b1_ref), custom_call_target="tpu_custom_call" | custom-call | flops 1073741824 | bytes 4194304 | tf_op jit(solution)/shard_map/key_pass/pallas_call | solution.py:108
  102.1 14.2 %collective-permute-done.9 = bf16[1024,256]{1,0:T(8,128)(2,1)S(1)} collective-permute-done((bf16[1024,256]{1,0:T(8,128)(2,1)S(1)}, bf16[1024,256]{1,0:T(8,128)(2,1)S(1)}, u32[]{:S(2)}, u32[]{:S(2)}) %collective-permute-start.9) | collective-permute-done | bytes 524320 | tf_op jit(solution)/shard_map/ppermute | solution.py:18
  116.7 1.3 %fusion.8 = f32[1024,256]{1,0:T(8,128)} fusion(bf16[1024,256]{1,0:T(8,128)(2,1)S(1)} %collective-permute-done.9, f32[1024,256]{1,0:T(8,128)S(1)} %copy-done.1, f32[1024]{0:T(1024)S(1)} %fusion.7, f32[1024]{0:T(1024)S(1)} %add_rsqrt_fusion.1), kind=kLoop, calls=%fused_computation.13 | loop fusion | flops 1310720 | bytes 2629632 | tf_op jit(solution)/shard_map/mul | solution.py:38
  (35 shorter events, 9.8 us)
Async XLA Ops:
  0.6 9.4 %copy-start = (f32[1024,256]{1,0:T(8,128)S(1)}, f32[1024,256]{1,0:T(8,128)}, u32[]{:S(2)}) copy-start(f32[1024,256]{1,0:T(8,128)} %param.4) | copy-start | bytes 3145732
  2.2 14.2 %copy-start.2 = (s32[1,1024]{1,0:T(1,128)S(1)}, s32[1,1024]{1,0:T(1,128)}, u32[]{:S(2)}) copy-start(s32[1,1024]{1,0:T(1,128)} %param.5) | copy-start | bytes 12292
  3.6 29.8 %collective-permute-start = (bf16[1024,256]{1,0:T(8,128)(2,1)S(1)}, bf16[1024,256]{1,0:T(8,128)(2,1)S(1)}, u32[]{:S(2)}, u32[]{:S(2)}) collective-permute-start(bf16[1024,256]{1,0:T(8,128)(2,1)S(1)} %multiply_convert_fusion.2), channel_id=1, source_target_pairs={{0,16},{1,17},{2,18},{3,19},{4,20},{5,21},{6,22},{7,23},{8,24},{9,... | collective-permute-start | bytes 1572872 | tf_op jit(solution)/shard_map/ppermute | solution.py:18
  10.4 26.0 %collective-permute-start.1 = (bf16[1024,256]{1,0:T(8,128)(2,1)S(1)}, bf16[1024,256]{1,0:T(8,128)(2,1)S(1)}, u32[]{:S(2)}, u32[]{:S(2)}) collective-permute-start(bf16[1024,256]{1,0:T(8,128)(2,1)S(1)} %multiply_convert_fusion.1.refs_0_), channel_id=1, source_target_pairs={{0,64},{32,96},{64,128},{96,160},{128,192},{160,224},{192,0},{224,... | collective-permute-start | bytes 1572872 | tf_op jit(solution)/shard_map/ppermute | solution.py:29
  12.1 25.5 %collective-permute-start.2 = (bf16[1024,256]{1,0:T(8,128)(2,1)S(1)}, bf16[1024,256]{1,0:T(8,128)(2,1)S(1)}, u32[]{:S(2)}, u32[]{:S(2)}) collective-permute-start(bf16[1024,256]{1,0:T(8,128)(2,1)S(1)} %multiply_convert_fusion.1.refs_0_), channel_id=1, source_target_pairs={{0,128},{32,160},{64,192},{96,224},{128,0},{160,32},{192,64},{224,... | collective-permute-start | bytes 1572872 | tf_op jit(solution)/shard_map/ppermute | solution.py:29
  15.0 22.6 %collective-permute-start.3 = (bf16[1024,256]{1,0:T(8,128)(2,1)S(1)}, bf16[1024,256]{1,0:T(8,128)(2,1)S(1)}, u32[]{:S(2)}, u32[]{:S(2)}) collective-permute-start(bf16[1024,256]{1,0:T(8,128)(2,1)S(1)} %multiply_convert_fusion.1.refs_0_), channel_id=1, source_target_pairs={{0,192},{32,224},{64,0},{96,32},{128,64},{160,96},{192,128},{224,1... | collective-permute-start | bytes 1572872 | tf_op jit(solution)/shard_map/ppermute | solution.py:29
  16.4 28.0 %collective-permute-start.6 = (s32[1,1024]{1,0:T(1,128)S(1)}, s32[1,1024]{1,0:T(1,128)S(1)}, u32[]{:S(2)}, u32[]{:S(2)}) collective-permute-start(s32[1,1024]{1,0:T(1,128)S(1)} %copy-done.2), channel_id=1, source_target_pairs={{0,16},{1,17},{2,18},{3,19},{4,20},{5,21},{6,22},{7,23},{8,24},{9,... | collective-permute-start | bytes 12296 | tf_op jit(solution)/shard_map/ppermute | solution.py:18
  33.4 14.4 %collective-permute-start.4 = (bf16[1024,256]{1,0:T(8,128)(2,1)S(1)}, bf16[1024,256]{1,0:T(8,128)(2,1)S(1)}, u32[]{:S(2)}, u32[]{:S(2)}) collective-permute-start(bf16[1024,256]{1,0:T(8,128)(2,1)S(1)} %collective-permute-done.a_ref), channel_id=1, source_target_pairs={{0,32},{32,0},{64,96},{96,64},{128,160},{160,128},{192,224},{224,1... | collective-permute-start | bytes 1572872 | tf_op jit(solution)/shard_map/ppermute | solution.py:22
  54.6 5.2 %collective-permute-start.5 = (f32[2,1024]{1,0:T(2,128)S(1)}, f32[2,1024]{1,0:T(2,128)S(1)}, u32[]{:S(2)}, u32[]{:S(2)}) collective-permute-start(f32[2,1024]{1,0:T(2,128)S(1)} %pad_maximum_fusion), channel_id=1, source_target_pairs={{0,32},{32,0},{64,96},{96,64},{128,160},{160,128},{192,224},{224,1... | collective-permute-start | bytes 24584 | tf_op jit(solution)/shard_map/ppermute | solution.py:22
  57.8 13.3 %collective-permute-start.8 = (bf16[1024,256]{1,0:T(8,128)(2,1)S(1)}, bf16[1024,256]{1,0:T(8,128)(2,1)S(1)}, u32[]{:S(2)}, u32[]{:S(2)}) collective-permute-start(bf16[1024,256]{1,0:T(8,128)(2,1)S(1)} %convert_element_type.44), channel_id=1, source_target_pairs={{0,32},{32,0},{64,96},{96,64},{128,160},{160,128},{192,224},{224,1... | collective-permute-start | bytes 1572872 | tf_op jit(solution)/shard_map/ppermute | solution.py:22
  74.0 26.3 %collective-permute-start.10 = (bf16[1024,256]{1,0:T(8,128)(2,1)S(1)}, bf16[1024,256]{1,0:T(8,128)(2,1)S(1)}, u32[]{:S(2)}, u32[]{:S(2)}) collective-permute-start(bf16[1024,256]{1,0:T(8,128)(2,1)S(1)} %key_pass.5), channel_id=1, source_target_pairs={{0,128},{32,160},{64,192},{96,224},{128,0},{160,32},{192,64},{224,... | collective-permute-start | bytes 1572872 | tf_op jit(solution)/shard_map/ppermute | solution.py:29
  79.9 20.4 %collective-permute-start.11 = (bf16[1024,256]{1,0:T(8,128)(2,1)S(1)}, bf16[1024,256]{1,0:T(8,128)(2,1)S(1)}, u32[]{:S(2)}, u32[]{:S(2)}) collective-permute-start(bf16[1024,256]{1,0:T(8,128)(2,1)S(1)} %key_pass.6), channel_id=1, source_target_pairs={{0,192},{32,224},{64,0},{96,32},{128,64},{160,96},{192,128},{224,1... | collective-permute-start | bytes 1572872 | tf_op jit(solution)/shard_map/ppermute | solution.py:29
  83.8 16.6 %collective-permute-start.12 = (bf16[1024,256]{1,0:T(8,128)(2,1)S(1)}, bf16[1024,256]{1,0:T(8,128)(2,1)S(1)}, u32[]{:S(2)}, u32[]{:S(2)}) collective-permute-start(bf16[1024,256]{1,0:T(8,128)(2,1)S(1)} %key_pass.7), channel_id=1, source_target_pairs={{0,64},{32,96},{64,128},{96,160},{128,192},{160,224},{192,0},{224,... | collective-permute-start | bytes 1572872 | tf_op jit(solution)/shard_map/ppermute | solution.py:29
  84.8 7.5 %collective-permute-start.7 = (f32[1,1024]{1,0:T(1,128)S(1)}, f32[1,1024]{1,0:T(1,128)S(1)}, u32[]{:S(2)}, u32[]{:S(2)}) collective-permute-start(f32[1,1024]{1,0:T(1,128)S(1)} %get-tuple-element.29), channel_id=1, source_target_pairs={{0,16},{1,17},{2,18},{3,19},{4,20},{5,21},{6,22},{7,23},{8,24},{9,... | collective-permute-start | bytes 12296 | tf_op jit(solution)/shard_map/ppermute | solution.py:18
  92.3 24.0 %collective-permute-start.9 = (bf16[1024,256]{1,0:T(8,128)(2,1)S(1)}, bf16[1024,256]{1,0:T(8,128)(2,1)S(1)}, u32[]{:S(2)}, u32[]{:S(2)}) collective-permute-start(bf16[1024,256]{1,0:T(8,128)(2,1)S(1)} %get-tuple-element.33), channel_id=1, source_target_pairs={{0,16},{1,17},{2,18},{3,19},{4,20},{5,21},{6,22},{7,23},{8,24},{9,... | collective-permute-start | bytes 1572872 | tf_op jit(solution)/shard_map/ppermute | solution.py:18
  100.8 15.5 %copy-start.1 = (f32[1024,256]{1,0:T(8,128)S(1)}, f32[1024,256]{1,0:T(8,128)}, u32[]{:S(2)}) copy-start(f32[1024,256]{1,0:T(8,128)} %param.3) | copy-start | bytes 3145732

commit v2 on v0

v2 whole, which is shorter than its diff:
```python
import functools
import math

import jax
import jax.numpy as jnp
from jax import lax
from jax.experimental import pallas as pl
from jax.experimental.pallas import tpu as pltpu
from jax.sharding import PartitionSpec as P

TAU_INV = 40.0
EXP2_SCALE = TAU_INV * math.log2(math.e)
STRIP = 256
LINE = 256
EXTRA = 16
TURN_AFTER = 2
ANCHOR_SIDE = 2
KEY_SIDE = (7, 6, 1)
VMEM = pl.BlockSpec(memory_space=pltpu.VMEM)
ANY = pl.BlockSpec(memory_space=pl.ANY)
PARAMS = pltpu.CompilerParams(vmem_limit_bytes=16 * 2**20)
HEAVY = pl.CostEstimate(flops=2**32, bytes_accessed=2**20, transcendentals=0)
LIGHT = pl.CostEstimate(flops=1024, bytes_accessed=1024, transcendentals=0)


def ordered(kernel, inputs, after):
    def body(*refs):
        kernel(*refs[:inputs], *refs[inputs + len(after) :])

    return body


def view_half(block):
    count = lax.axis_size("view")
    route = [(i, (i + count // 2) % count) for i in range(count)]
    return lax.ppermute(block, "view", route)


def swap(block, mask):
    return lax.ppermute(block, "blk", [(i, i ^ mask) for i in range(lax.axis_size("blk"))])


def dot_rows(left, right):
    return lax.dot_general(
        left, right, (((1,), (1,)), ((), ())), preferred_element_type=jnp.float32
    )


def dot_cols(left, right):
    return lax.dot_general(
        left, right, (((0,), (0,)), ((), ())), preferred_element_type=jnp.float32
    )


def as_row(column):
    wide = jnp.broadcast_to(column, (column.shape[0], 128))
    return wide.T[0:1]


def as_column(row):
    return jnp.broadcast_to(row, (128, row.shape[1])).T[:, 0:1]


def wide(row):
    width = LINE
    return jnp.concatenate([row[:, c : c + width] for c in range(0, row.shape[1], width)], axis=0)


def flat(block):
    return jnp.concatenate([block[i : i + 1] for i in range(block.shape[0])], axis=1)


def stow(ref, start, row):
    rest = wide(row)
    parts = []
    for _ in range(3):
        part = rest.astype(jnp.bfloat16).astype(jnp.float32)
        parts.append(part)
        rest = rest - part
    parts.append(jnp.zeros((EXTRA - 3 * rest.shape[0], LINE), jnp.float32))
    ref[start : start + EXTRA, :] = jnp.concatenate(parts, axis=0).astype(jnp.bfloat16)


def fetch(ref, start, count):
    block = ref[start : start + EXTRA, :].astype(jnp.float32)
    total = block[0:count] + block[count : 2 * count] + block[2 * count : 3 * count]
    return flat(total)


def unit(x):
    return x * lax.rsqrt(jnp.sum(x * x, axis=1, keepdims=True) + 1e-06)


def unit_kernel(x_ref, low_ref):
    low_ref[...] = unit(x_ref[...]).astype(low_ref.dtype)


def unit_match_kernel(x_ref, match_ref, low_ref):
    rows = x_ref.shape[0]
    low_ref[0:rows, :] = unit(x_ref[...]).astype(low_ref.dtype)
    match = match_ref[...]
    high = wide(lax.shift_right_logical(match, 5).astype(jnp.float32))
    low = wide((match & 31).astype(jnp.float32))
    fill = jnp.zeros((EXTRA - 2 * low.shape[0], LINE), jnp.float32)
    low_ref[rows : rows + EXTRA, :] = jnp.concatenate([high, low, fill], axis=0).astype(low_ref.dtype)


def unit_pass(x, start, rows, match=None):
    width = x.shape[1]
    extra = 0 if match is None else EXTRA
    specs = [pl.BlockSpec((rows, width), lambda i: (start // rows, 0))]
    if match is not None:
        specs.append(pl.BlockSpec((1, rows), lambda i: (0, start // rows)))
    return pl.pallas_call(
        unit_kernel if match is None else unit_match_kernel,
        grid=(1,),
        in_specs=specs,
        out_specs=pl.BlockSpec((rows + extra, width), lambda i: (0, 0)),
        out_shape=jax.ShapeDtypeStruct((rows + extra, width), jnp.bfloat16),
        compiler_params=PARAMS,
        cost_estimate=LIGHT,
        name="unit_pass",
    )(*([x] if match is None else [x, match]))


def match_kernel(k_ref, *refs):
    n = len(refs) - 3
    anchors, matched_ref, positive_ref, own_ref = refs[:n], *refs[n:]
    rows = k_ref.shape[0]
    part = rows // n
    count = part // LINE
    own = jnp.zeros(own_ref.shape, jnp.float32)
    for h, a_ref in enumerate(anchors):
        span = slice(h * part, (h + 1) * part)
        code = a_ref[part : part + EXTRA, :].astype(jnp.float32)
        match = flat(code[0:count] * 32.0 + code[count : 2 * count]).astype(jnp.int32)
        index = lax.broadcasted_iota(jnp.int32, (rows, part), 0)
        hot = (index == match).astype(jnp.float32).astype(jnp.bfloat16)
        a = a_ref[0:part, :]
        own += jnp.dot(hot, a, preferred_element_type=jnp.float32)
        matched = dot_cols(hot, k_ref[...])
        matched_ref[span, :] = matched
        score = jnp.sum(a.astype(jnp.float32) * matched, axis=1, keepdims=True)
        positive_ref[:, span] = as_row(score * TAU_INV)
    own_ref[...] = -TAU_INV * own


def match_pass(keys, anchors):
    rows, width = keys.shape
    return pl.pallas_call(
        match_kernel,
        in_specs=[VMEM] * (1 + len(anchors)),
        out_specs=[VMEM] * 3,
        out_shape=[
            jax.ShapeDtypeStruct((rows, width), jnp.float32),
            jax.ShapeDtypeStruct((1, rows), jnp.float32),
            jax.ShapeDtypeStruct((rows, width), jnp.float32),
        ],
        compiler_params=PARAMS,
        cost_estimate=HEAVY,
        name="match_pass",
    )(keys, *anchors)


def expo_body(a_ref, keys, expos):
    rows = a_ref.shape[0] - EXTRA
    a = a_ref[0:rows, :]
    lanes = jnp.zeros((rows, 128), jnp.float32)
    weighted = jnp.zeros((rows, a.shape[1]), jnp.float32)
    for k_ref, e_ref in zip(keys, expos):
        for j in range(0, k_ref.shape[0], STRIP):
            k = k_ref[j : j + STRIP, :]
            expo = jnp.exp2(dot_rows(a, k) * EXP2_SCALE)
            for c in range(0, STRIP, 128):
                lanes += expo[:, c : c + 128]
            low = expo.astype(jnp.bfloat16)
            e_ref[:, j : j + STRIP] = low
            weighted += jnp.dot(low, k, preferred_element_type=jnp.float32)
    return jnp.sum(lanes.T, axis=0, keepdims=True), weighted


def expo_mine_kernel(a_ref, *refs):
    n = (len(refs) - 2) // 2
    total, weighted = expo_body(a_ref, refs[:n], refs[n : 2 * n])
    refs[-2][...] = total
    refs[-1][...] = weighted


def expo_other_kernel(a_ref, mine_ref, *refs):
    n = (len(refs) - 2) // 2
    total, weighted = expo_body(a_ref, refs[:n], refs[n : 2 * n])
    rows = weighted.shape[0]
    mine = mine_ref[...]
    refs[-2][0:1, :] = total
    refs[-2][1:2, :] = mine
    refs[-1][0:rows, :] = weighted.astype(jnp.bfloat16)
    stow(refs[-1], rows, jnp.concatenate([total, mine], axis=1))


def expo_pass(a, keys, mine=None):
    rows, width = a.shape[0] - EXTRA, a.shape[1]
    n = len(keys)
    if mine is None:
        kernel, extra = expo_mine_kernel, []
        tail = [
            jax.ShapeDtypeStruct((1, rows), jnp.float32),
            jax.ShapeDtypeStruct((rows, width), jnp.float32),
        ]
    else:
        kernel, extra = expo_other_kernel, [mine]
        tail = [
            jax.ShapeDtypeStruct((2, rows), jnp.float32),
            jax.ShapeDtypeStruct((rows + EXTRA, width), jnp.bfloat16),
        ]
    out = pl.pallas_call(
        kernel,
        in_specs=[VMEM] * (1 + len(extra) + n),
        out_specs=[VMEM] * (n + 2),
        out_shape=[jax.ShapeDtypeStruct((rows, k.shape[0]), jnp.bfloat16) for k in keys] + tail,
        compiler_params=PARAMS,
        cost_estimate=LIGHT,
        name="expo_pass",
    )(a, *extra, *keys)
    return out[:n], out[n], out[n + 1]


def turn(weighted, sent, total, matched):
    weighted = weighted + sent.astype(jnp.float32)
    return (TAU_INV * (weighted * as_column(1.0 / total) - matched)).astype(jnp.bfloat16)


def turn_first_kernel(weighted_ref, sent_ref, own_ref, matched_ref, out_ref, mine_ref, other_ref):
    rows = weighted_ref.shape[0]
    got = fetch(sent_ref, rows, 2 * rows // LINE)
    mine = own_ref[1:2, :] + got[:, 0:rows]
    mine_ref[...] = mine
    other_ref[...] = own_ref[0:1, :] + got[:, rows : 2 * rows]
    out_ref[...] = turn(weighted_ref[...], sent_ref[0:rows, :], mine, matched_ref[0:rows, :])


def turn_first(weighted, sent, own, matched):
    rows, width = weighted.shape
    return pl.pallas_call(
        turn_first_kernel,
        in_specs=[VMEM] * 4,
        out_specs=[VMEM] * 3,
        out_shape=[jax.ShapeDtypeStruct((rows, width), jnp.bfloat16)]
        + [jax.ShapeDtypeStruct((1, rows), jnp.float32)] * 2,
        compiler_params=PARAMS,
        cost_estimate=LIGHT,
        name="turn_first",
    )(weighted, sent, own, matched)


def turn_last_kernel(weighted_ref, sent_ref, first_ref, last_ref, matched_ref, positive_ref, out_ref):
    rows = weighted_ref.shape[0]
    last = last_ref[...]
    out_ref[0:rows, :] = turn(
        weighted_ref[...], sent_ref[0:rows, :], last, matched_ref[rows : 2 * rows, :]
    )
    stow(
        out_ref,
        rows,
        jnp.log(jnp.concatenate([first_ref[...], last], axis=1)) - positive_ref[...],
    )


def turn_last(weighted, sent, first, last, matched, positive, after):
    rows, width = weighted.shape
    return pl.pallas_call(
        ordered(turn_last_kernel, 6, after),
        in_specs=[VMEM] * 6 + [ANY] * len(after),
        out_specs=VMEM,
        out_shape=jax.ShapeDtypeStruct((rows + EXTRA, width), jnp.bfloat16),
        compiler_params=PARAMS,
        cost_estimate=LIGHT,
        name="turn_last",
    )(weighted, sent, first, last, matched, positive, *after)


def share_kernel(*refs):
    anchors, (mine_ref, other_ref, own_ref, got_ref) = refs[:4], refs[4:8]
    outs, last_ref = refs[8:12], refs[12]
    last = own_ref[1:2, :] + got_ref[0:1, :]
    last_ref[...] = last
    totals = [mine_ref[...], last, other_ref[...], own_ref[0:1, :] + got_ref[1:2, :]]
    for a_ref, total, out_ref in zip(anchors, totals, outs):
        a = a_ref[0 : out_ref.shape[0], :].astype(jnp.float32)
        out_ref[...] = (a * as_column(1.0 / total)).astype(out_ref.dtype)


def share_pass(anchors, mine, other, own, got):
    rows, width = anchors[0].shape[0] - EXTRA, anchors[0].shape[1]
    out = pl.pallas_call(
        share_kernel,
        in_specs=[VMEM] * 8,
        out_specs=[VMEM] * 5,
        out_shape=[jax.ShapeDtypeStruct((rows, width), jnp.bfloat16)] * 4
        + [jax.ShapeDtypeStruct((1, rows), jnp.float32)],
        compiler_params=PARAMS,
        cost_estimate=LIGHT,
        name="share_pass",
    )(*anchors, mine, other, own, got)
    return out[:4], out[4]


def key_kernel(*refs):
    n = len(refs) // 2
    grad = dot_cols(refs[0][...], refs[n][...])
    for e_ref, b_ref in zip(refs[1:n], refs[n + 1 : 2 * n]):
        grad += dot_cols(e_ref[...], b_ref[...])
    refs[-1][...] = (TAU_INV * grad).astype(refs[-1].dtype)


def key_pass(expos, shares, dtype, after=(), cost=LIGHT):
    rows, width = expos[0].shape[1], shares[0].shape[1]
    return pl.pallas_call(
        ordered(key_kernel, 2 * len(expos), after),
        in_specs=[VMEM] * (2 * len(expos)) + [ANY] * len(after),
        out_specs=VMEM,
        out_shape=jax.ShapeDtypeStruct((rows, width), dtype),
        compiler_params=PARAMS,
        cost_estimate=cost,
        name="key_pass",
    )(*expos, *shares, *after)


def pull_kernel(x_ref, *refs):
    x = x_ref[...]
    scale = lax.rsqrt(jnp.sum(x * x, axis=1, keepdims=True) + 1e-06)
    unit = x * scale
    grad = refs[0][...].astype(jnp.float32)
    for ref in refs[1:-1]:
        grad += ref[...].astype(jnp.float32)
    refs[-1][...] = scale * (grad - unit * jnp.sum(unit * grad, axis=1, keepdims=True))


def pull_rest_kernel(x_ref, grad_ref, done_ref, out_ref, loss_ref):
    del done_ref
    rows = x_ref.shape[0]
    pull_kernel(x_ref, grad_ref.at[0:rows, :], out_ref)
    loss_ref[...] = fetch(grad_ref, rows, 2 * rows // LINE)


def pull_pass(x, terms, rows, after=(), cost=LIGHT):
    tile = pl.BlockSpec((STRIP, x.shape[1]), lambda i: (i, 0))
    return pl.pallas_call(
        ordered(pull_kernel, 1 + len(terms), after),
        grid=(rows // STRIP,),
        in_specs=[tile] * (1 + len(terms)) + [ANY] * len(after),
        out_specs=tile,
        out_shape=jax.ShapeDtypeStruct(x.shape, jnp.float32),
        compiler_params=PARAMS,
        cost_estimate=cost,
        name="pull_pass",
    )(x, *terms, *after)


def pull_rest(x, term, done):
    rows = x.shape[0] // 2
    moved = pl.BlockSpec((rows, x.shape[1]), lambda i: (1, 0))
    return pl.pallas_call(
        pull_rest_kernel,
        grid=(1,),
        in_specs=[
            moved,
            pl.BlockSpec(term.shape, lambda i: (0, 0)),
            ANY,
        ],
        out_specs=[moved, pl.BlockSpec((1, 2 * rows), lambda i: (0, 0))],
        out_shape=[
            jax.ShapeDtypeStruct(x.shape, jnp.float32),
            jax.ShapeDtypeStruct((1, 2 * rows), jnp.float32),
        ],
        input_output_aliases={2: 0},
        compiler_params=PARAMS,
        cost_estimate=HEAVY,
        name="pull_rest",
    )(x, term, done)


def per_device(anchors, keys, matches):
    rows = anchors.shape[0]
    part = rows // 2
    a_low = [unit_pass(anchors, s, part, matches) for s in (0, part)]
    a_low, keys = lax.optimization_barrier((a_low, keys))
    mine = [view_half(a) for a in a_low]
    k_low = unit_pass(keys, 0, rows)
    pool = [k_low] + [swap(k_low, d) for d in KEY_SIDE]
    other = [swap(a, ANCHOR_SIDE) for a in mine]
    matched, positive, key_own = match_pass(k_low, mine)
    matched, pool = lax.optimization_barrier((matched, pool))
    done_m, done_o, back = [], [], []
    for a, o in zip(mine, other):
        if done_o:
            a, done_o[-1] = lax.optimization_barrier((a, done_o[-1]))
        done_m.append(expo_pass(a, pool))
        o, done_m[-1] = lax.optimization_barrier((o, done_m[-1]))
        done_o.append(expo_pass(o, pool, done_m[-1][1]))
        back.append(swap(done_o[-1][2], ANCHOR_SIDE))
    expos = [d[0] for d in done_m + done_o]
    got = swap(done_o[1][1], ANCHOR_SIDE)
    turn_0, mine_0, other_0 = turn_first(done_m[0][2], back[0], done_o[0][1], matched)
    turned_0 = view_half(turn_0)
    shares, mine_1 = share_pass(mine + other, mine_0, other_0, done_o[1][1], got)
    parts, sent = [], []
    for d in (1, 2, 3):
        parts.append(key_pass([e[d] for e in expos], shares, jnp.bfloat16, parts[-1:]))
        sent.append(swap(parts[-1], KEY_SIDE[d - 1]))
    turn_1 = turn_last(done_m[1][2], back[1], mine_0, mine_1, matched, positive, parts[TURN_AFTER:])
    turned_1 = view_half(turn_1)
    key_0 = key_pass([e[0] for e in expos], shares, jnp.float32, [turn_1], HEAVY)
    anchor_grad = pull_pass(anchors, [turned_0], part, [key_0])
    anchor_grad, loss = pull_rest(anchors, turned_1, anchor_grad)
    key_grad = pull_pass(keys, [key_own, key_0, *sent], rows, [anchor_grad])
    return (loss.reshape(rows), anchor_grad, key_grad)


def solution(mesh):
    placed = (P(("blk", "view"), None), P(("blk", "view"), None), P(("blk", "view"), None))
    return jax.shard_map(
        per_device,
        mesh=mesh,
        in_specs=placed,
        out_specs=(P(("blk", "view")), P(("blk", "view"), None), P(("blk", "view"), None)),
        check_vma=False,
    )
```

time: 380 us -> 91.5 us (0.24)
  waiting for transfers between devices: 202 us -> 25.8 us
  matrix products: 98.8 us -> 0 us
  local copies, waits for them, and re-layouts: 33.2 us -> 3.14 us
  starting transfers between devices: 11.3 us -> 35.8 us
  Pallas kernels: 0 us -> 24.3 us
  between operations: 14.1 us -> 0.78 us
  loops' own time: 10.8 us -> 0 us
  other arithmetic: 7.91 us -> 0 us
    dot_general x50 -> x0, matrix products: 98.8 us -> none  [the longest x17 43.3 us: dot_cols(): lax.dot_general(left, right, (((0,), (0,)), ((), ())), preferred_element_...]
    reduce_scatter x1 -> x0, waiting for transfers between devices: 87.6 us -> none  [per_device(): lax.psum_scatter(parts.reshape(count, width_e).astype(jnp.bfloat16), 'blk...]
    all_gather x1 -> x0, waiting for transfers between devices: 72.4 us -> none  [per_device(): pool = lax.all_gather(partner, 'blk', axis=0, tiled=True)]
    ppermute x2 -> x15, starting transfers between devices: 11.2 us -> 35.8 us  [the longest x11 19.7 us: swap(): lax.ppermute(block, 'blk', [(i, i ^ mask) for i in range(lax.axis_size('b...]
    pallas_call x0 -> x18, Pallas kernels: none -> 24.3 us  [the longest x4 11.1 us: expo_pass(): pl.pallas_call(kernel, in_specs=[VMEM] * (1 + len(extra) + n), out_specs=...]
    ppermute x2 -> x15, waiting for transfers between devices: 41.4 us -> 25.8 us  [the longest x4 23.3 us: view_half(): return lax.ppermute(block, 'view', route)]
    unnamed x14 -> x10, local copies, waits for them, and re-layouts: 15.4 us -> 3.14 us
    another operation x2 -> x0, loops' own time: 10.8 us -> none  [the longest x1 10.2 us: per_device(): lax.scan(key_inner, None, jnp.arange(count // width, dtype=jnp.int32))]
  transfers between devices with their start and end apart: 4 -> 15, of which waited for: 4 -> 7; matrix products, arithmetic and copies ran while one was open for 3% -> 0% of each run, Pallas kernels for 0% -> 24%
where the time goes in v2:
time: 91.5 us; the launch traced here: 89.8 us
  starting transfers between devices  35.8 us (39%)
  waiting for transfers between devices  25.8 us (28%)
  Pallas kernels  24.3 us (27%)
  local copies, waits for them, and re-layouts  3.14 us (3%)
    ppermute x4, waiting for transfers between devices, view_half(): return lax.ppermute(block, 'view', route)  23.3 us
    ppermute x11, starting transfers between devices, swap(): lax.ppermute(block, 'blk', [(i, i ^ mask) for i in range(lax.axis_size('b...  19.7 us
    ppermute x4, starting transfers between devices, view_half(): return lax.ppermute(block, 'view', route)  16.1 us
    pallas_call x4, Pallas kernels, expo_pass(): pl.pallas_call(kernel, in_specs=[VMEM] * (1 + len(extra) + n), out_specs=...  11.1 us
    pallas_call x4, Pallas kernels, key_pass(): pl.pallas_call(ordered(key_kernel, 2 * len(expos), after), in_specs=[VMEM...  5.63 us
    pallas_call x2, Pallas kernels, pull_pass(): pl.pallas_call(ordered(pull_kernel, 1 + len(terms), after), grid=(rows //...  3.18 us
    unnamed x10, local copies, waits for them, and re-layouts  3.14 us
    ppermute x11, waiting for transfers between devices, swap(): lax.ppermute(block, 'blk', [(i, i ^ mask) for i in range(lax.axis_size('b...  2.43 us
  transfers between devices with their start and end apart: 15, of which 7 were waited for; matrix products, arithmetic and copies ran while one was open for 0% of the time, Pallas kernels for 24%

profile of v2, /device:TPU:32, one launch (start us, length us, event | category | flops | bytes accessed | tf_op | source)
XLA Modules:
  0.0 89.8 jit_solution(2805348126010571990)
XLA Ops:
  2.9 6.4 %collective-permute-start = (bf16[528,256]{1,0:T(8,128)(2,1)S(1)}, bf16[528,256]{1,0:T(8,128)(2,1)S(1)}, u32[]{:S(2)}, u32[]{:S(2)}) collective-permute-start(bf16[528,256]{1,0:T(8,128)(2,1)S(1)} %unit_pass.4), channel_id=1, source_target_pairs={{0,16},{1,17},{2,18},{3,19},{4,20},{5,21},{6,22},{7,23},{8,24},{9,... | collective-permute-start | bytes 811016 | tf_op jit(solution)/shard_map/ppermute | solution.py:36
  9.6 3.1 %collective-permute-start.6 = (bf16[1024,256]{1,0:T(8,128)(2,1)S(1)}, bf16[1024,256]{1,0:T(8,128)(2,1)S(1)}, u32[]{:S(2)}, u32[]{:S(2)}) collective-permute-start(bf16[1024,256]{1,0:T(8,128)(2,1)S(1)} %unit_pass.5.k_ref.refs_0_), channel_id=1, source_target_pairs={{0,32},{32,0},{64,96},{96,64},{128,160},{160,128},{192,224},{224,1... | collective-permute-start | bytes 1572872 | tf_op jit(solution)/shard_map/ppermute | solution.py:40
  12.7 3.0 %collective-permute-start.5 = (bf16[1024,256]{1,0:T(8,128)(2,1)S(1)}, bf16[1024,256]{1,0:T(8,128)(2,1)S(1)}, u32[]{:S(2)}, u32[]{:S(2)}) collective-permute-start(bf16[1024,256]{1,0:T(8,128)(2,1)S(1)} %unit_pass.5.k_ref.refs_0_), channel_id=1, source_target_pairs={{0,192},{32,224},{64,128},{96,160},{128,64},{160,96},{192,0},{224,... | collective-permute-start | bytes 1572872 | tf_op jit(solution)/shard_map/ppermute | solution.py:40
  15.9 10.2 %collective-permute-done.refs_1_.a_ref = bf16[528,256]{1,0:T(8,128)(2,1)S(1)} collective-permute-done((bf16[528,256]{1,0:T(8,128)(2,1)S(1)}, bf16[528,256]{1,0:T(8,128)(2,1)S(1)}, u32[]{:S(2)}, u32[]{:S(2)}) %collective-permute-start) | collective-permute-done | bytes 270368 | tf_op jit(solution)/shard_map/ppermute | solution.py:36
  26.1 1.6 %collective-permute-start.1 = (bf16[528,256]{1,0:T(8,128)(2,1)S(1)}, bf16[528,256]{1,0:T(8,128)(2,1)S(1)}, u32[]{:S(2)}, u32[]{:S(2)}) collective-permute-start(bf16[528,256]{1,0:T(8,128)(2,1)S(1)} %collective-permute-done.refs_1_.a_ref), channel_id=1, source_target_pairs={{0,64},{32,96},{64,0},{96,32},{128,192},{160,224},{192,128},{224,1... | collective-permute-start | bytes 811016 | tf_op jit(solution)/shard_map/ppermute | solution.py:40
  27.7 5.6 %collective-permute-done.2.refs_0_.a_ref = bf16[528,256]{1,0:T(8,128)(2,1)S(1)} collective-permute-done((bf16[528,256]{1,0:T(8,128)(2,1)S(1)}, bf16[528,256]{1,0:T(8,128)(2,1)S(1)}, u32[]{:S(2)}, u32[]{:S(2)}) %collective-permute-start.2) | collective-permute-done | bytes 270368 | tf_op jit(solution)/shard_map/ppermute | solution.py:36
  33.2 1.6 %collective-permute-start.3 = (bf16[528,256]{1,0:T(8,128)(2,1)S(1)}, bf16[528,256]{1,0:T(8,128)(2,1)S(1)}, u32[]{:S(2)}, u32[]{:S(2)}) collective-permute-start(bf16[528,256]{1,0:T(8,128)(2,1)S(1)} %collective-permute-done.2.refs_0_.a_ref), channel_id=1, source_target_pairs={{0,64},{32,96},{64,0},{96,32},{128,192},{160,224},{192,128},{224,1... | collective-permute-start | bytes 811016 | tf_op jit(solution)/shard_map/ppermute | solution.py:40
  34.8 1.6 %match_pass.1 = (f32[1024,256]{1,0:T(8,128)S(1)}, f32[1,1024]{1,0:T(1,128)S(1)}, f32[1024,256]{1,0:T(8,128)S(1)}) custom-call(bf16[1024,256]{1,0:T(8,128)(2,1)S(1)} %unit_pass.5.k_ref.refs_0_, bf16[528,256]{1,0:T(8,128)(2,1)S(1)} %collective-permute-done.2.refs_0_.a_ref, bf16[528,256]{1,0:T(8,128)(2,1)S(1)} %collective-permute-done.refs_1_.a_ref), custom_call_target="tpu_custom_call" | custom-call | flops 4294967296 | bytes 1048576 | tf_op jit(solution)/shard_map/match_pass/pallas_call | solution.py:150
  38.3 2.8 %expo_pass.4 = (bf16[512,1024]{1,0:T(8,128)(2,1)S(1)}, bf16[512,1024]{1,0:T(8,128)(2,1)S(1)}, bf16[512,1024]{1,0:T(8,128)(2,1)S(1)}, bf16[512,1024]{1,0:T(8,128)...) custom-call(bf16[528,256]{1,0:T(8,128)(2,1)S(1)} %collective-permute-done.2.refs_0_.a_ref, ...), custom_call_target="tpu_custom_call" | custom-call | flops 1024 | bytes 1024 | tf_op jit(solution)/shard_map/expo_pass/pallas_call | solution.py:215
  41.1 2.8 %expo_pass.5 = (bf16[512,1024]{1,0:T(8,128)(2,1)S(1)}, bf16[512,1024]{1,0:T(8,128)(2,1)S(1)}, bf16[512,1024]{1,0:T(8,128)(2,1)S(1)}, bf16[512,1024]{1,0:T(8,128)...) custom-call(bf16[528,256]{1,0:T(8,128)(2,1)S(1)} %collective-permute-done.3.a_ref.refs_2_, ...), custom_call_target="tpu_custom_call" | custom-call | flops 1024 | bytes 1024 | tf_op jit(solution)/shard_map/expo_pass/pallas_call | solution.py:215
  43.9 1.5 %collective-permute-start.8 = (bf16[528,256]{1,0:T(8,128)(2,1)S(1)}, bf16[528,256]{1,0:T(8,128)(2,1)S(1)}, u32[]{:S(2)}, u32[]{:S(2)}) collective-permute-start(bf16[528,256]{1,0:T(8,128)(2,1)S(1)} %get-tuple-element.89), channel_id=1, source_target_pairs={{0,64},{32,96},{64,0},{96,32},{128,192},{160,224},{192,128},{224,1... | collective-permute-start | bytes 811016 | tf_op jit(solution)/shard_map/ppermute | solution.py:40
  45.4 2.8 %expo_pass.6 = (bf16[512,1024]{1,0:T(8,128)(2,1)S(1)}, bf16[512,1024]{1,0:T(8,128)(2,1)S(1)}, bf16[512,1024]{1,0:T(8,128)(2,1)S(1)}, bf16[512,1024]{1,0:T(8,128)...) custom-call(bf16[528,256]{1,0:T(8,128)(2,1)S(1)} %collective-permute-done.refs_1_.a_ref, ...), custom_call_target="tpu_custom_call" | custom-call | flops 1024 | bytes 1024 | tf_op jit(solution)/shard_map/expo_pass/pallas_call | solution.py:215
  48.2 2.8 %expo_pass.7 = (bf16[512,1024]{1,0:T(8,128)(2,1)S(1)}, bf16[512,1024]{1,0:T(8,128)(2,1)S(1)}, bf16[512,1024]{1,0:T(8,128)(2,1)S(1)}, bf16[512,1024]{1,0:T(8,128)...) custom-call(bf16[528,256]{1,0:T(8,128)(2,1)S(1)} %collective-permute-done.1.a_ref.refs_3_, ...), custom_call_target="tpu_custom_call" | custom-call | flops 1024 | bytes 1024 | tf_op jit(solution)/shard_map/expo_pass/pallas_call | solution.py:215
  51.9 1.2 %collective-permute-start.9 = (f32[2,512]{1,0:T(2,128)S(1)}, f32[2,512]{1,0:T(2,128)S(1)}, u32[]{:S(2)}, u32[]{:S(2)}) collective-permute-start(f32[2,512]{1,0:T(2,128)S(1)} %get-tuple-element.106.refs_6_), channel_id=1, source_target_pairs={{0,64},{32,96},{64,0},{96,32},{128,192},{160,224},{192,128},{224,1... | collective-permute-start | bytes 12296 | tf_op jit(solution)/shard_map/ppermute | solution.py:40
  53.4 5.4 %collective-permute-start.11 = (bf16[512,256]{1,0:T(8,128)(2,1)S(1)}, bf16[512,256]{1,0:T(8,128)(2,1)S(1)}, u32[]{:S(2)}, u32[]{:S(2)}) collective-permute-start(bf16[512,256]{1,0:T(8,128)(2,1)S(1)} %get-tuple-element.125), channel_id=1, source_target_pairs={{0,16},{1,17},{2,18},{3,19},{4,20},{5,21},{6,22},{7,23},{8,24},{9,... | collective-permute-start | bytes 786440 | tf_op jit(solution)/shard_map/ppermute | solution.py:36
  59.4 1.4 %key_pass.4.refs_8_ = bf16[1024,256]{1,0:T(8,128)(2,1)S(1)} custom-call(bf16[512,1024]{1,0:T(8,128)(2,1)S(1)} %get-tuple-element.121.refs_0_, bf16[512,1024]{1,0:T(8,128)(2,1)S(1)} %get-tuple-element.122.refs_1_, bf16[512,1024]{1,0:T(8,128)(2,1)S(1)} %get-tuple-element.123.refs_2_, bf16[512,1024]{1,0:T(8,128)(2,1)S(1)} %get-tuple-element.124.refs_3_, ...), custom_call_target="tpu_custom_call" | custom-call | flops 1024 | bytes 1024 | tf_op jit(solution)/shard_map/key_pass/pallas_call | solution.py:317
  60.9 4.7 %collective-permute-start.12 = (bf16[1024,256]{1,0:T(8,128)(2,1)S(1)}, bf16[1024,256]{1,0:T(8,128)(2,1)S(1)}, u32[]{:S(2)}, u32[]{:S(2)}) collective-permute-start(bf16[1024,256]{1,0:T(8,128)(2,1)S(1)} %key_pass.4.refs_8_), channel_id=1, source_target_pairs={{0,224},{32,192},{64,160},{96,128},{128,96},{160,64},{192,32},{224... | collective-permute-start | bytes 1572872 | tf_op jit(solution)/shard_map/ppermute | solution.py:40
  65.6 1.4 %key_pass.5.refs_8_ = bf16[1024,256]{1,0:T(8,128)(2,1)S(1)} custom-call(bf16[512,1024]{1,0:T(8,128)(2,1)S(1)} %get-tuple-element.117.refs_0_, bf16[512,1024]{1,0:T(8,128)(2,1)S(1)} %get-tuple-element.118.refs_1_, bf16[512,1024]{1,0:T(8,128)(2,1)S(1)} %get-tuple-element.119.refs_2_, bf16[512,1024]{1,0:T(8,128)(2,1)S(1)} %get-tuple-element.120.refs_3_, ...), custom_call_target="tpu_custom_call" | custom-call | flops 1024 | bytes 1024 | tf_op jit(solution)/shard_map/key_pass/pallas_call | solution.py:317
  67.0 1.4 %collective-permute-start.13 = (bf16[1024,256]{1,0:T(8,128)(2,1)S(1)}, bf16[1024,256]{1,0:T(8,128)(2,1)S(1)}, u32[]{:S(2)}, u32[]{:S(2)}) collective-permute-start(bf16[1024,256]{1,0:T(8,128)(2,1)S(1)} %key_pass.5.refs_8_), channel_id=1, source_target_pairs={{0,192},{32,224},{64,128},{96,160},{128,64},{160,96},{192,0},{224,... | collective-permute-start | bytes 1572872 | tf_op jit(solution)/shard_map/ppermute | solution.py:40
  68.4 1.4 %key_pass.6.refs_6_ = bf16[1024,256]{1,0:T(8,128)(2,1)S(1)} custom-call(bf16[512,1024]{1,0:T(8,128)(2,1)S(1)} %get-tuple-element.109.refs_0_, bf16[512,1024]{1,0:T(8,128)(2,1)S(1)} %get-tuple-element.110.refs_1_, bf16[512,1024]{1,0:T(8,128)(2,1)S(1)} %get-tuple-element.111.refs_2_, bf16[512,1024]{1,0:T(8,128)(2,1)S(1)} %get-tuple-element.112.refs_3_, ...), custom_call_target="tpu_custom_call" | custom-call | flops 1024 | bytes 1024 | tf_op jit(solution)/shard_map/key_pass/pallas_call | solution.py:317
  70.6 4.2 %collective-permute-start.10 = (bf16[528,256]{1,0:T(8,128)(2,1)S(1)}, bf16[528,256]{1,0:T(8,128)(2,1)S(1)}, u32[]{:S(2)}, u32[]{:S(2)}) collective-permute-start(bf16[528,256]{1,0:T(8,128)(2,1)S(1)} %turn_last.1.refs_8_), channel_id=1, source_target_pairs={{0,16},{1,17},{2,18},{3,19},{4,20},{5,21},{6,22},{7,23},{8,24},{9,... | collective-permute-start | bytes 811016 | tf_op jit(solution)/shard_map/ppermute | solution.py:36
  74.8 1.4 %key_pass.7.refs_2_ = f32[1024,256]{1,0:T(8,128)S(1)} custom-call(bf16[512,1024]{1,0:T(8,128)(2,1)S(1)} %get-tuple-element.126.refs_0_, bf16[512,1024]{1,0:T(8,128)(2,1)S(1)} %get-tuple-element.127.refs_1_, bf16[512,1024]{1,0:T(8,128)(2,1)S(1)} %get-tuple-element.128.refs_2_, bf16[512,1024]{1,0:T(8,128)(2,1)S(1)} %get-tuple-element.129.refs_3_, ...), custom_call_target="tpu_custom_call" | custom-call | flops 4294967296 | bytes 1048576 | tf_op jit(solution)/shard_map/key_pass/pallas_call | solution.py:317
  77.4 7.5 %collective-permute-done.10.grad_ref = bf16[528,256]{1,0:T(8,128)(2,1)S(1)} collective-permute-done((bf16[528,256]{1,0:T(8,128)(2,1)S(1)}, bf16[528,256]{1,0:T(8,128)(2,1)S(1)}, u32[]{:S(2)}, u32[]{:S(2)}) %collective-permute-start.10) | collective-permute-done | bytes 270368 | tf_op jit(solution)/shard_map/ppermute | solution.py:36
  87.8 2.0 %pull_pass.3 = f32[1024,256]{1,0:T(8,128)} custom-call(f32[1024,256]{1,0:T(8,128)S(1)} %copy-done.2, f32[1024,256]{1,0:T(8,128)S(1)} %get-tuple-element.132.refs_1_, f32[1024,256]{1,0:T(8,128)S(1)} %key_pass.7.refs_2_, bf16[1024,256]{1,0:T(8,128)(2,1)S(1)} %collective-permute-done.12.refs_3_, bf16[1024,256]{1,0:T(8,128)(2,1)S(1)} %collective-permute-done.13.refs_4_, ...), custom_call_target="tpu_custom_call" | custom-call | flops 1024 | bytes 1024 | tf_op jit(solution)/shard_map/pull_pass/pallas_call | solution.py:347
  (34 shorter events, 11.2 us)
Async XLA Ops:
  0.6 1.2 %copy-start = (f32[1024,256]{1,0:T(8,128)S(1)}, f32[1024,256]{1,0:T(8,128)}, u32[]{:S(2)}) copy-start(f32[1024,256]{1,0:T(8,128)} %x_ref.6) | copy-start | bytes 3145732
  1.9 0.7 copy-start.4
  2.5 6.8 %copy-start.2 = (f32[1024,256]{1,0:T(8,128)S(1)}, f32[1024,256]{1,0:T(8,128)}, u32[]{:S(2)}) copy-start(f32[1024,256]{1,0:T(8,128)} %refs_0_.2) | copy-start | bytes 3145732
  2.9 23.2 %collective-permute-start = (bf16[528,256]{1,0:T(8,128)(2,1)S(1)}, bf16[528,256]{1,0:T(8,128)(2,1)S(1)}, u32[]{:S(2)}, u32[]{:S(2)}) collective-permute-start(bf16[528,256]{1,0:T(8,128)(2,1)S(1)} %unit_pass.4), channel_id=1, source_target_pairs={{0,16},{1,17},{2,18},{3,19},{4,20},{5,21},{6,22},{7,23},{8,24},{9,... | collective-permute-start | bytes 811016 | tf_op jit(solution)/shard_map/ppermute | solution.py:36
  9.2 24.0 %collective-permute-start.2 = (bf16[528,256]{1,0:T(8,128)(2,1)S(1)}, bf16[528,256]{1,0:T(8,128)(2,1)S(1)}, u32[]{:S(2)}, u32[]{:S(2)}) collective-permute-start(bf16[528,256]{1,0:T(8,128)(2,1)S(1)} %unit_pass.3), channel_id=1, source_target_pairs={{0,16},{1,17},{2,18},{3,19},{4,20},{5,21},{6,22},{7,23},{8,24},{9,... | collective-permute-start | bytes 811016 | tf_op jit(solution)/shard_map/ppermute | solution.py:36
  9.6 26.9 %collective-permute-start.6 = (bf16[1024,256]{1,0:T(8,128)(2,1)S(1)}, bf16[1024,256]{1,0:T(8,128)(2,1)S(1)}, u32[]{:S(2)}, u32[]{:S(2)}) collective-permute-start(bf16[1024,256]{1,0:T(8,128)(2,1)S(1)} %unit_pass.5.k_ref.refs_0_), channel_id=1, source_target_pairs={{0,32},{32,0},{64,96},{96,64},{128,160},{160,128},{192,224},{224,1... | collective-permute-start | bytes 1572872 | tf_op jit(solution)/shard_map/ppermute | solution.py:40
  12.7 24.9 %collective-permute-start.5 = (bf16[1024,256]{1,0:T(8,128)(2,1)S(1)}, bf16[1024,256]{1,0:T(8,128)(2,1)S(1)}, u32[]{:S(2)}, u32[]{:S(2)}) collective-permute-start(bf16[1024,256]{1,0:T(8,128)(2,1)S(1)} %unit_pass.5.k_ref.refs_0_), channel_id=1, source_target_pairs={{0,192},{32,224},{64,128},{96,160},{128,64},{160,96},{192,0},{224,... | collective-permute-start | bytes 1572872 | tf_op jit(solution)/shard_map/ppermute | solution.py:40
  15.7 22.6 %collective-permute-start.4 = (bf16[1024,256]{1,0:T(8,128)(2,1)S(1)}, bf16[1024,256]{1,0:T(8,128)(2,1)S(1)}, u32[]{:S(2)}, u32[]{:S(2)}) collective-permute-start(bf16[1024,256]{1,0:T(8,128)(2,1)S(1)} %unit_pass.5.k_ref.refs_0_), channel_id=1, source_target_pairs={{0,224},{32,192},{64,160},{96,128},{128,96},{160,64},{192,32},{224... | collective-permute-start | bytes 1572872 | tf_op jit(solution)/shard_map/ppermute | solution.py:40
  26.1 22.1 %collective-permute-start.1 = (bf16[528,256]{1,0:T(8,128)(2,1)S(1)}, bf16[528,256]{1,0:T(8,128)(2,1)S(1)}, u32[]{:S(2)}, u32[]{:S(2)}) collective-permute-start(bf16[528,256]{1,0:T(8,128)(2,1)S(1)} %collective-permute-done.refs_1_.a_ref), channel_id=1, source_target_pairs={{0,64},{32,96},{64,0},{96,32},{128,192},{160,224},{192,128},{224,1... | collective-permute-start | bytes 811016 | tf_op jit(solution)/shard_map/ppermute | solution.py:40
  33.2 7.9 %collective-permute-start.3 = (bf16[528,256]{1,0:T(8,128)(2,1)S(1)}, bf16[528,256]{1,0:T(8,128)(2,1)S(1)}, u32[]{:S(2)}, u32[]{:S(2)}) collective-permute-start(bf16[528,256]{1,0:T(8,128)(2,1)S(1)} %collective-permute-done.2.refs_0_.a_ref), channel_id=1, source_target_pairs={{0,64},{32,96},{64,0},{96,32},{128,192},{160,224},{192,128},{224,1... | collective-permute-start | bytes 811016 | tf_op jit(solution)/shard_map/ppermute | solution.py:40
  43.9 9.2 %collective-permute-start.8 = (bf16[528,256]{1,0:T(8,128)(2,1)S(1)}, bf16[528,256]{1,0:T(8,128)(2,1)S(1)}, u32[]{:S(2)}, u32[]{:S(2)}) collective-permute-start(bf16[528,256]{1,0:T(8,128)(2,1)S(1)} %get-tuple-element.89), channel_id=1, source_target_pairs={{0,64},{32,96},{64,0},{96,32},{128,192},{160,224},{192,128},{224,1... | collective-permute-start | bytes 811016 | tf_op jit(solution)/shard_map/ppermute | solution.py:40
  51.0 19.4 %collective-permute-start.7 = (bf16[528,256]{1,0:T(8,128)(2,1)S(1)}, bf16[528,256]{1,0:T(8,128)(2,1)S(1)}, u32[]{:S(2)}, u32[]{:S(2)}) collective-permute-start(bf16[528,256]{1,0:T(8,128)(2,1)S(1)} %get-tuple-element.100), channel_id=1, source_target_pairs={{0,64},{32,96},{64,0},{96,32},{128,192},{160,224},{192,128},{224,1... | collective-permute-start | bytes 811016 | tf_op jit(solution)/shard_map/ppermute | solution.py:40
  51.9 6.9 %collective-permute-start.9 = (f32[2,512]{1,0:T(2,128)S(1)}, f32[2,512]{1,0:T(2,128)S(1)}, u32[]{:S(2)}, u32[]{:S(2)}) collective-permute-start(f32[2,512]{1,0:T(2,128)S(1)} %get-tuple-element.106.refs_6_), channel_id=1, source_target_pairs={{0,64},{32,96},{64,0},{96,32},{128,192},{160,224},{192,128},{224,1... | collective-permute-start | bytes 12296 | tf_op jit(solution)/shard_map/ppermute | solution.py:40
  53.4 22.9 %collective-permute-start.11 = (bf16[512,256]{1,0:T(8,128)(2,1)S(1)}, bf16[512,256]{1,0:T(8,128)(2,1)S(1)}, u32[]{:S(2)}, u32[]{:S(2)}) collective-permute-start(bf16[512,256]{1,0:T(8,128)(2,1)S(1)} %get-tuple-element.125), channel_id=1, source_target_pairs={{0,16},{1,17},{2,18},{3,19},{4,20},{5,21},{6,22},{7,23},{8,24},{9,... | collective-permute-start | bytes 786440 | tf_op jit(solution)/shard_map/ppermute | solution.py:36
  60.9 25.7 %collective-permute-start.12 = (bf16[1024,256]{1,0:T(8,128)(2,1)S(1)}, bf16[1024,256]{1,0:T(8,128)(2,1)S(1)}, u32[]{:S(2)}, u32[]{:S(2)}) collective-permute-start(bf16[1024,256]{1,0:T(8,128)(2,1)S(1)} %key_pass.4.refs_8_), channel_id=1, source_target_pairs={{0,224},{32,192},{64,160},{96,128},{128,96},{160,64},{192,32},{224... | collective-permute-start | bytes 1572872 | tf_op jit(solution)/shard_map/ppermute | solution.py:40
  67.0 19.6 %collective-permute-start.13 = (bf16[1024,256]{1,0:T(8,128)(2,1)S(1)}, bf16[1024,256]{1,0:T(8,128)(2,1)S(1)}, u32[]{:S(2)}, u32[]{:S(2)}) collective-permute-start(bf16[1024,256]{1,0:T(8,128)(2,1)S(1)} %key_pass.5.refs_8_), channel_id=1, source_target_pairs={{0,192},{32,224},{64,128},{96,160},{128,64},{160,96},{192,0},{224,... | collective-permute-start | bytes 1572872 | tf_op jit(solution)/shard_map/ppermute | solution.py:40
  69.8 16.5 %collective-permute-start.14 = (bf16[1024,256]{1,0:T(8,128)(2,1)S(1)}, bf16[1024,256]{1,0:T(8,128)(2,1)S(1)}, u32[]{:S(2)}, u32[]{:S(2)}) collective-permute-start(bf16[1024,256]{1,0:T(8,128)(2,1)S(1)} %key_pass.6.refs_6_), channel_id=1, source_target_pairs={{0,32},{32,0},{64,96},{96,64},{128,160},{160,128},{192,224},{224,1... | collective-permute-start | bytes 1572872 | tf_op jit(solution)/shard_map/ppermute | solution.py:40
  70.6 14.3 %collective-permute-start.10 = (bf16[528,256]{1,0:T(8,128)(2,1)S(1)}, bf16[528,256]{1,0:T(8,128)(2,1)S(1)}, u32[]{:S(2)}, u32[]{:S(2)}) collective-permute-start(bf16[528,256]{1,0:T(8,128)(2,1)S(1)} %turn_last.1.refs_8_), channel_id=1, source_target_pairs={{0,16},{1,17},{2,18},{3,19},{4,20},{5,21},{6,22},{7,23},{8,24},{9,... | collective-permute-start | bytes 811016 | tf_op jit(solution)/shard_map/ppermute | solution.py:36
  74.8 1.4 %copy-start.1 = (f32[1024,256]{1,0:T(8,128)S(1)}, f32[1024,256]{1,0:T(8,128)}, u32[]{:S(2)}) copy-start(f32[1024,256]{1,0:T(8,128)} %x_ref.6) | copy-start | bytes 3145732
  86.6 1.2 %copy-start.3 = (f32[1024,256]{1,0:T(8,128)S(1)}, f32[1024,256]{1,0:T(8,128)}, u32[]{:S(2)}) copy-start(f32[1024,256]{1,0:T(8,128)} %get-tuple-element.66.refs_6_) | copy-start | bytes 3145732

commit v3 on v2

v3 whole, which is shorter than its diff:
```python
import functools
import math

import jax
import jax.numpy as jnp
from jax import lax
from jax.experimental import pallas as pl
from jax.experimental.pallas import tpu as pltpu
from jax.sharding import PartitionSpec as P

TAU_INV = 40.0
EXP2_SCALE = TAU_INV * math.log2(math.e)
STRIP = 256
LINE = 256
EXTRA = 16
ANCHOR_SIDE = 1
KEY_SIDE = (2, 6, 4)
VMEM = pl.BlockSpec(memory_space=pltpu.VMEM)
ANY = pl.BlockSpec(memory_space=pl.ANY)
HBM = pl.BlockSpec(memory_space=pltpu.HBM)
PARAMS = pltpu.CompilerParams(vmem_limit_bytes=16 * 2**20)
HEAVY = pl.CostEstimate(flops=2**32, bytes_accessed=2**20, transcendentals=0)
FIRST = pl.CostEstimate(flops=2**32, bytes_accessed=2**20, transcendentals=0)
LIGHT = pl.CostEstimate(flops=1024, bytes_accessed=1024, transcendentals=0)


def ordered(kernel, inputs, after):
    def body(*refs):
        kernel(*refs[:inputs], *refs[inputs + len(after) :])

    return body


def view_half(block):
    count = lax.axis_size("view")
    route = [(i, (i + count // 2) % count) for i in range(count)]
    return lax.ppermute(block, "view", route)


def swap(block, mask):
    return lax.ppermute(block, "blk", [(i, i ^ mask) for i in range(lax.axis_size("blk"))])


def dot_rows(left, right):
    return lax.dot_general(
        left, right, (((1,), (1,)), ((), ())), preferred_element_type=jnp.float32
    )


def dot_cols(left, right):
    return lax.dot_general(
        left, right, (((0,), (0,)), ((), ())), preferred_element_type=jnp.float32
    )


def as_row(column):
    wide = jnp.broadcast_to(column, (column.shape[0], 128))
    return wide.T[0:1]


def as_column(row):
    return jnp.broadcast_to(row, (128, row.shape[1])).T[:, 0:1]


def wide(row):
    width = LINE
    return jnp.concatenate([row[:, c : c + width] for c in range(0, row.shape[1], width)], axis=0)


def flat(block):
    return jnp.concatenate([block[i : i + 1] for i in range(block.shape[0])], axis=1)


def stow(ref, start, row):
    rest = wide(row)
    parts = []
    for _ in range(3):
        part = rest.astype(jnp.bfloat16).astype(jnp.float32)
        parts.append(part)
        rest = rest - part
    parts.append(jnp.zeros((EXTRA - 3 * rest.shape[0], LINE), jnp.float32))
    ref[start : start + EXTRA, :] = jnp.concatenate(parts, axis=0).astype(jnp.bfloat16)


def fetch(ref, start, count):
    block = ref[start : start + EXTRA, :].astype(jnp.float32)
    total = block[0:count] + block[count : 2 * count] + block[2 * count : 3 * count]
    return flat(total)


def unit(x):
    return x * lax.rsqrt(jnp.sum(x * x, axis=1, keepdims=True) + 1e-06)


def unit_kernel(start, x_hbm, low_ref, x_ref, sem):
    rows = x_ref.shape[0]
    load = pltpu.make_async_copy(x_hbm.at[pl.ds(start, rows)], x_ref, sem)
    load.start()
    load.wait()
    low_ref[0:rows, :] = unit(x_ref[...]).astype(low_ref.dtype)


def unit_match_kernel(start, x_hbm, match_ref, low_ref, x_ref, sem):
    rows = x_ref.shape[0]
    load = pltpu.make_async_copy(x_hbm.at[pl.ds(start, rows)], x_ref, sem)
    load.start()
    match = match_ref[...]
    high = wide(lax.shift_right_logical(match, 5).astype(jnp.float32))
    low = wide((match & 31).astype(jnp.float32))
    fill = jnp.zeros((EXTRA - 2 * low.shape[0], LINE), jnp.float32)
    low_ref[rows : rows + EXTRA, :] = jnp.concatenate([high, low, fill], axis=0).astype(low_ref.dtype)
    load.wait()
    low_ref[0:rows, :] = unit(x_ref[...]).astype(low_ref.dtype)


def unit_pass(x, start, rows, match=None, after=()):
    width = x.shape[1]
    kernel = functools.partial(unit_kernel if match is None else unit_match_kernel, start)
    given = [x] if match is None else [x, match]
    extra = 0 if match is None else EXTRA
    return pl.pallas_call(
        ordered(kernel, len(given), after),
        in_specs=[HBM] + [VMEM] * (len(given) - 1) + [ANY] * len(after),
        out_specs=VMEM,
        out_shape=jax.ShapeDtypeStruct((rows + extra, width), jnp.bfloat16),
        scratch_shapes=[pltpu.VMEM((rows, width), jnp.float32), pltpu.SemaphoreType.DMA],
        compiler_params=PARAMS,
        cost_estimate=LIGHT,
        name="unit_pass",
    )(*given, *after)


def match_kernel(start, k_ref, a_ref, code_ref, matched_ref, positive_ref, own_ref):
    rows = k_ref.shape[0]
    part = matched_ref.shape[0]
    count = rows // LINE
    code = code_ref[part : part + EXTRA, :].astype(jnp.float32)
    match = flat(code[0:count] * 32.0 + code[count : 2 * count]).astype(jnp.int32)
    index = lax.broadcasted_iota(jnp.int32, (rows, part), 0)
    hot = (index == match[:, start : start + part]).astype(jnp.float32).astype(jnp.bfloat16)
    a = a_ref[0:part, :]
    matched = dot_cols(hot, k_ref[...])
    matched_ref[...] = matched
    score = jnp.sum(a.astype(jnp.float32) * matched, axis=1, keepdims=True)
    positive_ref[...] = as_row(score * TAU_INV)
    own_ref[...] = -TAU_INV * jnp.dot(hot, a, preferred_element_type=jnp.float32)


def match_pass(keys, anchors, code, start, after=(), cost=LIGHT):
    rows, width = keys.shape
    part = rows // 2
    return pl.pallas_call(
        ordered(functools.partial(match_kernel, start), 3, after),
        in_specs=[VMEM] * 3 + [ANY] * len(after),
        out_specs=[VMEM] * 3,
        out_shape=[
            jax.ShapeDtypeStruct((part, width), jnp.float32),
            jax.ShapeDtypeStruct((1, part), jnp.float32),
            jax.ShapeDtypeStruct((rows, width), jnp.float32),
        ],
        compiler_params=PARAMS,
        cost_estimate=cost,
        name="match_pass",
    )(keys, anchors, code, *after)


def expo_body(a_ref, keys, expos):
    rows = expos[0].shape[0]
    a = a_ref[0:rows, :]
    lanes = jnp.zeros((rows, 128), jnp.float32)
    weighted = jnp.zeros((rows, a.shape[1]), jnp.float32)
    for k_ref, e_ref in zip(keys, expos):
        for j in range(0, k_ref.shape[0], STRIP):
            k = k_ref[j : j + STRIP, :]
            expo = jnp.exp2(dot_rows(a, k) * EXP2_SCALE)
            for c in range(0, STRIP, 128):
                lanes += expo[:, c : c + 128]
            low = expo.astype(jnp.bfloat16)
            e_ref[:, j : j + STRIP] = low
            weighted += jnp.dot(low, k, preferred_element_type=jnp.float32)
    return jnp.sum(lanes.T, axis=0, keepdims=True), weighted


def expo_mine_kernel(a_ref, *refs):
    n = (len(refs) - 2) // 2
    total, weighted = expo_body(a_ref, refs[:n], refs[n : 2 * n])
    refs[-2][...] = total
    refs[-1][...] = weighted


def expo_rest_kernel(k_ref, *refs):
    n = len(refs) // 6
    for i in range(n):
        a_ref, total_ref, weighted_ref = refs[i], refs[n + i], refs[2 * n + i]
        total, weighted = expo_body(a_ref, [k_ref], [refs[3 * n + i]])
        refs[4 * n + i][...] = total_ref[...] + total
        refs[5 * n + i][...] = weighted_ref[...] + weighted


def expo_rest(key, anchors, totals, weighted):
    rows = weighted[0].shape[0]
    n = len(anchors)
    out = pl.pallas_call(
        expo_rest_kernel,
        in_specs=[VMEM] * (1 + 3 * n),
        out_specs=[VMEM] * (3 * n),
        out_shape=[jax.ShapeDtypeStruct((rows, key.shape[0]), jnp.bfloat16)] * n
        + [jax.ShapeDtypeStruct(totals[0].shape, jnp.float32)] * n
        + [jax.ShapeDtypeStruct(weighted[0].shape, jnp.float32)] * n,
        compiler_params=PARAMS,
        cost_estimate=LIGHT,
        name="expo_rest",
    )(key, *anchors, *totals, *weighted)
    return out[:n], out[n : 2 * n], out[2 * n :]


def expo_other_kernel(a_ref, mine_ref, *refs):
    n = (len(refs) - 2) // 2
    total, weighted = expo_body(a_ref, refs[:n], refs[n : 2 * n])
    rows = weighted.shape[0]
    mine = mine_ref[...]
    refs[-2][0:1, :] = total
    refs[-2][1:2, :] = mine
    refs[-1][0:rows, :] = weighted.astype(jnp.bfloat16)
    stow(refs[-1], rows, jnp.concatenate([total, mine], axis=1))


def expo_pass(a, keys, mine=None, after=()):
    rows, width = a.shape[0] // STRIP * STRIP, a.shape[1]
    n = len(keys)
    if mine is None:
        kernel, extra = expo_mine_kernel, []
        tail = [
            jax.ShapeDtypeStruct((1, rows), jnp.float32),
            jax.ShapeDtypeStruct((rows, width), jnp.float32),
        ]
    else:
        kernel, extra = expo_other_kernel, [mine]
        tail = [
            jax.ShapeDtypeStruct((2, rows), jnp.float32),
            jax.ShapeDtypeStruct((rows + EXTRA, width), jnp.bfloat16),
        ]
    out = pl.pallas_call(
        ordered(kernel, 1 + len(extra) + n, after),
        in_specs=[VMEM] * (1 + len(extra) + n) + [ANY] * len(after),
        out_specs=[VMEM] * (n + 2),
        out_shape=[jax.ShapeDtypeStruct((rows, k.shape[0]), jnp.bfloat16) for k in keys] + tail,
        compiler_params=PARAMS,
        cost_estimate=LIGHT,
        name="expo_pass",
    )(a, *extra, *keys, *after)
    return out[:n], out[n], out[n + 1]


def turn(weighted, sent, total, matched):
    weighted = weighted + sent.astype(jnp.float32)
    return (TAU_INV * (weighted * as_column(1.0 / total) - matched)).astype(jnp.bfloat16)


def turn_first_kernel(weighted_ref, sent_ref, own_ref, matched_ref, out_ref, mine_ref, other_ref):
    rows = weighted_ref.shape[0]
    got = fetch(sent_ref, rows, 2 * rows // LINE)
    mine = own_ref[1:2, :] + got[:, 0:rows]
    mine_ref[...] = mine
    other_ref[...] = own_ref[0:1, :] + got[:, rows : 2 * rows]
    out_ref[...] = turn(weighted_ref[...], sent_ref[0:rows, :], mine, matched_ref[...])


def turn_first(weighted, sent, own, matched):
    rows, width = weighted.shape
    return pl.pallas_call(
        turn_first_kernel,
        in_specs=[VMEM] * 4,
        out_specs=[VMEM] * 3,
        out_shape=[jax.ShapeDtypeStruct((rows, width), jnp.bfloat16)]
        + [jax.ShapeDtypeStruct((1, rows), jnp.float32)] * 2,
        compiler_params=PARAMS,
        cost_estimate=LIGHT,
        name="turn_first",
    )(weighted, sent, own, matched)


def turn_last_kernel(
    weighted_ref, sent_ref, first_ref, last_ref, matched_ref, positive_ref, positive_last_ref, out_ref
):
    rows = weighted_ref.shape[0]
    last = last_ref[...]
    out_ref[0:rows, :] = turn(weighted_ref[...], sent_ref[0:rows, :], last, matched_ref[...])
    stow(
        out_ref,
        rows,
        jnp.log(jnp.concatenate([first_ref[...], last], axis=1))
        - jnp.concatenate([positive_ref[...], positive_last_ref[...]], axis=1),
    )


def turn_last(weighted, sent, first, last, matched, positive, positive_last, after):
    rows, width = weighted.shape
    return pl.pallas_call(
        ordered(turn_last_kernel, 7, after),
        in_specs=[VMEM] * 7 + [ANY] * len(after),
        out_specs=VMEM,
        out_shape=jax.ShapeDtypeStruct((rows + EXTRA, width), jnp.bfloat16),
        compiler_params=PARAMS,
        cost_estimate=LIGHT,
        name="turn_last",
    )(weighted, sent, first, last, matched, positive, positive_last, *after)


def share_kernel(*refs):
    anchors, (mine_ref, other_ref, own_ref, sent_ref) = refs[:4], refs[4:8]
    outs, last_ref = refs[8:12], refs[12]
    rows = outs[0].shape[0]
    got = fetch(sent_ref, rows, 2 * rows // LINE)
    last = own_ref[1:2, :] + got[:, 0:rows]
    last_ref[...] = last
    totals = [mine_ref[...], last, other_ref[...], own_ref[0:1, :] + got[:, rows : 2 * rows]]
    for a_ref, total, out_ref in zip(anchors, totals, outs):
        a = a_ref[0:rows, :].astype(jnp.float32)
        out_ref[...] = (a * as_column(1.0 / total)).astype(out_ref.dtype)


def share_pass(anchors, mine, other, own, sent):
    rows, width = anchors[0].shape
    out = pl.pallas_call(
        share_kernel,
        in_specs=[VMEM] * 8,
        out_specs=[VMEM] * 5,
        out_shape=[jax.ShapeDtypeStruct((rows, width), jnp.bfloat16)] * 4
        + [jax.ShapeDtypeStruct((1, rows), jnp.float32)],
        compiler_params=PARAMS,
        cost_estimate=LIGHT,
        name="share_pass",
    )(*anchors, mine, other, own, sent)
    return out[:4], out[4]


def key_kernel(*refs):
    n = len(refs) // 2
    grad = dot_cols(refs[0][...], refs[n][...])
    for e_ref, b_ref in zip(refs[1:n], refs[n + 1 : 2 * n]):
        grad += dot_cols(e_ref[...], b_ref[...])
    refs[-1][...] = (TAU_INV * grad).astype(refs[-1].dtype)


def key_pass(expos, shares, dtype, after=(), cost=LIGHT):
    rows, width = expos[0].shape[1], shares[0].shape[1]
    return pl.pallas_call(
        ordered(key_kernel, 2 * len(expos), after),
        in_specs=[VMEM] * (2 * len(expos)) + [ANY] * len(after),
        out_specs=VMEM,
        out_shape=jax.ShapeDtypeStruct((rows, width), dtype),
        compiler_params=PARAMS,
        cost_estimate=cost,
        name="key_pass",
    )(*expos, *shares, *after)


def pull(x, grad):
    scale = lax.rsqrt(jnp.sum(x * x, axis=1, keepdims=True) + 1e-06)
    unit = x * scale
    return scale * (grad - unit * jnp.sum(unit * grad, axis=1, keepdims=True))


def pull_first_kernel(x_ref, grad_ref, out_ref):
    out_ref[...] = pull(x_ref[...], grad_ref[...].astype(jnp.float32))


def pull_first(x, term, after):
    rows = term.shape[0]
    half = pl.BlockSpec((rows, x.shape[1]), lambda i: (0, 0))
    return pl.pallas_call(
        ordered(pull_first_kernel, 2, after),
        grid=(1,),
        in_specs=[half, half] + [ANY] * len(after),
        out_specs=half,
        out_shape=jax.ShapeDtypeStruct(x.shape, jnp.float32),
        compiler_params=PARAMS,
        cost_estimate=LIGHT,
        name="pull_first",
    )(x, term, *after)


def key_base_kernel(x_hbm, *refs):
    n = (len(refs) - 7) // 2
    owns, (base_ref, unit_ref, scale_ref, x_ref, sem) = refs[2 * n : 2 * n + 2], refs[2 * n + 2 :]
    load = pltpu.make_async_copy(x_hbm, x_ref, sem)
    load.start()
    grad = dot_cols(refs[0][...], refs[n][...])
    for e_ref, b_ref in zip(refs[1:n], refs[n + 1 : 2 * n]):
        grad += dot_cols(e_ref[...], b_ref[...])
    base_ref[...] = TAU_INV * grad + owns[0][...] + owns[1][...]
    load.wait()
    x = x_ref[...]
    scale = lax.rsqrt(jnp.sum(x * x, axis=1, keepdims=True) + 1e-06)
    unit_ref[...] = x * scale
    scale_ref[...] = jnp.broadcast_to(scale, scale_ref.shape)


def key_base(x, expos, shares, owns, after):
    return pl.pallas_call(
        ordered(key_base_kernel, 1 + 2 * len(expos) + 2, after),
        in_specs=[HBM] + [VMEM] * (2 * len(expos) + 2) + [ANY] * len(after),
        out_specs=[VMEM] * 3,
        out_shape=[
            jax.ShapeDtypeStruct(x.shape, jnp.float32),
            jax.ShapeDtypeStruct(x.shape, jnp.float32),
            jax.ShapeDtypeStruct((x.shape[0], 128), jnp.float32),
        ],
        scratch_shapes=[pltpu.VMEM(x.shape, jnp.float32), pltpu.SemaphoreType.DMA],
        compiler_params=PARAMS,
        cost_estimate=HEAVY,
        name="key_base",
    )(x, *expos, *shares, *owns, *after)


def pull_key_kernel(base_ref, unit_ref, scale_ref, *refs):
    terms, (out_hbm, done_ref, sems) = refs[:-3], refs[-3:]
    copies = []
    for i, start in enumerate(range(0, done_ref.shape[0], STRIP)):
        span = slice(start, start + STRIP)
        grad = base_ref[span, :]
        for ref in terms:
            grad += ref[span, :].astype(jnp.float32)
        unit = unit_ref[span, :]
        scale = scale_ref[span, 0:1]
        done_ref[span, :] = scale * (grad - unit * jnp.sum(unit * grad, axis=1, keepdims=True))
        copies.append(
            pltpu.make_async_copy(
                done_ref.at[pl.ds(start, STRIP)], out_hbm.at[pl.ds(start, STRIP)], sems.at[i]
            )
        )
        copies[-1].start()
    for copy in copies:
        copy.wait()


def pull_key(base, terms, after):
    rows, width = base[0].shape
    return pl.pallas_call(
        ordered(pull_key_kernel, 3 + len(terms), after),
        in_specs=[VMEM] * (3 + len(terms)) + [ANY] * len(after),
        out_specs=HBM,
        out_shape=jax.ShapeDtypeStruct((rows, width), jnp.float32),
        scratch_shapes=[
            pltpu.VMEM((rows, width), jnp.float32),
            pltpu.SemaphoreType.DMA((rows // STRIP,)),
        ],
        compiler_params=PARAMS,
        cost_estimate=LIGHT,
        name="pull_key",
    )(*base, *terms, *after)


def pull_rest_kernel(x_ref, grad_ref, done_ref, out_ref, loss_ref):
    del done_ref
    rows = x_ref.shape[0]
    out_ref[...] = pull(x_ref[...], grad_ref[0:rows, :].astype(jnp.float32))
    loss_ref[...] = fetch(grad_ref, rows, 2 * rows // LINE)


def pull_rest(x, term, done):
    rows = x.shape[0] // 2
    moved = pl.BlockSpec((rows, x.shape[1]), lambda i: (1, 0))
    return pl.pallas_call(
        pull_rest_kernel,
        grid=(1,),
        in_specs=[
            moved,
            pl.BlockSpec(term.shape, lambda i: (0, 0)),
            ANY,
        ],
        out_specs=[moved, pl.BlockSpec((1, 2 * rows), lambda i: (0, 0))],
        out_shape=[
            jax.ShapeDtypeStruct(x.shape, jnp.float32),
            jax.ShapeDtypeStruct((1, 2 * rows), jnp.float32),
        ],
        input_output_aliases={2: 0},
        compiler_params=PARAMS,
        cost_estimate=HEAVY,
        name="pull_rest",
    )(x, term, done)


def per_device(anchors, keys, matches):
    rows = anchors.shape[0]
    part = rows // 2
    low_0 = unit_pass(anchors, 0, part)
    low_1 = unit_pass(anchors, part, part, matches, [low_0])
    mine = [view_half(low_0), view_half(low_1)]
    k_low = unit_pass(keys, 0, rows, None, [low_1])
    pool = [k_low] + [swap(k_low, d) for d in KEY_SIDE]
    other = [swap(a, ANCHOR_SIDE) for a in mine]
    matched_0, positive_0, own_0 = match_pass(k_low, mine[0], mine[1], 0, (), FIRST)
    expo_m, total_m, weighted_m = [], [], []
    for a, after in zip(mine, ([own_0], None)):
        after = after or [total_m[0]]
        e, t, w = expo_pass(a, pool[:3], after=after)
        expo_m.append(e)
        total_m.append(t)
        weighted_m.append(w)
    rest, total_m, weighted_m = expo_rest(pool[3], mine, total_m, weighted_m)
    expo_m = [[*e, r] for e, r in zip(expo_m, rest)]
    expo_o, pair_0, weighted_o = expo_pass(other[0], pool, total_m[0], after=[total_m[1]])
    expo_o = [expo_o]
    back = [swap(weighted_o, ANCHOR_SIDE)]
    e, pair_1, weighted_o = expo_pass(other[1], pool, total_m[1], after=[pair_0])
    expo_o.append(e)
    back.append(swap(weighted_o, ANCHOR_SIDE))
    matched_1, positive_1, own_1 = match_pass(k_low, mine[1], mine[1], part, [pair_1])
    expos = expo_m + expo_o
    turn_0, mine_0, other_0 = turn_first(weighted_m[0], back[0], pair_0, matched_0)
    turned_0 = view_half(turn_0)
    shares, mine_1 = share_pass(mine + other, mine_0, other_0, pair_1, back[1])
    parts, sent = [], []
    for d in (3, 1, 2):
        parts.append(key_pass([e[d] for e in expos], shares, jnp.bfloat16, parts[-1:]))
        sent.append(swap(parts[-1], KEY_SIDE[d - 1]))
    turn_1 = turn_last(
        weighted_m[1], back[1], mine_0, mine_1, matched_1, positive_0, positive_1, parts[2:]
    )
    turned_1 = view_half(turn_1)
    base = key_base(keys, [e[0] for e in expos], shares, [own_0, own_1], [turn_1])
    anchor_grad = pull_first(anchors, turned_0, base[2:])
    anchor_grad, loss = pull_rest(anchors, turned_1, anchor_grad)
    key_grad = pull_key(base, sent, [])
    return (loss.reshape(rows), anchor_grad, key_grad)


def solution(mesh):
    placed = (P(("blk", "view"), None), P(("blk", "view"), None), P(("blk", "view"), None))
    return jax.shard_map(
        per_device,
        mesh=mesh,
        in_specs=placed,
        out_specs=(P(("blk", "view")), P(("blk", "view"), None), P(("blk", "view"), None)),
        check_vma=False,
    )
```

time: 91.5 us -> 90 us (0.984)
  starting transfers between devices: 35.8 us -> 33.4 us
  waiting for transfers between devices: 25.8 us -> 27.8 us
  local copies, waits for them, and re-layouts: 3.14 us -> 1.71 us
    ppermute x11 -> x10, starting transfers between devices: 19.7 us -> 17 us  [swap(): lax.ppermute(block, 'blk', [(i, i ^ mask) for i in range(lax.axis_size('b...]
    pallas_call x11 -> x14, Pallas kernels: 16.7 us -> 18.7 us  [the longest x4 10.1 us: expo_pass(): pl.pallas_call(ordered(kernel, 1 + len(extra) + n, after), in_specs=[VMEM...]
    unnamed x10 -> x8, local copies, waits for them, and re-layouts: 3.14 us -> 1.71 us
    pallas_call x4 -> x3, Pallas kernels: 5.63 us -> 4.23 us  [key_pass(): pl.pallas_call(ordered(key_kernel, 2 * len(expos), after), in_specs=[VMEM...]
    ppermute x4, waiting for transfers between devices: 23.3 us -> 24.4 us  [view_half(): return lax.ppermute(block, 'view', route)]
    ppermute x11 -> x10, waiting for transfers between devices: 2.43 us -> 3.36 us  [swap(): lax.ppermute(block, 'blk', [(i, i ^ mask) for i in range(lax.axis_size('b...]
  transfers between devices with their start and end apart: 15 -> 14, of which waited for: 7 -> 6; matrix products, arithmetic and copies ran while one was open for 0% -> 0% of each run, Pallas kernels for 24% -> 26%
where the time goes in v3:
time: 90 us; the launch traced here: 88.8 us
  starting transfers between devices  33.4 us (37%)
  waiting for transfers between devices  27.8 us (31%)
  Pallas kernels  24.9 us (28%)
  local copies, waits for them, and re-layouts  1.71 us (2%)
  between operations  0.99 us (1%)
    ppermute x4, waiting for transfers between devices, view_half(): return lax.ppermute(block, 'view', route)  24.4 us
    ppermute x10, starting transfers between devices, swap(): lax.ppermute(block, 'blk', [(i, i ^ mask) for i in range(lax.axis_size('b...  17 us
    ppermute x4, starting transfers between devices, view_half(): return lax.ppermute(block, 'view', route)  16.4 us
    pallas_call x4, Pallas kernels, expo_pass(): pl.pallas_call(ordered(kernel, 1 + len(extra) + n, after), in_specs=[VMEM...  10.1 us
    pallas_call x3, Pallas kernels, key_pass(): pl.pallas_call(ordered(key_kernel, 2 * len(expos), after), in_specs=[VMEM...  4.23 us
    ppermute x10, waiting for transfers between devices, swap(): lax.ppermute(block, 'blk', [(i, i ^ mask) for i in range(lax.axis_size('b...  3.36 us
    pallas_call x2, Pallas kernels, match_pass(): pl.pallas_call(ordered(functools.partial(match_kernel, start), 3, after),...  1.92 us
  transfers between devices with their start and end apart: 14, of which 6 were waited for; matrix products, arithmetic and copies ran while one was open for 0% of the time, Pallas kernels for 26%

profile of v3, /device:TPU:32, one launch (start us, length us, event | category | flops | bytes accessed | tf_op | source)
XLA Modules:
  0.0 88.8 jit_solution(11358625028590995498)
XLA Ops:
  0.6 1.2 %copy-done = f32[1024,256]{1,0:T(8,128)S(1)} copy-done((f32[1024,256]{1,0:T(8,128)S(1)}, f32[1024,256]{1,0:T(8,128)}, u32[]{:S(2)}) %copy-start) | copy-done | bytes 1048600
  2.8 6.4 %collective-permute-start.2 = (bf16[528,256]{1,0:T(8,128)(2,1)S(1)}, bf16[528,256]{1,0:T(8,128)(2,1)S(1)}, u32[]{:S(2)}, u32[]{:S(2)}) collective-permute-start(bf16[528,256]{1,0:T(8,128)(2,1)S(1)} %unit_pass.4.refs_1_), channel_id=1, source_target_pairs={{0,16},{1,17},{2,18},{3,19},{4,20},{5,21},{6,22},{7,23},{8,24},{9,... | collective-permute-start | bytes 811016 | tf_op jit(solution)/shard_map/ppermute | solution.py:37
  9.6 3.1 %collective-permute-start.4 = (bf16[1024,256]{1,0:T(8,128)(2,1)S(1)}, bf16[1024,256]{1,0:T(8,128)(2,1)S(1)}, u32[]{:S(2)}, u32[]{:S(2)}) collective-permute-start(bf16[1024,256]{1,0:T(8,128)(2,1)S(1)} %unit_pass.5.refs_0_.refs_1_.refs_2_), channel_id=1, source_target_pairs={{0,192},{32,224},{64,128},{96,160},{128,64},{160,96},{192,0},{224,... | collective-permute-start | bytes 1572872 | tf_op jit(solution)/shard_map/ppermute | solution.py:41
  12.8 1.5 %collective-permute-start = (bf16[1024,256]{1,0:T(8,128)(2,1)S(1)}, bf16[1024,256]{1,0:T(8,128)(2,1)S(1)}, u32[]{:S(2)}, u32[]{:S(2)}) collective-permute-start(bf16[1024,256]{1,0:T(8,128)(2,1)S(1)} %unit_pass.5.refs_0_.refs_1_.refs_2_), channel_id=1, source_target_pairs={{0,128},{32,160},{64,192},{96,224},{128,0},{160,32},{192,64},{224,... | collective-permute-start | bytes 1572872 | tf_op jit(solution)/shard_map/ppermute | solution.py:41
  14.3 18.4 %collective-permute-done.1.refs_1_.refs_0_ = bf16[512,256]{1,0:T(8,128)(2,1)S(1)} collective-permute-done((bf16[512,256]{1,0:T(8,128)(2,1)S(1)}, bf16[512,256]{1,0:T(8,128)(2,1)S(1)}, u32[]{:S(2)}, u32[]{:S(2)}) %collective-permute-start.1) | collective-permute-done | bytes 262176 | tf_op jit(solution)/shard_map/ppermute | solution.py:37
  32.8 3.0 %collective-permute-start.6 = (bf16[512,256]{1,0:T(8,128)(2,1)S(1)}, bf16[512,256]{1,0:T(8,128)(2,1)S(1)}, u32[]{:S(2)}, u32[]{:S(2)}) collective-permute-start(bf16[512,256]{1,0:T(8,128)(2,1)S(1)} %collective-permute-done.1.refs_1_.refs_0_), channel_id=1, source_target_pairs={{0,32},{32,0},{64,96},{96,64},{128,160},{160,128},{192,224},{224,1... | collective-permute-start | bytes 786440 | tf_op jit(solution)/shard_map/ppermute | solution.py:41
  37.3 2.2 %expo_pass.4 = (bf16[512,1024]{1,0:T(8,128)(2,1)S(1)}, bf16[512,1024]{1,0:T(8,128)(2,1)S(1)}, bf16[512,1024]{1,0:T(8,128)(2,1)S(1)}, f32[1,512]{1,0:T(1,128)S(1)}, f32[512,256]{1,0:T(8,128)S(1)}) custom-call(bf16[512,256]{1,0:T(8,128)(2,1)S(1)} %collective-permute-done.1.refs_1_.refs_0_, bf16[1024,256]{1,0:T(8,128)(2,1)S(1)} %unit_pass.5.refs_0_.refs_1_.refs_2_, ...), custom_call_target="tpu_custom_call" | custom-call | flops 1024 | bytes 1024 | tf_op jit(solution)/shard_map/expo_pass/pallas_call | solution.py:243
  39.5 2.2 %expo_pass.5 = (bf16[512,1024]{1,0:T(8,128)(2,1)S(1)}, bf16[512,1024]{1,0:T(8,128)(2,1)S(1)}, bf16[512,1024]{1,0:T(8,128)(2,1)S(1)}, f32[1,512]{1,0:T(1,128)S(1)}, f32[512,256]{1,0:T(8,128)S(1)}) custom-call(bf16[528,256]{1,0:T(8,128)(2,1)S(1)} %collective-permute-done.2.refs_2_.refs_0_.refs_1_, bf16[1024,256]{1,0:T(8,128)(2,1)S(1)} %unit_pass.5.refs_0_.refs_1_.refs_2_, ...), custom_call_target="tpu_custom_call" | custom-call | flops 1024 | bytes 1024 | tf_op jit(solution)/shard_map/expo_pass/pallas_call | solution.py:243
  41.7 1.6 %expo_rest.1 = (bf16[512,1024]{1,0:T(8,128)(2,1)S(1)}, bf16[512,1024]{1,0:T(8,128)(2,1)S(1)}, f32[1,512]{1,0:T(1,128)S(1)}, f32[1,512]{1,0:T(1,128)S(1)}, f32[51...) custom-call(bf16[1024,256]{1,0:T(8,128)(2,1)S(1)} %collective-permute-done.k_ref.refs_5_, ...), custom_call_target="tpu_custom_call" | custom-call | flops 1024 | bytes 1024 | tf_op jit(solution)/shard_map/expo_rest/pallas_call | solution.py:203
  43.5 2.8 %expo_pass.6 = (bf16[512,1024]{1,0:T(8,128)(2,1)S(1)}, bf16[512,1024]{1,0:T(8,128)(2,1)S(1)}, bf16[512,1024]{1,0:T(8,128)(2,1)S(1)}, bf16[512,1024]{1,0:T(8,128)...) custom-call(bf16[512,256]{1,0:T(8,128)(2,1)S(1)} %collective-permute-done.6.refs_0_.refs_2_, ...), custom_call_target="tpu_custom_call" | custom-call | flops 1024 | bytes 1024 | tf_op jit(solution)/shard_map/expo_pass/pallas_call | solution.py:243
  46.4 3.3 %collective-permute-start.8 = (bf16[528,256]{1,0:T(8,128)(2,1)S(1)}, bf16[528,256]{1,0:T(8,128)(2,1)S(1)}, u32[]{:S(2)}, u32[]{:S(2)}) collective-permute-start(bf16[528,256]{1,0:T(8,128)(2,1)S(1)} %get-tuple-element.61), channel_id=1, source_target_pairs={{0,32},{32,0},{64,96},{96,64},{128,160},{160,128},{192,224},{224,1... | collective-permute-start | bytes 811016 | tf_op jit(solution)/shard_map/ppermute | solution.py:41
  49.7 2.8 %expo_pass.7 = (bf16[512,1024]{1,0:T(8,128)(2,1)S(1)}, bf16[512,1024]{1,0:T(8,128)(2,1)S(1)}, bf16[512,1024]{1,0:T(8,128)(2,1)S(1)}, bf16[512,1024]{1,0:T(8,128)...) custom-call(bf16[528,256]{1,0:T(8,128)(2,1)S(1)} %collective-permute-done.5.refs_0_.refs_3_, ...), custom_call_target="tpu_custom_call" | custom-call | flops 1024 | bytes 1024 | tf_op jit(solution)/shard_map/expo_pass/pallas_call | solution.py:243
  54.3 1.9 %collective-permute-done.8.sent_ref = bf16[528,256]{1,0:T(8,128)(2,1)S(1)} collective-permute-done((bf16[528,256]{1,0:T(8,128)(2,1)S(1)}, bf16[528,256]{1,0:T(8,128)(2,1)S(1)}, u32[]{:S(2)}, u32[]{:S(2)}) %collective-permute-start.8) | collective-permute-done | bytes 270368 | tf_op jit(solution)/shard_map/ppermute | solution.py:41
  56.5 5.7 %collective-permute-start.10 = (bf16[512,256]{1,0:T(8,128)(2,1)S(1)}, bf16[512,256]{1,0:T(8,128)(2,1)S(1)}, u32[]{:S(2)}, u32[]{:S(2)}) collective-permute-start(bf16[512,256]{1,0:T(8,128)(2,1)S(1)} %get-tuple-element.86), channel_id=1, source_target_pairs={{0,16},{1,17},{2,18},{3,19},{4,20},{5,21},{6,22},{7,23},{8,24},{9,... | collective-permute-start | bytes 786440 | tf_op jit(solution)/shard_map/ppermute | solution.py:37
  62.8 1.4 %key_pass.3.refs_8_ = bf16[1024,256]{1,0:T(8,128)(2,1)S(1)} custom-call(bf16[512,1024]{1,0:T(8,128)(2,1)S(1)} %get-tuple-element.82.refs_0_, bf16[512,1024]{1,0:T(8,128)(2,1)S(1)} %get-tuple-element.83.refs_1_, bf16[512,1024]{1,0:T(8,128)(2,1)S(1)} %get-tuple-element.84.refs_2_, bf16[512,1024]{1,0:T(8,128)(2,1)S(1)} %get-tuple-element.85.refs_3_, ...), custom_call_target="tpu_custom_call" | custom-call | flops 1024 | bytes 1024 | tf_op jit(solution)/shard_map/key_pass/pallas_call | solution.py:348
  64.3 3.3 %collective-permute-start.11 = (bf16[1024,256]{1,0:T(8,128)(2,1)S(1)}, bf16[1024,256]{1,0:T(8,128)(2,1)S(1)}, u32[]{:S(2)}, u32[]{:S(2)}) collective-permute-start(bf16[1024,256]{1,0:T(8,128)(2,1)S(1)} %key_pass.3.refs_8_), channel_id=1, source_target_pairs={{0,128},{32,160},{64,192},{96,224},{128,0},{160,32},{192,64},{224,... | collective-permute-start | bytes 1572872 | tf_op jit(solution)/shard_map/ppermute | solution.py:41
  67.5 1.4 %key_pass.4.refs_8_ = bf16[1024,256]{1,0:T(8,128)(2,1)S(1)} custom-call(bf16[512,1024]{1,0:T(8,128)(2,1)S(1)} %get-tuple-element.78.refs_0_, bf16[512,1024]{1,0:T(8,128)(2,1)S(1)} %get-tuple-element.79.refs_1_, bf16[512,1024]{1,0:T(8,128)(2,1)S(1)} %get-tuple-element.80.refs_2_, bf16[512,1024]{1,0:T(8,128)(2,1)S(1)} %get-tuple-element.81.refs_3_, ...), custom_call_target="tpu_custom_call" | custom-call | flops 1024 | bytes 1024 | tf_op jit(solution)/shard_map/key_pass/pallas_call | solution.py:348
  69.7 1.4 %key_pass.5.refs_7_ = bf16[1024,256]{1,0:T(8,128)(2,1)S(1)} custom-call(bf16[512,1024]{1,0:T(8,128)(2,1)S(1)} %get-tuple-element.70.refs_0_, bf16[512,1024]{1,0:T(8,128)(2,1)S(1)} %get-tuple-element.71.refs_1_, bf16[512,1024]{1,0:T(8,128)(2,1)S(1)} %get-tuple-element.72.refs_2_, bf16[512,1024]{1,0:T(8,128)(2,1)S(1)} %get-tuple-element.73.refs_3_, ...), custom_call_target="tpu_custom_call" | custom-call | flops 1024 | bytes 1024 | tf_op jit(solution)/shard_map/key_pass/pallas_call | solution.py:348
  71.9 4.3 %collective-permute-start.9 = (bf16[528,256]{1,0:T(8,128)(2,1)S(1)}, bf16[528,256]{1,0:T(8,128)(2,1)S(1)}, u32[]{:S(2)}, u32[]{:S(2)}) collective-permute-start(bf16[528,256]{1,0:T(8,128)(2,1)S(1)} %turn_last.1.refs_11_), channel_id=1, source_target_pairs={{0,16},{1,17},{2,18},{3,19},{4,20},{5,21},{6,22},{7,23},{8,24},{9,... | collective-permute-start | bytes 811016 | tf_op jit(solution)/shard_map/ppermute | solution.py:37
  76.2 1.7 %key_base.1 = (f32[1024,256]{1,0:T(8,128)S(1)}, f32[1024,256]{1,0:T(8,128)S(1)}, f32[1024,128]{1,0:T(8,128)S(1)}) custom-call(f32[1024,256]{1,0:T(8,128)S(1)} %copy-done.2, bf16[512,1024]{1,0:T(8,128)(2,1)S(1)} %get-tuple-element.87.refs_1_, bf16[512,1024]{1,0:T(8,128)(2,1)S(1)} %get-tuple-element.88.refs_2_, ...), custom_call_target="tpu_custom_call" | custom-call | flops 4294967296 | bytes 1048576 | tf_op jit(solution)/shard_map/key_base/pallas_call | solution.py:401
  77.9 1.0 %pull_first.1.done_ref = f32[1024,256]{1,0:T(8,128)} custom-call(f32[1024,256]{1,0:T(8,128)S(1)} %copy-done.1, bf16[512,256]{1,0:T(8,128)(2,1)S(1)} %collective-permute-done.10.refs_1_, f32[1024,128]{1,0:T(8,128)S(1)} %get-tuple-element.92.refs_2_), custom_call_target="tpu_custom_call" | custom-call | flops 1024 | bytes 1024 | tf_op jit(solution)/shard_map/pull_first/pallas_call | solution.py:372
  79.0 6.0 %collective-permute-done.9.grad_ref = bf16[528,256]{1,0:T(8,128)(2,1)S(1)} collective-permute-done((bf16[528,256]{1,0:T(8,128)(2,1)S(1)}, bf16[528,256]{1,0:T(8,128)(2,1)S(1)}, u32[]{:S(2)}, u32[]{:S(2)}) %collective-permute-start.9) | collective-permute-done | bytes 270368 | tf_op jit(solution)/shard_map/ppermute | solution.py:37
  84.9 1.0 %pull_rest.1 = (f32[1024,256]{1,0:T(8,128)}, f32[1,1024]{1,0:T(1,128)}) custom-call(f32[1024,256]{1,0:T(8,128)S(1)} %copy-done.1, bf16[528,256]{1,0:T(8,128)(2,1)S(1)} %collective-permute-done.9.grad_ref, f32[1024,256]{1,0:T(8,128)} %pull_first.1.done_ref), custom_call_target="tpu_custom_call", output_to_operand_aliasing={{0}: (2, {})} | custom-call | flops 4294967296 | bytes 1048576 | tf_op jit(solution)/shard_map/pull_rest/pallas_call | solution.py:465
  87.1 1.4 %pull_key.1 = f32[1024,256]{1,0:T(8,128)} custom-call(f32[1024,256]{1,0:T(8,128)S(1)} %get-tuple-element.95.refs_0_, f32[1024,256]{1,0:T(8,128)S(1)} %get-tuple-element.96.refs_1_, f32[1024,128]{1,0:T(8,128)S(1)} %get-tuple-element.92.refs_2_, bf16[1024,256]{1,0:T(8,128)(2,1)S(1)} %collective-permute-done.11.refs_3_, ...), custom_call_target="tpu_custom_call" | custom-call | flops 1024 | bytes 1024 | tf_op jit(solution)/shard_map/pull_key/pallas_call | solution.py:440
  (32 shorter events, 8.5 us)
Async XLA Ops:
  0.6 1.2 %copy-start = (f32[1024,256]{1,0:T(8,128)S(1)}, f32[1024,256]{1,0:T(8,128)}, u32[]{:S(2)}) copy-start(f32[1024,256]{1,0:T(8,128)} %x_ref.1) | copy-start | bytes 3145732
  1.9 0.7 copy-start.3
  2.5 6.7 %copy-start.2 = (f32[1024,256]{1,0:T(8,128)S(1)}, f32[1024,256]{1,0:T(8,128)}, u32[]{:S(2)}) copy-start(f32[1024,256]{1,0:T(8,128)} %refs_0_.8) | copy-start | bytes 3145732
  2.8 33.0 %collective-permute-start.2 = (bf16[528,256]{1,0:T(8,128)(2,1)S(1)}, bf16[528,256]{1,0:T(8,128)(2,1)S(1)}, u32[]{:S(2)}, u32[]{:S(2)}) collective-permute-start(bf16[528,256]{1,0:T(8,128)(2,1)S(1)} %unit_pass.4.refs_1_), channel_id=1, source_target_pairs={{0,16},{1,17},{2,18},{3,19},{4,20},{5,21},{6,22},{7,23},{8,24},{9,... | collective-permute-start | bytes 811016 | tf_op jit(solution)/shard_map/ppermute | solution.py:37
  9.1 23.6 %collective-permute-start.1 = (bf16[512,256]{1,0:T(8,128)(2,1)S(1)}, bf16[512,256]{1,0:T(8,128)(2,1)S(1)}, u32[]{:S(2)}, u32[]{:S(2)}) collective-permute-start(bf16[512,256]{1,0:T(8,128)(2,1)S(1)} %unit_pass.3.refs_2_), channel_id=1, source_target_pairs={{0,16},{1,17},{2,18},{3,19},{4,20},{5,21},{6,22},{7,23},{8,24},{9,... | collective-permute-start | bytes 786440 | tf_op jit(solution)/shard_map/ppermute | solution.py:37
  9.6 27.7 %collective-permute-start.4 = (bf16[1024,256]{1,0:T(8,128)(2,1)S(1)}, bf16[1024,256]{1,0:T(8,128)(2,1)S(1)}, u32[]{:S(2)}, u32[]{:S(2)}) collective-permute-start(bf16[1024,256]{1,0:T(8,128)(2,1)S(1)} %unit_pass.5.refs_0_.refs_1_.refs_2_), channel_id=1, source_target_pairs={{0,192},{32,224},{64,128},{96,160},{128,64},{160,96},{192,0},{224,... | collective-permute-start | bytes 1572872 | tf_op jit(solution)/shard_map/ppermute | solution.py:41
  12.7 24.6 %collective-permute-start.3 = (bf16[1024,256]{1,0:T(8,128)(2,1)S(1)}, bf16[1024,256]{1,0:T(8,128)(2,1)S(1)}, u32[]{:S(2)}, u32[]{:S(2)}) collective-permute-start(bf16[1024,256]{1,0:T(8,128)(2,1)S(1)} %unit_pass.5.refs_0_.refs_1_.refs_2_), channel_id=1, source_target_pairs={{0,64},{32,96},{64,0},{96,32},{128,192},{160,224},{192,128},{224,1... | collective-permute-start | bytes 1572872 | tf_op jit(solution)/shard_map/ppermute | solution.py:41
  12.8 28.9 %collective-permute-start = (bf16[1024,256]{1,0:T(8,128)(2,1)S(1)}, bf16[1024,256]{1,0:T(8,128)(2,1)S(1)}, u32[]{:S(2)}, u32[]{:S(2)}) collective-permute-start(bf16[1024,256]{1,0:T(8,128)(2,1)S(1)} %unit_pass.5.refs_0_.refs_1_.refs_2_), channel_id=1, source_target_pairs={{0,128},{32,160},{64,192},{96,224},{128,0},{160,32},{192,64},{224,... | collective-permute-start | bytes 1572872 | tf_op jit(solution)/shard_map/ppermute | solution.py:41
  32.8 10.7 %collective-permute-start.6 = (bf16[512,256]{1,0:T(8,128)(2,1)S(1)}, bf16[512,256]{1,0:T(8,128)(2,1)S(1)}, u32[]{:S(2)}, u32[]{:S(2)}) collective-permute-start(bf16[512,256]{1,0:T(8,128)(2,1)S(1)} %collective-permute-done.1.refs_1_.refs_0_), channel_id=1, source_target_pairs={{0,32},{32,0},{64,96},{96,64},{128,160},{160,128},{192,224},{224,1... | collective-permute-start | bytes 786440 | tf_op jit(solution)/shard_map/ppermute | solution.py:41
  35.8 13.9 %collective-permute-start.5 = (bf16[528,256]{1,0:T(8,128)(2,1)S(1)}, bf16[528,256]{1,0:T(8,128)(2,1)S(1)}, u32[]{:S(2)}, u32[]{:S(2)}) collective-permute-start(bf16[528,256]{1,0:T(8,128)(2,1)S(1)} %collective-permute-done.2.refs_2_.refs_0_.refs_1_), channel_id=1, source_target_pairs={{0,32},{32,0},{64,96},{96,64},{128,160},{160,128},{192,224},{224,1... | collective-permute-start | bytes 811016 | tf_op jit(solution)/shard_map/ppermute | solution.py:41
  46.4 9.9 %collective-permute-start.8 = (bf16[528,256]{1,0:T(8,128)(2,1)S(1)}, bf16[528,256]{1,0:T(8,128)(2,1)S(1)}, u32[]{:S(2)}, u32[]{:S(2)}) collective-permute-start(bf16[528,256]{1,0:T(8,128)(2,1)S(1)} %get-tuple-element.61), channel_id=1, source_target_pairs={{0,32},{32,0},{64,96},{96,64},{128,160},{160,128},{192,224},{224,1... | collective-permute-start | bytes 811016 | tf_op jit(solution)/shard_map/ppermute | solution.py:41
  52.5 9.6 %collective-permute-start.7 = (bf16[528,256]{1,0:T(8,128)(2,1)S(1)}, bf16[528,256]{1,0:T(8,128)(2,1)S(1)}, u32[]{:S(2)}, u32[]{:S(2)}) collective-permute-start(bf16[528,256]{1,0:T(8,128)(2,1)S(1)} %get-tuple-element.59), channel_id=1, source_target_pairs={{0,32},{32,0},{64,96},{96,64},{128,160},{160,128},{192,224},{224,1... | collective-permute-start | bytes 811016 | tf_op jit(solution)/shard_map/ppermute | solution.py:41
  56.5 21.4 %collective-permute-start.10 = (bf16[512,256]{1,0:T(8,128)(2,1)S(1)}, bf16[512,256]{1,0:T(8,128)(2,1)S(1)}, u32[]{:S(2)}, u32[]{:S(2)}) collective-permute-start(bf16[512,256]{1,0:T(8,128)(2,1)S(1)} %get-tuple-element.86), channel_id=1, source_target_pairs={{0,16},{1,17},{2,18},{3,19},{4,20},{5,21},{6,22},{7,23},{8,24},{9,... | collective-permute-start | bytes 786440 | tf_op jit(solution)/shard_map/ppermute | solution.py:37
  64.3 22.9 %collective-permute-start.11 = (bf16[1024,256]{1,0:T(8,128)(2,1)S(1)}, bf16[1024,256]{1,0:T(8,128)(2,1)S(1)}, u32[]{:S(2)}, u32[]{:S(2)}) collective-permute-start(bf16[1024,256]{1,0:T(8,128)(2,1)S(1)} %key_pass.3.refs_8_), channel_id=1, source_target_pairs={{0,128},{32,160},{64,192},{96,224},{128,0},{160,32},{192,64},{224,... | collective-permute-start | bytes 1572872 | tf_op jit(solution)/shard_map/ppermute | solution.py:41
  69.0 18.2 %collective-permute-start.12 = (bf16[1024,256]{1,0:T(8,128)(2,1)S(1)}, bf16[1024,256]{1,0:T(8,128)(2,1)S(1)}, u32[]{:S(2)}, u32[]{:S(2)}) collective-permute-start(bf16[1024,256]{1,0:T(8,128)(2,1)S(1)} %key_pass.4.refs_8_), channel_id=1, source_target_pairs={{0,64},{32,96},{64,0},{96,32},{128,192},{160,224},{192,128},{224,1... | collective-permute-start | bytes 1572872 | tf_op jit(solution)/shard_map/ppermute | solution.py:41
  71.1 15.6 %collective-permute-start.13 = (bf16[1024,256]{1,0:T(8,128)(2,1)S(1)}, bf16[1024,256]{1,0:T(8,128)(2,1)S(1)}, u32[]{:S(2)}, u32[]{:S(2)}) collective-permute-start(bf16[1024,256]{1,0:T(8,128)(2,1)S(1)} %key_pass.5.refs_7_), channel_id=1, source_target_pairs={{0,192},{32,224},{64,128},{96,160},{128,64},{160,96},{192,0},{224,... | collective-permute-start | bytes 1572872 | tf_op jit(solution)/shard_map/ppermute | solution.py:41
  71.9 13.1 %collective-permute-start.9 = (bf16[528,256]{1,0:T(8,128)(2,1)S(1)}, bf16[528,256]{1,0:T(8,128)(2,1)S(1)}, u32[]{:S(2)}, u32[]{:S(2)}) collective-permute-start(bf16[528,256]{1,0:T(8,128)(2,1)S(1)} %turn_last.1.refs_11_), channel_id=1, source_target_pairs={{0,16},{1,17},{2,18},{3,19},{4,20},{5,21},{6,22},{7,23},{8,24},{9,... | collective-permute-start | bytes 811016 | tf_op jit(solution)/shard_map/ppermute | solution.py:37
  76.1 1.8 %copy-start.1 = (f32[1024,256]{1,0:T(8,128)S(1)}, f32[1024,256]{1,0:T(8,128)}, u32[]{:S(2)}) copy-start(f32[1024,256]{1,0:T(8,128)} %x_ref.1) | copy-start | bytes 3145732

commit v4 on v3

--- a/solution.py
+++ b/solution.py
@@ -13,8 +13,8 @@
 STRIP = 256
 LINE = 256
 EXTRA = 16
-ANCHOR_SIDE = 1
-KEY_SIDE = (2, 6, 4)
+ANCHOR_SIDE = 2
+KEY_SIDE = (1, 6, 7)
 VMEM = pl.BlockSpec(memory_space=pltpu.VMEM)
 ANY = pl.BlockSpec(memory_space=pl.ANY)
 HBM = pl.BlockSpec(memory_space=pltpu.HBM)
@@ -29,6 +29,23 @@
         kernel(*refs[:inputs], *refs[inputs + len(after) :])
 
     return body
+
+
+def gate_kernel(*refs):
+    del refs
+
+
+def gate(x, after):
+    return pl.pallas_call(
+        gate_kernel,
+        in_specs=[ANY] * (1 + len(after)),
+        out_specs=ANY,
+        out_shape=jax.ShapeDtypeStruct(x.shape, x.dtype),
+        input_output_aliases={0: 0},
+        compiler_params=PARAMS,
+        cost_estimate=LIGHT,
+        name="gate",
+    )(x, *after)
 
 
 def view_half(block):
@@ -321,7 +338,7 @@
 
 
 def share_pass(anchors, mine, other, own, sent):
-    rows, width = anchors[0].shape
+    rows, width = anchors[0].shape[0] // STRIP * STRIP, anchors[0].shape[1]
     out = pl.pallas_call(
         share_kernel,
         in_specs=[VMEM] * 8,
@@ -485,29 +502,38 @@
 def per_device(anchors, keys, matches):
     rows = anchors.shape[0]
     part = rows // 2
-    low_0 = unit_pass(anchors, 0, part)
-    low_1 = unit_pass(anchors, part, part, matches, [low_0])
+    low_0 = unit_pass(anchors, 0, part, matches)
+    low_1 = unit_pass(anchors, part, part, None, [low_0])
     mine = [view_half(low_0), view_half(low_1)]
     k_low = unit_pass(keys, 0, rows, None, [low_1])
     pool = [k_low] + [swap(k_low, d) for d in KEY_SIDE]
-    other = [swap(a, ANCHOR_SIDE) for a in mine]
-    matched_0, positive_0, own_0 = match_pass(k_low, mine[0], mine[1], 0, (), FIRST)
+    matched_0, positive_0, own_0 = match_pass(k_low, mine[0], mine[0], 0, (), FIRST)
+    code = mine[0]
+    other_0 = swap(mine[0], ANCHOR_SIDE)
+    mine[1] = gate(mine[1], [own_0])
+    other = [other_0, swap(mine[1], ANCHOR_SIDE)]
     expo_m, total_m, weighted_m = [], [], []
-    for a, after in zip(mine, ([own_0], None)):
+    for a, after in zip(mine, ([mine[1]], None)):
         after = after or [total_m[0]]
         e, t, w = expo_pass(a, pool[:3], after=after)
         expo_m.append(e)
         total_m.append(t)
         weighted_m.append(w)
-    rest, total_m, weighted_m = expo_rest(pool[3], mine, total_m, weighted_m)
-    expo_m = [[*e, r] for e, r in zip(expo_m, rest)]
-    expo_o, pair_0, weighted_o = expo_pass(other[0], pool, total_m[0], after=[total_m[1]])
-    expo_o = [expo_o]
-    back = [swap(weighted_o, ANCHOR_SIDE)]
-    e, pair_1, weighted_o = expo_pass(other[1], pool, total_m[1], after=[pair_0])
-    expo_o.append(e)
-    back.append(swap(weighted_o, ANCHOR_SIDE))
-    matched_1, positive_1, own_1 = match_pass(k_low, mine[1], mine[1], part, [pair_1])
+    for i, a in enumerate(mine):
+        if i:
+            a = gate(a, [pair_0])
+        rest, total, weighted = expo_rest(pool[3], [a], [total_m[i]], [weighted_m[i]])
+        expo_m[i] = [*expo_m[i], *rest]
+        total_m[i], weighted_m[i] = total[0], weighted[0]
+        e, pair, weighted_o = expo_pass(other[i], pool, total_m[i])
+        if i:
+            expo_o.append(e)
+            pair_1 = pair
+        else:
+            expo_o, pair_0 = [e], pair
+            back = []
+        back.append(swap(weighted_o, ANCHOR_SIDE))
+    matched_1, positive_1, own_1 = match_pass(k_low, mine[1], code, part, [pair_1])
     expos = expo_m + expo_o
     turn_0, mine_0, other_0 = turn_first(weighted_m[0], back[0], pair_0, matched_0)
     turned_0 = view_half(turn_0)

time: 90 us -> 87.3 us (0.970); the launches traced: 88.8 us -> 87 us
  waiting for transfers between devices: 27.8 us -> 24.3 us
  starting transfers between devices: 33.4 us -> 34.4 us
    ppermute x4, waiting for transfers between devices: 24.4 us -> 22 us  [view_half(): return lax.ppermute(block, 'view', route)]
    ppermute x10, starting transfers between devices: 17 us -> 18.3 us  [swap(): lax.ppermute(block, 'blk', [(i, i ^ mask) for i in range(lax.axis_size('b...]
    ppermute x10, waiting for transfers between devices: 3.36 us -> 2.25 us  [swap(): lax.ppermute(block, 'blk', [(i, i ^ mask) for i in range(lax.axis_size('b...]
    pallas_call x1 -> x2, Pallas kernels: 1.57 us -> 2 us  [expo_rest(): pl.pallas_call(expo_rest_kernel, in_specs=[VMEM] * (1 + 3 * n), out_specs...]
    unnamed x8 -> x9, local copies, waits for them, and re-layouts: 1.71 us -> 1.93 us
  transfers between devices with their start and end apart: 14 -> 14, of which waited for: 6 -> 5; matrix products, arithmetic and copies ran while one was open for 0% -> 0% of each run, Pallas kernels for 26% -> 27%
where the time goes in v4:
time: 87.3 us; the launch traced here: 87 us
  starting transfers between devices  34.4 us (39%)
  Pallas kernels  25.4 us (29%)
  waiting for transfers between devices  24.3 us (28%)
  local copies, waits for them, and re-layouts  1.93 us (2%)
  between operations  1.01 us (1%)
    ppermute x4, waiting for transfers between devices, view_half(): return lax.ppermute(block, 'view', route)  22 us
    ppermute x10, starting transfers between devices, swap(): lax.ppermute(block, 'blk', [(i, i ^ mask) for i in range(lax.axis_size('b...  18.3 us
    ppermute x4, starting transfers between devices, view_half(): return lax.ppermute(block, 'view', route)  16.1 us
    pallas_call x4, Pallas kernels, expo_pass(): pl.pallas_call(ordered(kernel, 1 + len(extra) + n, after), in_specs=[VMEM...  10.1 us
    pallas_call x3, Pallas kernels, key_pass(): pl.pallas_call(ordered(key_kernel, 2 * len(expos), after), in_specs=[VMEM...  4.25 us
    ppermute x10, waiting for transfers between devices, swap(): lax.ppermute(block, 'blk', [(i, i ^ mask) for i in range(lax.axis_size('b...  2.25 us
    pallas_call x2, Pallas kernels, expo_rest(): pl.pallas_call(expo_rest_kernel, in_specs=[VMEM] * (1 + 3 * n), out_specs...  2 us
    unnamed x9, local copies, waits for them, and re-layouts  1.93 us
  transfers between devices with their start and end apart: 14, of which 5 were waited for; matrix products, arithmetic and copies ran while one was open for 0% of the time, Pallas kernels for 27%

profile of v4, /device:TPU:32, one launch (start us, length us, event | category | flops | bytes accessed | tf_op | source)
XLA Modules:
  0.0 87.0 jit_solution(13562785396437353695)
XLA Ops:
  0.6 1.2 %copy-done = f32[1024,256]{1,0:T(8,128)S(1)} copy-done((f32[1024,256]{1,0:T(8,128)S(1)}, f32[1024,256]{1,0:T(8,128)}, u32[]{:S(2)}) %copy-start) | copy-done | bytes 1048600
  2.8 6.4 %collective-permute-start.2 = (bf16[528,256]{1,0:T(8,128)(2,1)S(1)}, bf16[528,256]{1,0:T(8,128)(2,1)S(1)}, u32[]{:S(2)}, u32[]{:S(2)}) collective-permute-start(bf16[528,256]{1,0:T(8,128)(2,1)S(1)} %unit_pass.3.refs_1_), channel_id=1, source_target_pairs={{0,16},{1,17},{2,18},{3,19},{4,20},{5,21},{6,22},{7,23},{8,24},{9,... | collective-permute-start | bytes 811016 | tf_op jit(solution)/shard_map/ppermute | solution.py:54
  9.8 3.1 %collective-permute-start.5 = (bf16[1024,256]{1,0:T(8,128)(2,1)S(1)}, bf16[1024,256]{1,0:T(8,128)(2,1)S(1)}, u32[]{:S(2)}, u32[]{:S(2)}) collective-permute-start(bf16[1024,256]{1,0:T(8,128)(2,1)S(1)} %unit_pass.5.refs_0_.refs_1_.refs_2_), channel_id=1, source_target_pairs={{0,192},{32,224},{64,128},{96,160},{128,64},{160,96},{192,0},{224,... | collective-permute-start | bytes 1572872 | tf_op jit(solution)/shard_map/ppermute | solution.py:58
  12.9 3.0 %collective-permute-start.4 = (bf16[1024,256]{1,0:T(8,128)(2,1)S(1)}, bf16[1024,256]{1,0:T(8,128)(2,1)S(1)}, u32[]{:S(2)}, u32[]{:S(2)}) collective-permute-start(bf16[1024,256]{1,0:T(8,128)(2,1)S(1)} %unit_pass.5.refs_0_.refs_1_.refs_2_), channel_id=1, source_target_pairs={{0,32},{32,0},{64,96},{96,64},{128,160},{160,128},{192,224},{224,1... | collective-permute-start | bytes 1572872 | tf_op jit(solution)/shard_map/ppermute | solution.py:58
  16.1 9.9 %collective-permute-done.2.refs_1_.refs_2_.refs_0_ = bf16[528,256]{1,0:T(8,128)(2,1)S(1)} collective-permute-done((bf16[528,256]{1,0:T(8,128)(2,1)S(1)}, bf16[528,256]{1,0:T(8,128)(2,1)S(1)}, u32[]{:S(2)}, u32[]{:S(2)}) %collective-permute-start.2) | collective-permute-done | bytes 270368 | tf_op jit(solution)/shard_map/ppermute | solution.py:54
  26.0 1.6 %collective-permute-start.3 = (bf16[528,256]{1,0:T(8,128)(2,1)S(1)}, bf16[528,256]{1,0:T(8,128)(2,1)S(1)}, u32[]{:S(2)}, u32[]{:S(2)}) collective-permute-start(bf16[528,256]{1,0:T(8,128)(2,1)S(1)} %collective-permute-done.2.refs_1_.refs_2_.refs_0_), channel_id=1, source_target_pairs={{0,64},{32,96},{64,0},{96,32},{128,192},{160,224},{192,128},{224,1... | collective-permute-start | bytes 811016 | tf_op jit(solution)/shard_map/ppermute | solution.py:58
  28.5 4.2 %collective-permute-done.1.refs_0_ = bf16[512,256]{1,0:T(8,128)(2,1)S(1)} collective-permute-done((bf16[512,256]{1,0:T(8,128)(2,1)S(1)}, bf16[512,256]{1,0:T(8,128)(2,1)S(1)}, u32[]{:S(2)}, u32[]{:S(2)}) %collective-permute-start.1) | collective-permute-done | bytes 262176 | tf_op jit(solution)/shard_map/ppermute | solution.py:54
  32.8 1.6 %collective-permute-start.6 = (bf16[512,256]{1,0:T(8,128)(2,1)S(1)}, bf16[512,256]{1,0:T(8,128)(2,1)S(1)}, u32[]{:S(2)}, u32[]{:S(2)}) collective-permute-start(bf16[512,256]{1,0:T(8,128)(2,1)S(1)} %gate.2.refs_4_.refs_0_.refs_1_), channel_id=1, source_target_pairs={{0,64},{32,96},{64,0},{96,32},{128,192},{160,224},{192,128},{224,1... | collective-permute-start | bytes 786440 | tf_op jit(solution)/shard_map/ppermute | solution.py:58
  34.4 2.2 %expo_pass.4 = (bf16[512,1024]{1,0:T(8,128)(2,1)S(1)}, bf16[512,1024]{1,0:T(8,128)(2,1)S(1)}, bf16[512,1024]{1,0:T(8,128)(2,1)S(1)}, f32[1,512]{1,0:T(1,128)S(1)}, f32[512,256]{1,0:T(8,128)S(1)}) custom-call(bf16[528,256]{1,0:T(8,128)(2,1)S(1)} %collective-permute-done.2.refs_1_.refs_2_.refs_0_, bf16[1024,256]{1,0:T(8,128)(2,1)S(1)} %unit_pass.5.refs_0_.refs_1_.refs_2_, ...), custom_call_target="tpu_custom_call" | custom-call | flops 1024 | bytes 1024 | tf_op jit(solution)/shard_map/expo_pass/pallas_call | solution.py:260
  36.6 2.2 %expo_pass.6 = (bf16[512,1024]{1,0:T(8,128)(2,1)S(1)}, bf16[512,1024]{1,0:T(8,128)(2,1)S(1)}, bf16[512,1024]{1,0:T(8,128)(2,1)S(1)}, f32[1,512]{1,0:T(1,128)S(1)}, f32[512,256]{1,0:T(8,128)S(1)}) custom-call(bf16[512,256]{1,0:T(8,128)(2,1)S(1)} %gate.2.refs_4_.refs_0_.refs_1_, bf16[1024,256]{1,0:T(8,128)(2,1)S(1)} %unit_pass.5.refs_0_.refs_1_.refs_2_, ...), custom_call_target="tpu_custom_call" | custom-call | flops 1024 | bytes 1024 | tf_op jit(solution)/shard_map/expo_pass/pallas_call | solution.py:260
  39.9 2.8 %expo_pass.5 = (bf16[512,1024]{1,0:T(8,128)(2,1)S(1)}, bf16[512,1024]{1,0:T(8,128)(2,1)S(1)}, bf16[512,1024]{1,0:T(8,128)(2,1)S(1)}, bf16[512,1024]{1,0:T(8,128)...) custom-call(bf16[528,256]{1,0:T(8,128)(2,1)S(1)} %collective-permute-done.3.refs_0_.refs_2_, ...), custom_call_target="tpu_custom_call" | custom-call | flops 1024 | bytes 1024 | tf_op jit(solution)/shard_map/expo_pass/pallas_call | solution.py:260
  44.2 2.9 %expo_pass.7 = (bf16[512,1024]{1,0:T(8,128)(2,1)S(1)}, bf16[512,1024]{1,0:T(8,128)(2,1)S(1)}, bf16[512,1024]{1,0:T(8,128)(2,1)S(1)}, bf16[512,1024]{1,0:T(8,128)...) custom-call(bf16[512,256]{1,0:T(8,128)(2,1)S(1)} %collective-permute-done.6.refs_0_.refs_3_, ...), custom_call_target="tpu_custom_call" | custom-call | flops 1024 | bytes 1024 | tf_op jit(solution)/shard_map/expo_pass/pallas_call | solution.py:260
  47.1 1.9 %collective-permute-start.7 = (bf16[528,256]{1,0:T(8,128)(2,1)S(1)}, bf16[528,256]{1,0:T(8,128)(2,1)S(1)}, u32[]{:S(2)}, u32[]{:S(2)}) collective-permute-start(bf16[528,256]{1,0:T(8,128)(2,1)S(1)} %get-tuple-element.59), channel_id=1, source_target_pairs={{0,64},{32,96},{64,0},{96,32},{128,192},{160,224},{192,128},{224,1... | collective-permute-start | bytes 811016 | tf_op jit(solution)/shard_map/ppermute | solution.py:58
  49.9 1.4 %collective-permute-done.8.sent_ref = bf16[528,256]{1,0:T(8,128)(2,1)S(1)} collective-permute-done((bf16[528,256]{1,0:T(8,128)(2,1)S(1)}, bf16[528,256]{1,0:T(8,128)(2,1)S(1)}, u32[]{:S(2)}, u32[]{:S(2)}) %collective-permute-start.8) | collective-permute-done | bytes 270368 | tf_op jit(solution)/shard_map/ppermute | solution.py:58
  51.7 5.4 %collective-permute-start.10 = (bf16[512,256]{1,0:T(8,128)(2,1)S(1)}, bf16[512,256]{1,0:T(8,128)(2,1)S(1)}, u32[]{:S(2)}, u32[]{:S(2)}) collective-permute-start(bf16[512,256]{1,0:T(8,128)(2,1)S(1)} %get-tuple-element.86), channel_id=1, source_target_pairs={{0,16},{1,17},{2,18},{3,19},{4,20},{5,21},{6,22},{7,23},{8,24},{9,... | collective-permute-start | bytes 786440 | tf_op jit(solution)/shard_map/ppermute | solution.py:54
  57.7 1.4 %key_pass.3.refs_8_ = bf16[1024,256]{1,0:T(8,128)(2,1)S(1)} custom-call(bf16[512,1024]{1,0:T(8,128)(2,1)S(1)} %get-tuple-element.82.refs_0_, bf16[512,1024]{1,0:T(8,128)(2,1)S(1)} %get-tuple-element.83.refs_1_, bf16[512,1024]{1,0:T(8,128)(2,1)S(1)} %get-tuple-element.84.refs_2_, bf16[512,1024]{1,0:T(8,128)(2,1)S(1)} %get-tuple-element.85.refs_3_, ...), custom_call_target="tpu_custom_call" | custom-call | flops 1024 | bytes 1024 | tf_op jit(solution)/shard_map/key_pass/pallas_call | solution.py:365
  59.2 3.9 %collective-permute-start.11 = (bf16[1024,256]{1,0:T(8,128)(2,1)S(1)}, bf16[1024,256]{1,0:T(8,128)(2,1)S(1)}, u32[]{:S(2)}, u32[]{:S(2)}) collective-permute-start(bf16[1024,256]{1,0:T(8,128)(2,1)S(1)} %key_pass.3.refs_8_), channel_id=1, source_target_pairs={{0,224},{32,192},{64,160},{96,128},{128,96},{160,64},{192,32},{224... | collective-permute-start | bytes 1572872 | tf_op jit(solution)/shard_map/ppermute | solution.py:58
  63.1 1.4 %key_pass.4.refs_8_ = bf16[1024,256]{1,0:T(8,128)(2,1)S(1)} custom-call(bf16[512,1024]{1,0:T(8,128)(2,1)S(1)} %get-tuple-element.78.refs_0_, bf16[512,1024]{1,0:T(8,128)(2,1)S(1)} %get-tuple-element.79.refs_1_, bf16[512,1024]{1,0:T(8,128)(2,1)S(1)} %get-tuple-element.80.refs_2_, bf16[512,1024]{1,0:T(8,128)(2,1)S(1)} %get-tuple-element.81.refs_3_, ...), custom_call_target="tpu_custom_call" | custom-call | flops 1024 | bytes 1024 | tf_op jit(solution)/shard_map/key_pass/pallas_call | solution.py:365
  65.1 1.4 %key_pass.5.refs_7_ = bf16[1024,256]{1,0:T(8,128)(2,1)S(1)} custom-call(bf16[512,1024]{1,0:T(8,128)(2,1)S(1)} %get-tuple-element.70.refs_0_, bf16[512,1024]{1,0:T(8,128)(2,1)S(1)} %get-tuple-element.71.refs_1_, bf16[512,1024]{1,0:T(8,128)(2,1)S(1)} %get-tuple-element.72.refs_2_, bf16[512,1024]{1,0:T(8,128)(2,1)S(1)} %get-tuple-element.73.refs_3_, ...), custom_call_target="tpu_custom_call" | custom-call | flops 1024 | bytes 1024 | tf_op jit(solution)/shard_map/key_pass/pallas_call | solution.py:365
  66.5 1.9 %collective-permute-start.13 = (bf16[1024,256]{1,0:T(8,128)(2,1)S(1)}, bf16[1024,256]{1,0:T(8,128)(2,1)S(1)}, u32[]{:S(2)}, u32[]{:S(2)}) collective-permute-start(bf16[1024,256]{1,0:T(8,128)(2,1)S(1)} %key_pass.5.refs_7_), channel_id=1, source_target_pairs={{0,192},{32,224},{64,128},{96,160},{128,64},{160,96},{192,0},{224,... | collective-permute-start | bytes 1572872 | tf_op jit(solution)/shard_map/ppermute | solution.py:58
  68.7 4.2 %collective-permute-start.9 = (bf16[528,256]{1,0:T(8,128)(2,1)S(1)}, bf16[528,256]{1,0:T(8,128)(2,1)S(1)}, u32[]{:S(2)}, u32[]{:S(2)}) collective-permute-start(bf16[528,256]{1,0:T(8,128)(2,1)S(1)} %turn_last.1.refs_11_), channel_id=1, source_target_pairs={{0,16},{1,17},{2,18},{3,19},{4,20},{5,21},{6,22},{7,23},{8,24},{9,... | collective-permute-start | bytes 811016 | tf_op jit(solution)/shard_map/ppermute | solution.py:54
  72.9 1.8 %key_base.1 = (f32[1024,256]{1,0:T(8,128)S(1)}, f32[1024,256]{1,0:T(8,128)S(1)}, f32[1024,128]{1,0:T(8,128)S(1)}) custom-call(f32[1024,256]{1,0:T(8,128)S(1)} %copy-done.2, bf16[512,1024]{1,0:T(8,128)(2,1)S(1)} %get-tuple-element.87.refs_1_, bf16[512,1024]{1,0:T(8,128)(2,1)S(1)} %get-tuple-element.88.refs_2_, ...), custom_call_target="tpu_custom_call" | custom-call | flops 4294967296 | bytes 1048576 | tf_op jit(solution)/shard_map/key_base/pallas_call | solution.py:418
  75.7 7.8 %collective-permute-done.9.grad_ref = bf16[528,256]{1,0:T(8,128)(2,1)S(1)} collective-permute-done((bf16[528,256]{1,0:T(8,128)(2,1)S(1)}, bf16[528,256]{1,0:T(8,128)(2,1)S(1)}, u32[]{:S(2)}, u32[]{:S(2)}) %collective-permute-start.9) | collective-permute-done | bytes 270368 | tf_op jit(solution)/shard_map/ppermute | solution.py:54
  85.4 1.4 %pull_key.1 = f32[1024,256]{1,0:T(8,128)} custom-call(f32[1024,256]{1,0:T(8,128)S(1)} %get-tuple-element.95.refs_0_, f32[1024,256]{1,0:T(8,128)S(1)} %get-tuple-element.96.refs_1_, f32[1024,128]{1,0:T(8,128)S(1)} %get-tuple-element.92.refs_2_, bf16[1024,256]{1,0:T(8,128)(2,1)S(1)} %collective-permute-done.11.refs_3_, ...), custom_call_target="tpu_custom_call" | custom-call | flops 1024 | bytes 1024 | tf_op jit(solution)/shard_map/pull_key/pallas_call | solution.py:457
  (36 shorter events, 10.8 us)
Async XLA Ops:
  0.6 1.2 %copy-start = (f32[1024,256]{1,0:T(8,128)S(1)}, f32[1024,256]{1,0:T(8,128)}, u32[]{:S(2)}) copy-start(f32[1024,256]{1,0:T(8,128)} %x_ref.1) | copy-start | bytes 3145732
  1.9 0.7 copy-start.3
  2.8 6.7 %copy-start.2 = (f32[1024,256]{1,0:T(8,128)S(1)}, f32[1024,256]{1,0:T(8,128)}, u32[]{:S(2)}) copy-start(f32[1024,256]{1,0:T(8,128)} %refs_0_.8) | copy-start | bytes 3145732
  2.8 23.2 %collective-permute-start.2 = (bf16[528,256]{1,0:T(8,128)(2,1)S(1)}, bf16[528,256]{1,0:T(8,128)(2,1)S(1)}, u32[]{:S(2)}, u32[]{:S(2)}) collective-permute-start(bf16[528,256]{1,0:T(8,128)(2,1)S(1)} %unit_pass.3.refs_1_), channel_id=1, source_target_pairs={{0,16},{1,17},{2,18},{3,19},{4,20},{5,21},{6,22},{7,23},{8,24},{9,... | collective-permute-start | bytes 811016 | tf_op jit(solution)/shard_map/ppermute | solution.py:54
  9.4 23.4 %collective-permute-start.1 = (bf16[512,256]{1,0:T(8,128)(2,1)S(1)}, bf16[512,256]{1,0:T(8,128)(2,1)S(1)}, u32[]{:S(2)}, u32[]{:S(2)}) collective-permute-start(bf16[512,256]{1,0:T(8,128)(2,1)S(1)} %unit_pass.4.refs_1_), channel_id=1, source_target_pairs={{0,16},{1,17},{2,18},{3,19},{4,20},{5,21},{6,22},{7,23},{8,24},{9,... | collective-permute-start | bytes 786440 | tf_op jit(solution)/shard_map/ppermute | solution.py:54
  9.8 24.6 %collective-permute-start.5 = (bf16[1024,256]{1,0:T(8,128)(2,1)S(1)}, bf16[1024,256]{1,0:T(8,128)(2,1)S(1)}, u32[]{:S(2)}, u32[]{:S(2)}) collective-permute-start(bf16[1024,256]{1,0:T(8,128)(2,1)S(1)} %unit_pass.5.refs_0_.refs_1_.refs_2_), channel_id=1, source_target_pairs={{0,192},{32,224},{64,128},{96,160},{128,64},{160,96},{192,0},{224,... | collective-permute-start | bytes 1572872 | tf_op jit(solution)/shard_map/ppermute | solution.py:58
  12.9 21.5 %collective-permute-start.4 = (bf16[1024,256]{1,0:T(8,128)(2,1)S(1)}, bf16[1024,256]{1,0:T(8,128)(2,1)S(1)}, u32[]{:S(2)}, u32[]{:S(2)}) collective-permute-start(bf16[1024,256]{1,0:T(8,128)(2,1)S(1)} %unit_pass.5.refs_0_.refs_1_.refs_2_), channel_id=1, source_target_pairs={{0,32},{32,0},{64,96},{96,64},{128,160},{160,128},{192,224},{224,1... | collective-permute-start | bytes 1572872 | tf_op jit(solution)/shard_map/ppermute | solution.py:58
  15.9 22.9 %collective-permute-start = (bf16[1024,256]{1,0:T(8,128)(2,1)S(1)}, bf16[1024,256]{1,0:T(8,128)(2,1)S(1)}, u32[]{:S(2)}, u32[]{:S(2)}) collective-permute-start(bf16[1024,256]{1,0:T(8,128)(2,1)S(1)} %unit_pass.5.refs_0_.refs_1_.refs_2_), channel_id=1, source_target_pairs={{0,224},{32,192},{64,160},{96,128},{128,96},{160,64},{192,32},{224... | collective-permute-start | bytes 1572872 | tf_op jit(solution)/shard_map/ppermute | solution.py:58
  26.0 13.8 %collective-permute-start.3 = (bf16[528,256]{1,0:T(8,128)(2,1)S(1)}, bf16[528,256]{1,0:T(8,128)(2,1)S(1)}, u32[]{:S(2)}, u32[]{:S(2)}) collective-permute-start(bf16[528,256]{1,0:T(8,128)(2,1)S(1)} %collective-permute-done.2.refs_1_.refs_2_.refs_0_), channel_id=1, source_target_pairs={{0,64},{32,96},{64,0},{96,32},{128,192},{160,224},{192,128},{224,1... | collective-permute-start | bytes 811016 | tf_op jit(solution)/shard_map/ppermute | solution.py:58
  32.8 11.4 %collective-permute-start.6 = (bf16[512,256]{1,0:T(8,128)(2,1)S(1)}, bf16[512,256]{1,0:T(8,128)(2,1)S(1)}, u32[]{:S(2)}, u32[]{:S(2)}) collective-permute-start(bf16[512,256]{1,0:T(8,128)(2,1)S(1)} %gate.2.refs_4_.refs_0_.refs_1_), channel_id=1, source_target_pairs={{0,64},{32,96},{64,0},{96,32},{128,192},{160,224},{192,128},{224,1... | collective-permute-start | bytes 786440 | tf_op jit(solution)/shard_map/ppermute | solution.py:58
  42.7 8.7 %collective-permute-start.8 = (bf16[528,256]{1,0:T(8,128)(2,1)S(1)}, bf16[528,256]{1,0:T(8,128)(2,1)S(1)}, u32[]{:S(2)}, u32[]{:S(2)}) collective-permute-start(bf16[528,256]{1,0:T(8,128)(2,1)S(1)} %get-tuple-element.61), channel_id=1, source_target_pairs={{0,64},{32,96},{64,0},{96,32},{128,192},{160,224},{192,128},{224,1... | collective-permute-start | bytes 811016 | tf_op jit(solution)/shard_map/ppermute | solution.py:58
  47.1 10.0 %collective-permute-start.7 = (bf16[528,256]{1,0:T(8,128)(2,1)S(1)}, bf16[528,256]{1,0:T(8,128)(2,1)S(1)}, u32[]{:S(2)}, u32[]{:S(2)}) collective-permute-start(bf16[528,256]{1,0:T(8,128)(2,1)S(1)} %get-tuple-element.59), channel_id=1, source_target_pairs={{0,64},{32,96},{64,0},{96,32},{128,192},{160,224},{192,128},{224,1... | collective-permute-start | bytes 811016 | tf_op jit(solution)/shard_map/ppermute | solution.py:58
  51.7 23.0 %collective-permute-start.10 = (bf16[512,256]{1,0:T(8,128)(2,1)S(1)}, bf16[512,256]{1,0:T(8,128)(2,1)S(1)}, u32[]{:S(2)}, u32[]{:S(2)}) collective-permute-start(bf16[512,256]{1,0:T(8,128)(2,1)S(1)} %get-tuple-element.86), channel_id=1, source_target_pairs={{0,16},{1,17},{2,18},{3,19},{4,20},{5,21},{6,22},{7,23},{8,24},{9,... | collective-permute-start | bytes 786440 | tf_op jit(solution)/shard_map/ppermute | solution.py:54
  59.2 26.2 %collective-permute-start.11 = (bf16[1024,256]{1,0:T(8,128)(2,1)S(1)}, bf16[1024,256]{1,0:T(8,128)(2,1)S(1)}, u32[]{:S(2)}, u32[]{:S(2)}) collective-permute-start(bf16[1024,256]{1,0:T(8,128)(2,1)S(1)} %key_pass.3.refs_8_), channel_id=1, source_target_pairs={{0,224},{32,192},{64,160},{96,128},{128,96},{160,64},{192,32},{224... | collective-permute-start | bytes 1572872 | tf_op jit(solution)/shard_map/ppermute | solution.py:58
  64.5 20.9 %collective-permute-start.12 = (bf16[1024,256]{1,0:T(8,128)(2,1)S(1)}, bf16[1024,256]{1,0:T(8,128)(2,1)S(1)}, u32[]{:S(2)}, u32[]{:S(2)}) collective-permute-start(bf16[1024,256]{1,0:T(8,128)(2,1)S(1)} %key_pass.4.refs_8_), channel_id=1, source_target_pairs={{0,32},{32,0},{64,96},{96,64},{128,160},{160,128},{192,224},{224,1... | collective-permute-start | bytes 1572872 | tf_op jit(solution)/shard_map/ppermute | solution.py:58
  66.5 18.8 %collective-permute-start.13 = (bf16[1024,256]{1,0:T(8,128)(2,1)S(1)}, bf16[1024,256]{1,0:T(8,128)(2,1)S(1)}, u32[]{:S(2)}, u32[]{:S(2)}) collective-permute-start(bf16[1024,256]{1,0:T(8,128)(2,1)S(1)} %key_pass.5.refs_7_), channel_id=1, source_target_pairs={{0,192},{32,224},{64,128},{96,160},{128,64},{160,96},{192,0},{224,... | collective-permute-start | bytes 1572872 | tf_op jit(solution)/shard_map/ppermute | solution.py:58
  68.7 14.8 %collective-permute-start.9 = (bf16[528,256]{1,0:T(8,128)(2,1)S(1)}, bf16[528,256]{1,0:T(8,128)(2,1)S(1)}, u32[]{:S(2)}, u32[]{:S(2)}) collective-permute-start(bf16[528,256]{1,0:T(8,128)(2,1)S(1)} %turn_last.1.refs_11_), channel_id=1, source_target_pairs={{0,16},{1,17},{2,18},{3,19},{4,20},{5,21},{6,22},{7,23},{8,24},{9,... | collective-permute-start | bytes 811016 | tf_op jit(solution)/shard_map/ppermute | solution.py:54
  72.9 1.8 %copy-start.1 = (f32[1024,256]{1,0:T(8,128)S(1)}, f32[1024,256]{1,0:T(8,128)}, u32[]{:S(2)}) copy-start(f32[1024,256]{1,0:T(8,128)} %x_ref.1) | copy-start | bytes 3145732

commit v5 on v4

--- a/solution.py
+++ b/solution.py
@@ -21,6 +21,7 @@
 PARAMS = pltpu.CompilerParams(vmem_limit_bytes=16 * 2**20)
 HEAVY = pl.CostEstimate(flops=2**32, bytes_accessed=2**20, transcendentals=0)
 FIRST = pl.CostEstimate(flops=2**32, bytes_accessed=2**20, transcendentals=0)
+SECOND = pl.CostEstimate(flops=2**31, bytes_accessed=2**20, transcendentals=0)
 LIGHT = pl.CostEstimate(flops=1024, bytes_accessed=1024, transcendentals=0)
 
 
@@ -205,30 +206,38 @@
     refs[-1][...] = weighted
 
 
-def expo_rest_kernel(k_ref, *refs):
-    n = len(refs) // 6
-    for i in range(n):
-        a_ref, total_ref, weighted_ref = refs[i], refs[n + i], refs[2 * n + i]
-        total, weighted = expo_body(a_ref, [k_ref], [refs[3 * n + i]])
-        refs[4 * n + i][...] = total_ref[...] + total
-        refs[5 * n + i][...] = weighted_ref[...] + weighted
-
-
-def expo_rest(key, anchors, totals, weighted):
-    rows = weighted[0].shape[0]
-    n = len(anchors)
-    out = pl.pallas_call(
-        expo_rest_kernel,
-        in_specs=[VMEM] * (1 + 3 * n),
-        out_specs=[VMEM] * (3 * n),
-        out_shape=[jax.ShapeDtypeStruct((rows, key.shape[0]), jnp.bfloat16)] * n
-        + [jax.ShapeDtypeStruct(totals[0].shape, jnp.float32)] * n
-        + [jax.ShapeDtypeStruct(weighted[0].shape, jnp.float32)] * n,
-        compiler_params=PARAMS,
-        cost_estimate=LIGHT,
-        name="expo_rest",
-    )(key, *anchors, *totals, *weighted)
-    return out[:n], out[n : 2 * n], out[2 * n :]
+def expo_close_kernel(k_ref, a_ref, o_ref, *refs):
+    total_m, total_o, part_m, part_o, last_m, last_o, pair_ref, weighted_ref, sent_ref = refs
+    total, weighted = expo_body(a_ref, [k_ref], [last_m])
+    mine = total_m[...] + total
+    weighted_ref[...] = part_m[...] + weighted
+    total, weighted = expo_body(o_ref, [k_ref], [last_o])
+    other = total_o[...] + total
+    rows = weighted.shape[0]
+    pair_ref[0:1, :] = other
+    pair_ref[1:2, :] = mine
+    sent_ref[0:rows, :] = (part_o[...] + weighted).astype(jnp.bfloat16)
+    stow(sent_ref, rows, jnp.concatenate([other, mine], axis=1))
+
+
+def expo_close(key, mine, other, total_m, total_o, part_m, part_o):
+    rows, width = part_m.shape
+    expo = jax.ShapeDtypeStruct((rows, key.shape[0]), jnp.bfloat16)
+    return pl.pallas_call(
+        expo_close_kernel,
+        in_specs=[VMEM] * 7,
+        out_specs=[VMEM] * 5,
+        out_shape=[
+            expo,
+            expo,
+            jax.ShapeDtypeStruct((2, rows), jnp.float32),
+            jax.ShapeDtypeStruct((rows, width), jnp.float32),
+            jax.ShapeDtypeStruct((rows + EXTRA, width), jnp.bfloat16),
+        ],
+        compiler_params=PARAMS,
+        cost_estimate=LIGHT,
+        name="expo_close",
+    )(key, mine, other, total_m, total_o, part_m, part_o)
 
 
 def expo_other_kernel(a_ref, mine_ref, *refs):
@@ -242,7 +251,7 @@
     stow(refs[-1], rows, jnp.concatenate([total, mine], axis=1))
 
 
-def expo_pass(a, keys, mine=None, after=()):
+def expo_pass(a, keys, mine=None, after=(), cost=LIGHT):
     rows, width = a.shape[0] // STRIP * STRIP, a.shape[1]
     n = len(keys)
     if mine is None:
@@ -263,7 +272,7 @@
         out_specs=[VMEM] * (n + 2),
         out_shape=[jax.ShapeDtypeStruct((rows, k.shape[0]), jnp.bfloat16) for k in keys] + tail,
         compiler_params=PARAMS,
-        cost_estimate=LIGHT,
+        cost_estimate=cost,
         name="expo_pass",
     )(a, *extra, *keys, *after)
     return out[:n], out[n], out[n + 1]
@@ -512,27 +521,18 @@
     other_0 = swap(mine[0], ANCHOR_SIDE)
     mine[1] = gate(mine[1], [own_0])
     other = [other_0, swap(mine[1], ANCHOR_SIDE)]
-    expo_m, total_m, weighted_m = [], [], []
-    for a, after in zip(mine, ([mine[1]], None)):
-        after = after or [total_m[0]]
-        e, t, w = expo_pass(a, pool[:3], after=after)
-        expo_m.append(e)
-        total_m.append(t)
-        weighted_m.append(w)
-    for i, a in enumerate(mine):
-        if i:
-            a = gate(a, [pair_0])
-        rest, total, weighted = expo_rest(pool[3], [a], [total_m[i]], [weighted_m[i]])
-        expo_m[i] = [*expo_m[i], *rest]
-        total_m[i], weighted_m[i] = total[0], weighted[0]
-        e, pair, weighted_o = expo_pass(other[i], pool, total_m[i])
-        if i:
-            expo_o.append(e)
-            pair_1 = pair
-        else:
-            expo_o, pair_0 = [e], pair
-            back = []
-        back.append(swap(weighted_o, ANCHOR_SIDE))
+    expo_m0, total_m, part_m = expo_pass(mine[0], pool[:3], after=[mine[1]])
+    expo_o0, total_o, part_o = expo_pass(other[0], pool[:3], after=[total_m], cost=SECOND)
+    last_m, last_o, pair_0, part_m, sent_0 = expo_close(
+        pool[3], mine[0], other[0], total_m, total_o, part_m, part_o
+    )
+    back = [swap(sent_0, ANCHOR_SIDE)]
+    expo_m1, total_m1, part_m1 = expo_pass(mine[1], pool, after=[pair_0])
+    weighted_m = [part_m, part_m1]
+    expo_o1, pair_1, sent_1 = expo_pass(other[1], pool, total_m1)
+    back.append(swap(sent_1, ANCHOR_SIDE))
+    expo_m = [[*expo_m0, last_m], expo_m1]
+    expo_o = [[*expo_o0, last_o], expo_o1]
     matched_1, positive_1, own_1 = match_pass(k_low, mine[1], code, part, [pair_1])
     expos = expo_m + expo_o
     turn_0, mine_0, other_0 = turn_first(weighted_m[0], back[0], pair_0, matched_0)

time: 87.3 us -> 90.1 us (1.032)
  the two profiles are of different devices: /device:TPU:32 before, /device:TPU:1 now
where the time goes in v5:
time: 90.1 us; the launch traced here: 89.9 us
  waiting for transfers between devices  34.1 us (38%)
  starting transfers between devices  27.9 us (31%)
  Pallas kernels  24.9 us (28%)
  local copies, waits for them, and re-layouts  1.92 us (2%)
  between operations  1 us (1%)
    ppermute x4, waiting for transfers between devices, view_half(): return lax.ppermute(block, 'view', route)  29.4 us
    ppermute x10, starting transfers between devices, swap(): lax.ppermute(block, 'blk', [(i, i ^ mask) for i in range(lax.axis_size('b...  14.7 us
    ppermute x4, starting transfers between devices, view_half(): return lax.ppermute(block, 'view', route)  13.2 us
    pallas_call x4, Pallas kernels, expo_pass(): pl.pallas_call(ordered(kernel, 1 + len(extra) + n, after), in_specs=[VMEM...  10.1 us
    ppermute x10, waiting for transfers between devices, swap(): lax.ppermute(block, 'blk', [(i, i ^ mask) for i in range(lax.axis_size('b...  4.68 us
    pallas_call x3, Pallas kernels, key_pass(): pl.pallas_call(ordered(key_kernel, 2 * len(expos), after), in_specs=[VMEM...  4.26 us
    pallas_call x2, Pallas kernels, match_pass(): pl.pallas_call(ordered(functools.partial(match_kernel, start), 3, after),...  1.92 us
    unnamed x8, local copies, waits for them, and re-layouts  1.92 us
  transfers between devices with their start and end apart: 14, of which 4 were waited for; matrix products, arithmetic and copies ran while one was open for 0% of the time, Pallas kernels for 26%

profile of v5, /device:TPU:1, one launch (start us, length us, event | category | flops | bytes accessed | tf_op | source)
XLA Modules:
  0.0 89.9 jit_solution(11731581218750588128)
XLA Ops:
  0.6 1.2 %copy-done = f32[1024,256]{1,0:T(8,128)S(1)} copy-done((f32[1024,256]{1,0:T(8,128)S(1)}, f32[1024,256]{1,0:T(8,128)}, u32[]{:S(2)}) %copy-start) | copy-done | bytes 1048600
  2.8 7.8 %collective-permute-start.1 = (bf16[528,256]{1,0:T(8,128)(2,1)S(1)}, bf16[528,256]{1,0:T(8,128)(2,1)S(1)}, u32[]{:S(2)}, u32[]{:S(2)}) collective-permute-start(bf16[528,256]{1,0:T(8,128)(2,1)S(1)} %unit_pass.3.refs_1_), channel_id=1, source_target_pairs={{0,16},{1,17},{2,18},{3,19},{4,20},{5,21},{6,22},{7,23},{8,24},{9,... | collective-permute-start | bytes 811016 | tf_op jit(solution)/shard_map/ppermute | solution.py:55
  11.1 2.8 %collective-permute-start.3 = (bf16[1024,256]{1,0:T(8,128)(2,1)S(1)}, bf16[1024,256]{1,0:T(8,128)(2,1)S(1)}, u32[]{:S(2)}, u32[]{:S(2)}) collective-permute-start(bf16[1024,256]{1,0:T(8,128)(2,1)S(1)} %unit_pass.5.refs_0_.refs_1_.refs_2_), channel_id=1, source_target_pairs={{0,192},{32,224},{64,128},{96,160},{128,64},{160,96},{192,0},{224,... | collective-permute-start | bytes 1572872 | tf_op jit(solution)/shard_map/ppermute | solution.py:59
  13.9 2.7 %collective-permute-start.2 = (bf16[1024,256]{1,0:T(8,128)(2,1)S(1)}, bf16[1024,256]{1,0:T(8,128)(2,1)S(1)}, u32[]{:S(2)}, u32[]{:S(2)}) collective-permute-start(bf16[1024,256]{1,0:T(8,128)(2,1)S(1)} %unit_pass.5.refs_0_.refs_1_.refs_2_), channel_id=1, source_target_pairs={{0,32},{32,0},{64,96},{96,64},{128,160},{160,128},{192,224},{224,1... | collective-permute-start | bytes 1572872 | tf_op jit(solution)/shard_map/ppermute | solution.py:59
  17.6 1.4 %collective-permute-start.5 = (bf16[528,256]{1,0:T(8,128)(2,1)S(1)}, bf16[528,256]{1,0:T(8,128)(2,1)S(1)}, u32[]{:S(2)}, u32[]{:S(2)}) collective-permute-start(bf16[528,256]{1,0:T(8,128)(2,1)S(1)} %collective-permute-done.1.refs_1_.refs_2_.refs_0_.a_ref), channel_id=1, source_target_pairs={{0,64},{32,96},{64,0},{96,32},{128,192},{160,224},{192,128},{224,1... | collective-permute-start | bytes 811016 | tf_op jit(solution)/shard_map/ppermute | solution.py:59
  20.1 17.5 %collective-permute-done.refs_0_ = bf16[512,256]{1,0:T(8,128)(2,1)S(1)} collective-permute-done((bf16[512,256]{1,0:T(8,128)(2,1)S(1)}, bf16[512,256]{1,0:T(8,128)(2,1)S(1)}, u32[]{:S(2)}, u32[]{:S(2)}) %collective-permute-start) | collective-permute-done | bytes 262176 | tf_op jit(solution)/shard_map/ppermute | solution.py:55
  37.6 2.2 %expo_pass.4 = (bf16[512,1024]{1,0:T(8,128)(2,1)S(1)}, bf16[512,1024]{1,0:T(8,128)(2,1)S(1)}, bf16[512,1024]{1,0:T(8,128)(2,1)S(1)}, f32[1,512]{1,0:T(1,128)S(1)}, f32[512,256]{1,0:T(8,128)S(1)}) custom-call(bf16[528,256]{1,0:T(8,128)(2,1)S(1)} %collective-permute-done.1.refs_1_.refs_2_.refs_0_.a_ref, ...), custom_call_target="tpu_custom_call" | custom-call | flops 1024 | bytes 1024 | tf_op jit(solution)/shard_map/expo_pass/pallas_call | solution.py:269
  39.8 2.2 %expo_pass.5 = (bf16[512,1024]{1,0:T(8,128)(2,1)S(1)}, bf16[512,1024]{1,0:T(8,128)(2,1)S(1)}, bf16[512,1024]{1,0:T(8,128)(2,1)S(1)}, f32[1,512]{1,0:T(1,128)S(1)}, f32[512,256]{1,0:T(8,128)S(1)}) custom-call(bf16[528,256]{1,0:T(8,128)(2,1)S(1)} %collective-permute-done.5.refs_0_.o_ref.refs_2_, bf16[1024,256]{1,0:T(8,128)(2,1)S(1)} %unit_pass.5.refs_0_.refs_1_.refs_2_, ...), custom_call_target="tpu_custom_call" | custom-call | flops 2147483648 | bytes 1048576 | tf_op jit(solution)/shard_map/expo_pass/pallas_call | solution.py:269
  42.0 1.6 %expo_close.1 = (bf16[512,1024]{1,0:T(8,128)(2,1)S(1)}, bf16[512,1024]{1,0:T(8,128)(2,1)S(1)}, f32[2,512]{1,0:T(2,128)S(1)}, f32[512,256]{1,0:T(8,128)S(1)}, bf16[528,256]{1,0:T(8,128)(2,1)S(1)}) custom-call(bf16[1024,256]{1,0:T(8,128)(2,1)S(1)} %collective-permute-done.4.k_ref.refs_4_.refs_5_, ...), custom_call_target="tpu_custom_call" | custom-call | flops 1024 | bytes 1024 | tf_op jit(solution)/shard_map/expo_close/pallas_call | solution.py:226
  43.6 1.7 %collective-permute-start.8 = (bf16[528,256]{1,0:T(8,128)(2,1)S(1)}, bf16[528,256]{1,0:T(8,128)(2,1)S(1)}, u32[]{:S(2)}, u32[]{:S(2)}) collective-permute-start(bf16[528,256]{1,0:T(8,128)(2,1)S(1)} %get-tuple-element.59), channel_id=1, source_target_pairs={{0,64},{32,96},{64,0},{96,32},{128,192},{160,224},{192,128},{224,1... | collective-permute-start | bytes 811016 | tf_op jit(solution)/shard_map/ppermute | solution.py:59
  45.3 2.8 %expo_pass.6 = (bf16[512,1024]{1,0:T(8,128)(2,1)S(1)}, bf16[512,1024]{1,0:T(8,128)(2,1)S(1)}, bf16[512,1024]{1,0:T(8,128)(2,1)S(1)}, bf16[512,1024]{1,0:T(8,128)...) custom-call(bf16[512,256]{1,0:T(8,128)(2,1)S(1)} %gate.1.refs_4_.refs_0_.refs_1_, ...), custom_call_target="tpu_custom_call" | custom-call | flops 1024 | bytes 1024 | tf_op jit(solution)/shard_map/expo_pass/pallas_call | solution.py:269
  48.2 2.9 %expo_pass.7 = (bf16[512,1024]{1,0:T(8,128)(2,1)S(1)}, bf16[512,1024]{1,0:T(8,128)(2,1)S(1)}, bf16[512,1024]{1,0:T(8,128)(2,1)S(1)}, bf16[512,1024]{1,0:T(8,128)...) custom-call(bf16[512,256]{1,0:T(8,128)(2,1)S(1)} %collective-permute-done.6.refs_0_.refs_3_, ...), custom_call_target="tpu_custom_call" | custom-call | flops 1024 | bytes 1024 | tf_op jit(solution)/shard_map/expo_pass/pallas_call | solution.py:269
  52.4 2.1 %collective-permute-start.10 = (bf16[512,256]{1,0:T(8,128)(2,1)S(1)}, bf16[512,256]{1,0:T(8,128)(2,1)S(1)}, u32[]{:S(2)}, u32[]{:S(2)}) collective-permute-start(bf16[512,256]{1,0:T(8,128)(2,1)S(1)} %get-tuple-element.84), channel_id=1, source_target_pairs={{0,16},{1,17},{2,18},{3,19},{4,20},{5,21},{6,22},{7,23},{8,24},{9,... | collective-permute-start | bytes 786440 | tf_op jit(solution)/shard_map/ppermute | solution.py:55
  54.5 3.0 %collective-permute-done.7.refs_7_.refs_1_ = bf16[528,256]{1,0:T(8,128)(2,1)S(1)} collective-permute-done((bf16[528,256]{1,0:T(8,128)(2,1)S(1)}, bf16[528,256]{1,0:T(8,128)(2,1)S(1)}, u32[]{:S(2)}, u32[]{:S(2)}) %collective-permute-start.7) | collective-permute-done | bytes 270368 | tf_op jit(solution)/shard_map/ppermute | solution.py:59
  58.1 1.4 %key_pass.3.refs_8_ = bf16[1024,256]{1,0:T(8,128)(2,1)S(1)} custom-call(bf16[512,1024]{1,0:T(8,128)(2,1)S(1)} %get-tuple-element.80.refs_0_, bf16[512,1024]{1,0:T(8,128)(2,1)S(1)} %get-tuple-element.81.refs_1_, bf16[512,1024]{1,0:T(8,128)(2,1)S(1)} %get-tuple-element.82.refs_2_, bf16[512,1024]{1,0:T(8,128)(2,1)S(1)} %get-tuple-element.83.refs_3_, ...), custom_call_target="tpu_custom_call" | custom-call | flops 1024 | bytes 1024 | tf_op jit(solution)/shard_map/key_pass/pallas_call | solution.py:374
  59.6 1.4 %key_pass.4.refs_8_ = bf16[1024,256]{1,0:T(8,128)(2,1)S(1)} custom-call(bf16[512,1024]{1,0:T(8,128)(2,1)S(1)} %get-tuple-element.76.refs_0_, bf16[512,1024]{1,0:T(8,128)(2,1)S(1)} %get-tuple-element.77.refs_1_, bf16[512,1024]{1,0:T(8,128)(2,1)S(1)} %get-tuple-element.78.refs_2_, bf16[512,1024]{1,0:T(8,128)(2,1)S(1)} %get-tuple-element.79.refs_3_, ...), custom_call_target="tpu_custom_call" | custom-call | flops 1024 | bytes 1024 | tf_op jit(solution)/shard_map/key_pass/pallas_call | solution.py:374
  61.1 1.8 %collective-permute-start.12 = (bf16[1024,256]{1,0:T(8,128)(2,1)S(1)}, bf16[1024,256]{1,0:T(8,128)(2,1)S(1)}, u32[]{:S(2)}, u32[]{:S(2)}) collective-permute-start(bf16[1024,256]{1,0:T(8,128)(2,1)S(1)} %key_pass.4.refs_8_), channel_id=1, source_target_pairs={{0,32},{32,0},{64,96},{96,64},{128,160},{160,128},{192,224},{224,1... | collective-permute-start | bytes 1572872 | tf_op jit(solution)/shard_map/ppermute | solution.py:59
  62.8 1.4 %key_pass.5.refs_7_ = bf16[1024,256]{1,0:T(8,128)(2,1)S(1)} custom-call(bf16[512,1024]{1,0:T(8,128)(2,1)S(1)} %get-tuple-element.68.refs_0_, bf16[512,1024]{1,0:T(8,128)(2,1)S(1)} %get-tuple-element.69.refs_1_, bf16[512,1024]{1,0:T(8,128)(2,1)S(1)} %get-tuple-element.70.refs_2_, bf16[512,1024]{1,0:T(8,128)(2,1)S(1)} %get-tuple-element.71.refs_3_, ...), custom_call_target="tpu_custom_call" | custom-call | flops 1024 | bytes 1024 | tf_op jit(solution)/shard_map/key_pass/pallas_call | solution.py:374
  64.3 4.0 %collective-permute-start.13 = (bf16[1024,256]{1,0:T(8,128)(2,1)S(1)}, bf16[1024,256]{1,0:T(8,128)(2,1)S(1)}, u32[]{:S(2)}, u32[]{:S(2)}) collective-permute-start(bf16[1024,256]{1,0:T(8,128)(2,1)S(1)} %key_pass.5.refs_7_), channel_id=1, source_target_pairs={{0,192},{32,224},{64,128},{96,160},{128,64},{160,96},{192,0},{224,... | collective-permute-start | bytes 1572872 | tf_op jit(solution)/shard_map/ppermute | solution.py:59
  68.5 2.4 %collective-permute-start.9 = (bf16[528,256]{1,0:T(8,128)(2,1)S(1)}, bf16[528,256]{1,0:T(8,128)(2,1)S(1)}, u32[]{:S(2)}, u32[]{:S(2)}) collective-permute-start(bf16[528,256]{1,0:T(8,128)(2,1)S(1)} %turn_last.1.refs_11_), channel_id=1, source_target_pairs={{0,16},{1,17},{2,18},{3,19},{4,20},{5,21},{6,22},{7,23},{8,24},{9,... | collective-permute-start | bytes 811016 | tf_op jit(solution)/shard_map/ppermute | solution.py:55
  70.9 1.7 %key_base.1 = (f32[1024,256]{1,0:T(8,128)S(1)}, f32[1024,256]{1,0:T(8,128)S(1)}, f32[1024,128]{1,0:T(8,128)S(1)}) custom-call(f32[1024,256]{1,0:T(8,128)S(1)} %copy-done.2, bf16[512,1024]{1,0:T(8,128)(2,1)S(1)} %get-tuple-element.85.refs_1_, bf16[512,1024]{1,0:T(8,128)(2,1)S(1)} %get-tuple-element.86.refs_2_, ...), custom_call_target="tpu_custom_call" | custom-call | flops 4294967296 | bytes 1048576 | tf_op jit(solution)/shard_map/key_base/pallas_call | solution.py:427
  73.7 11.9 %collective-permute-done.9.grad_ref = bf16[528,256]{1,0:T(8,128)(2,1)S(1)} collective-permute-done((bf16[528,256]{1,0:T(8,128)(2,1)S(1)}, bf16[528,256]{1,0:T(8,128)(2,1)S(1)}, u32[]{:S(2)}, u32[]{:S(2)}) %collective-permute-start.9) | collective-permute-done | bytes 270368 | tf_op jit(solution)/shard_map/ppermute | solution.py:55
  86.7 1.7 %collective-permute-done.13.refs_5_ = bf16[1024,256]{1,0:T(8,128)(2,1)S(1)} collective-permute-done((bf16[1024,256]{1,0:T(8,128)(2,1)S(1)}, bf16[1024,256]{1,0:T(8,128)(2,1)S(1)}, u32[]{:S(2)}, u32[]{:S(2)}) %collective-permute-start.13) | collective-permute-done | bytes 524320 | tf_op jit(solution)/shard_map/ppermute | solution.py:59
  88.3 1.4 %pull_key.1 = f32[1024,256]{1,0:T(8,128)} custom-call(f32[1024,256]{1,0:T(8,128)S(1)} %get-tuple-element.93.refs_0_, f32[1024,256]{1,0:T(8,128)S(1)} %get-tuple-element.94.refs_1_, f32[1024,128]{1,0:T(8,128)S(1)} %get-tuple-element.90.refs_2_, bf16[1024,256]{1,0:T(8,128)(2,1)S(1)} %collective-permute-done.11.refs_3_, ...), custom_call_target="tpu_custom_call" | custom-call | flops 1024 | bytes 1024 | tf_op jit(solution)/shard_map/pull_key/pallas_call | solution.py:466
  (33 shorter events, 7.7 us)
Async XLA Ops:
  0.6 1.2 %copy-start = (f32[1024,256]{1,0:T(8,128)S(1)}, f32[1024,256]{1,0:T(8,128)}, u32[]{:S(2)}) copy-start(f32[1024,256]{1,0:T(8,128)} %x_ref.1) | copy-start | bytes 3145732
  1.9 0.7 copy-start.3
  2.8 8.0 %copy-start.2 = (f32[1024,256]{1,0:T(8,128)S(1)}, f32[1024,256]{1,0:T(8,128)}, u32[]{:S(2)}) copy-start(f32[1024,256]{1,0:T(8,128)} %refs_0_.8) | copy-start | bytes 3145732
  2.8 14.9 %collective-permute-start.1 = (bf16[528,256]{1,0:T(8,128)(2,1)S(1)}, bf16[528,256]{1,0:T(8,128)(2,1)S(1)}, u32[]{:S(2)}, u32[]{:S(2)}) collective-permute-start(bf16[528,256]{1,0:T(8,128)(2,1)S(1)} %unit_pass.3.refs_1_), channel_id=1, source_target_pairs={{0,16},{1,17},{2,18},{3,19},{4,20},{5,21},{6,22},{7,23},{8,24},{9,... | collective-permute-start | bytes 811016 | tf_op jit(solution)/shard_map/ppermute | solution.py:55
  11.1 26.5 %collective-permute-start.3 = (bf16[1024,256]{1,0:T(8,128)(2,1)S(1)}, bf16[1024,256]{1,0:T(8,128)(2,1)S(1)}, u32[]{:S(2)}, u32[]{:S(2)}) collective-permute-start(bf16[1024,256]{1,0:T(8,128)(2,1)S(1)} %unit_pass.5.refs_0_.refs_1_.refs_2_), channel_id=1, source_target_pairs={{0,192},{32,224},{64,128},{96,160},{128,64},{160,96},{192,0},{224,... | collective-permute-start | bytes 1572872 | tf_op jit(solution)/shard_map/ppermute | solution.py:59
  13.9 23.7 %collective-permute-start.2 = (bf16[1024,256]{1,0:T(8,128)(2,1)S(1)}, bf16[1024,256]{1,0:T(8,128)(2,1)S(1)}, u32[]{:S(2)}, u32[]{:S(2)}) collective-permute-start(bf16[1024,256]{1,0:T(8,128)(2,1)S(1)} %unit_pass.5.refs_0_.refs_1_.refs_2_), channel_id=1, source_target_pairs={{0,32},{32,0},{64,96},{96,64},{128,160},{160,128},{192,224},{224,1... | collective-permute-start | bytes 1572872 | tf_op jit(solution)/shard_map/ppermute | solution.py:59
  16.7 20.9 %collective-permute-start = (bf16[512,256]{1,0:T(8,128)(2,1)S(1)}, bf16[512,256]{1,0:T(8,128)(2,1)S(1)}, u32[]{:S(2)}, u32[]{:S(2)}) collective-permute-start(bf16[512,256]{1,0:T(8,128)(2,1)S(1)} %unit_pass.4.refs_1_), channel_id=1, source_target_pairs={{0,16},{1,17},{2,18},{3,19},{4,20},{5,21},{6,22},{7,23},{8,24},{9,... | collective-permute-start | bytes 786440 | tf_op jit(solution)/shard_map/ppermute | solution.py:55
  17.6 24.4 %collective-permute-start.4 = (bf16[1024,256]{1,0:T(8,128)(2,1)S(1)}, bf16[1024,256]{1,0:T(8,128)(2,1)S(1)}, u32[]{:S(2)}, u32[]{:S(2)}) collective-permute-start(bf16[1024,256]{1,0:T(8,128)(2,1)S(1)} %unit_pass.5.refs_0_.refs_1_.refs_2_), channel_id=1, source_target_pairs={{0,224},{32,192},{64,160},{96,128},{128,96},{160,64},{192,32},{224... | collective-permute-start | bytes 1572872 | tf_op jit(solution)/shard_map/ppermute | solution.py:59
  17.6 22.2 %collective-permute-start.5 = (bf16[528,256]{1,0:T(8,128)(2,1)S(1)}, bf16[528,256]{1,0:T(8,128)(2,1)S(1)}, u32[]{:S(2)}, u32[]{:S(2)}) collective-permute-start(bf16[528,256]{1,0:T(8,128)(2,1)S(1)} %collective-permute-done.1.refs_1_.refs_2_.refs_0_.a_ref), channel_id=1, source_target_pairs={{0,64},{32,96},{64,0},{96,32},{128,192},{160,224},{192,128},{224,1... | collective-permute-start | bytes 811016 | tf_op jit(solution)/shard_map/ppermute | solution.py:59
  37.6 10.6 %collective-permute-start.6 = (bf16[512,256]{1,0:T(8,128)(2,1)S(1)}, bf16[512,256]{1,0:T(8,128)(2,1)S(1)}, u32[]{:S(2)}, u32[]{:S(2)}) collective-permute-start(bf16[512,256]{1,0:T(8,128)(2,1)S(1)} %gate.1.refs_4_.refs_0_.refs_1_), channel_id=1, source_target_pairs={{0,64},{32,96},{64,0},{96,32},{128,192},{160,224},{192,128},{224,1... | collective-permute-start | bytes 786440 | tf_op jit(solution)/shard_map/ppermute | solution.py:59
  43.6 8.5 %collective-permute-start.8 = (bf16[528,256]{1,0:T(8,128)(2,1)S(1)}, bf16[528,256]{1,0:T(8,128)(2,1)S(1)}, u32[]{:S(2)}, u32[]{:S(2)}) collective-permute-start(bf16[528,256]{1,0:T(8,128)(2,1)S(1)} %get-tuple-element.59), channel_id=1, source_target_pairs={{0,64},{32,96},{64,0},{96,32},{128,192},{160,224},{192,128},{224,1... | collective-permute-start | bytes 811016 | tf_op jit(solution)/shard_map/ppermute | solution.py:59
  51.0 6.4 %collective-permute-start.7 = (bf16[528,256]{1,0:T(8,128)(2,1)S(1)}, bf16[528,256]{1,0:T(8,128)(2,1)S(1)}, u32[]{:S(2)}, u32[]{:S(2)}) collective-permute-start(bf16[528,256]{1,0:T(8,128)(2,1)S(1)} %get-tuple-element.57), channel_id=1, source_target_pairs={{0,64},{32,96},{64,0},{96,32},{128,192},{160,224},{192,128},{224,1... | collective-permute-start | bytes 811016 | tf_op jit(solution)/shard_map/ppermute | solution.py:59
  52.4 20.3 %collective-permute-start.10 = (bf16[512,256]{1,0:T(8,128)(2,1)S(1)}, bf16[512,256]{1,0:T(8,128)(2,1)S(1)}, u32[]{:S(2)}, u32[]{:S(2)}) collective-permute-start(bf16[512,256]{1,0:T(8,128)(2,1)S(1)} %get-tuple-element.84), channel_id=1, source_target_pairs={{0,16},{1,17},{2,18},{3,19},{4,20},{5,21},{6,22},{7,23},{8,24},{9,... | collective-permute-start | bytes 786440 | tf_op jit(solution)/shard_map/ppermute | solution.py:55
  59.5 28.8 %collective-permute-start.11 = (bf16[1024,256]{1,0:T(8,128)(2,1)S(1)}, bf16[1024,256]{1,0:T(8,128)(2,1)S(1)}, u32[]{:S(2)}, u32[]{:S(2)}) collective-permute-start(bf16[1024,256]{1,0:T(8,128)(2,1)S(1)} %key_pass.3.refs_8_), channel_id=1, source_target_pairs={{0,224},{32,192},{64,160},{96,128},{128,96},{160,64},{192,32},{224... | collective-permute-start | bytes 1572872 | tf_op jit(solution)/shard_map/ppermute | solution.py:59
  61.1 27.3 %collective-permute-start.12 = (bf16[1024,256]{1,0:T(8,128)(2,1)S(1)}, bf16[1024,256]{1,0:T(8,128)(2,1)S(1)}, u32[]{:S(2)}, u32[]{:S(2)}) collective-permute-start(bf16[1024,256]{1,0:T(8,128)(2,1)S(1)} %key_pass.4.refs_8_), channel_id=1, source_target_pairs={{0,32},{32,0},{64,96},{96,64},{128,160},{160,128},{192,224},{224,1... | collective-permute-start | bytes 1572872 | tf_op jit(solution)/shard_map/ppermute | solution.py:59
  64.3 24.1 %collective-permute-start.13 = (bf16[1024,256]{1,0:T(8,128)(2,1)S(1)}, bf16[1024,256]{1,0:T(8,128)(2,1)S(1)}, u32[]{:S(2)}, u32[]{:S(2)}) collective-permute-start(bf16[1024,256]{1,0:T(8,128)(2,1)S(1)} %key_pass.5.refs_7_), channel_id=1, source_target_pairs={{0,192},{32,224},{64,128},{96,160},{128,64},{160,96},{192,0},{224,... | collective-permute-start | bytes 1572872 | tf_op jit(solution)/shard_map/ppermute | solution.py:59
  68.5 17.2 %collective-permute-start.9 = (bf16[528,256]{1,0:T(8,128)(2,1)S(1)}, bf16[528,256]{1,0:T(8,128)(2,1)S(1)}, u32[]{:S(2)}, u32[]{:S(2)}) collective-permute-start(bf16[528,256]{1,0:T(8,128)(2,1)S(1)} %turn_last.1.refs_11_), channel_id=1, source_target_pairs={{0,16},{1,17},{2,18},{3,19},{4,20},{5,21},{6,22},{7,23},{8,24},{9,... | collective-permute-start | bytes 811016 | tf_op jit(solution)/shard_map/ppermute | solution.py:55
  70.9 1.8 %copy-start.1 = (f32[1024,256]{1,0:T(8,128)S(1)}, f32[1024,256]{1,0:T(8,128)}, u32[]{:S(2)}) copy-start(f32[1024,256]{1,0:T(8,128)} %x_ref.1) | copy-start | bytes 3145732
